TPU v7x, 1024 devices: a whole 4x4x32 slice. The times are simulated.
1024 devices in a mesh: grp: 16 (over y, x_lo, core), blk: 64 (over x_hi, z).
Axes of the slice: x: 4 (x_hi: 2, x_lo: 2; x = x_hi * 2 + x_lo), y: 4, z: 32, core: 2. Of those that a mesh axis runs over, the one named last changes fastest.
Arguments:
- adj_tiles: bfloat16 [16384, 256, 256], P(('grp', 'blk')), may hold values from -0.375 to 0.375
- tile_pos: int32 [16384], P(('grp', 'blk')), may hold values from 0 to 255
- tile_count: int32 [1024], P(('grp', 'blk')), may hold values from 1 to 16, as said below
- node_feats: bfloat16 [131072, 128], P(('grp', 'blk')), may hold values from -6 to 6
- stale_part: bfloat16 [16, 16, 8192, 128], P('grp', None, 'blk'), may hold values from -4 to 4
- w_self: bfloat16 [128, 256], replicated, may hold values from -0.5 to 0.5
- w_neigh: bfloat16 [128, 256], replicated, may hold values from -0.25 to 0.25
- bias_vec: float32 [256], replicated, may hold values from -3 to 3
- cotangent: bfloat16 [131072, 256], P(('grp', 'blk')), may hold values from -6 to 6
Outputs:
- new_part: bfloat16 [16, 16, 8192, 128], P('grp', None, 'blk')
- hidden: bfloat16 [131072, 256], P(('grp', 'blk'))
- grad_self: float32 [128, 256], replicated
- grad_neigh: float32 [128, 256], replicated
- grad_bias: float32 [256], replicated
Inputs may be any that keep to these rules, and one draw needn't show every extreme that they name: `tile_count`: slots are live only below a device's count; one device has exactly 16 live slots. Tile positions of one device may repeat, and their products then add.
All inputs are finite; a program needn't handle non-finite values.
Results may differ from a plain program's by a relative error of at most 0.019.
Values may be sent and summed in bfloat16 or wider, within the bound.
No kernel may reach another device: no remote copies, remote signals or barrier semaphores. Data moves between devices by JAX's collectives and lax.ppermute only.
A program may use at most 32 MiB of HBM per device.

v0:
```python
import jax
import jax.numpy as jnp
from jax import lax
from jax.sharding import PartitionSpec as P


def body(
    adj_tiles, tile_pos, tile_count, node_feats, stale_part, w_self, w_neigh, bias_vec, cotangent
):
    tile_side = adj_tiles.shape[1]
    node_dev = node_feats.shape[0]
    feat_width = node_feats.shape[1]
    group_count = lax.axis_size("grp")
    own_group = lax.axis_index("grp")
    group_rows = lax.all_gather(node_feats, "blk", axis=0, tiled=True)
    col_tiles = group_rows.shape[0] // tile_side
    row_tiles = group_count * node_dev // tile_side
    keep_mask = (jnp.arange(group_count) != own_group)[None, :, None, None]
    terms = jnp.where(keep_mask, stale_part.astype(jnp.float32), jnp.float32(0.0))
    stale_sum = lax.psum_scatter(
        terms.astype(jnp.bfloat16), "grp", scatter_dimension=1, tiled=True
    ).astype(jnp.float32)[0, 0]

    def add_tile(slot, running):
        position = tile_pos[slot]
        row_tile = position // col_tiles
        col_tile = position % col_tiles
        source = lax.dynamic_slice_in_dim(group_rows, col_tile * tile_side, tile_side, 0)
        product = jnp.dot(adj_tiles[slot], source, preferred_element_type=jnp.float32)
        current = lax.dynamic_index_in_dim(running, row_tile, 0, keepdims=False)
        return lax.dynamic_update_index_in_dim(running, current + product, row_tile, 0)

    start = jnp.zeros((row_tiles, tile_side, feat_width), jnp.float32)
    running = lax.fori_loop(0, tile_count[0], add_tile, start)
    partial_rows = running.reshape(group_count, node_dev, feat_width)
    new_part = partial_rows.astype(jnp.bfloat16)[None]
    own_fresh = lax.dynamic_index_in_dim(partial_rows, own_group, 0, keepdims=False)
    aggregate = (own_fresh + stale_sum).astype(jnp.bfloat16)
    preact = jnp.dot(node_feats, w_self, preferred_element_type=jnp.float32)
    preact = preact + jnp.dot(aggregate, w_neigh, preferred_element_type=jnp.float32) + bias_vec
    gate = jax.nn.sigmoid(preact)
    hidden = (preact * gate).astype(jnp.bfloat16)
    grad_pre = (cotangent.astype(jnp.float32) * gate * (1.0 + preact * (1.0 - gate))).astype(
        jnp.bfloat16
    )
    local_self = jnp.dot(node_feats.T, grad_pre, preferred_element_type=jnp.float32)
    local_neigh = jnp.dot(aggregate.T, grad_pre, preferred_element_type=jnp.float32)
    local_bias = jnp.sum(grad_pre.astype(jnp.float32), axis=0)
    grad_self, grad_neigh, grad_bias = lax.psum(
        (local_self, local_neigh, local_bias), ("grp", "blk")
    )
    node_total = node_dev * group_count * lax.axis_size("blk")
    scaling = float(node_total) ** (-0.5)
    return (new_part, hidden, grad_self * scaling, grad_neigh * scaling, grad_bias * scaling)


def solution(mesh):
    placed = (
        P(("grp", "blk"), None, None),
        P(("grp", "blk")),
        P(("grp", "blk")),
        P(("grp", "blk"), None),
        P("grp", None, "blk", None),
        P(),
        P(),
        P(),
        P(("grp", "blk"), None),
    )
    return jax.shard_map(
        body,
        mesh=mesh,
        in_specs=placed,
        out_specs=(P("grp", None, "blk", None), P(("grp", "blk"), None), P(), P(), P()),
        check_vma=False,
    )
```

profile of v0, /device:TPU:1, one launch (start us, length us, event | category | flops | bytes accessed | tf_op | source)
XLA Modules:
  0.0 1392.8 jit_solution(15328890143732733905)
XLA Ops:
  8.0 0.0 all-gather.2.cloned.1.call-start
  8.1 0.7 all-gather.2.cloned.1.call-update
  8.8 0.0 reduce-scatter.2.cloned.1.call-start
  8.8 2.0 select_convert_fusion
  10.8 0.0 reduce-scatter.2.cloned.1.call-update
  10.9 0.0 all-reduce.3.cloned.1.call-start
  10.9 1.0 fusion.8
  11.9 267.4 %all-gather.2.cloned.1.call-done = bf16[8192,128]{1,0:T(8,128)(2,1)} async-done(((bf16[128,128]{1,0:T(8,128)(2,1)}), bf16[8192,128]{1,0:T(8,128)(2,1)}) %all-gather.2.cloned.1.call-update) | async-done | bytes 2097168 | tf_op jit(solution)/shard_map/all_gather | solution.py:15
  279.3 0.1 broadcast_in_dim.25
  279.4 5.7 while.12
  280.1 0.6 dynamic_slice.45
  283.3 1.1 fusion.23
  285.1 0.9 convert_element_type.35
  286.0 0.8 fusion.7
  286.8 0.8 convert_reduce_fusion
  287.6 0.8 convolution_bitcast_fusion
  288.5 0.9 fusion.9
  289.3 241.5 %psum.23 = f32[256]{0:T(256)S(1)} all-reduce(f32[256]{0:T(256)S(1)} %get-tuple-element.108), channel_id=1, replica_groups=mesh['grp'=16,'blk'=64] {'grp','blk'}, use_global_device_ids=true, to_apply=%region_6.7 | all-reduce | flops 256 | bytes 2048 | tf_op jit(solution)/shard_map/psum | solution.py:49
  530.9 0.0 all-reduce.3.cloned.1.call-update
  530.9 0.6 broadcast_multiply_fusion.2
  531.4 851.4 %all-reduce.3.cloned.1.call-done = (f32[128,256]{0,1:T(8,128)}, f32[128,256]{0,1:T(8,128)}) async-done(((f32[128,256]{0,1:T(8,128)}, f32[128,256]{0,1:T(8,128)}), (f32[128,256]{0,1:T(8,128)}, f32[128,256]{0,1:T(8,128)})) %all-reduce.3.cloned.1.call-update) | async-done | bytes 262160 | tf_op jit(solution)/shard_map/psum | solution.py:49
  1382.9 1.0 broadcast_multiply_fusion
  1383.8 0.8 copy.15
  1384.6 0.8 copy.16
  (13 shorter events, 0.1 us)
Async XLA Ops:
  8.0 278.8 %copy-start = (bf16[128,256]{1,0:T(8,128)(2,1)S(1)}, bf16[128,256]{1,0:T(8,128)(2,1)}, u32[]{:S(2)}) copy-start(bf16[128,256]{1,0:T(8,128)(2,1)} %param.17) | copy-start | bytes 196612
  8.0 271.4 %copy-start.4 = (s32[16]{0:T(128)S(1)}, s32[16]{0:T(128)}, u32[]{:S(2)}) copy-start(s32[16]{0:T(128)} %param.12) | copy-start | bytes 196
  8.0 271.3 %all-gather.2.cloned.1.call-start = ((), (), s32[]{:S(2)}) async-start(), calls=%async_computation.1 | async-start | bytes 2129920 | tf_op jit(solution)/shard_map/all_gather | solution.py:15
  8.8 277.2 %reduce-scatter.2.cloned.1.call-start = ((), (), s32[]{:S(2)}) async-start(), calls=%async_computation.2 | async-start | bytes 557056 | tf_op jit(solution)/shard_map/reduce_scatter | solution.py:20
  10.9 1372.0 %all-reduce.3.cloned.1.call-start = ((), (), s32[]{:S(2)}) async-start(), calls=%async_computation.3 | async-start | bytes 524288 | tf_op jit(solution)/shard_map/psum | solution.py:49
  279.4 7.4 copy-start.2
  279.4 7.4 copy-start.3
  285.1 2.5 copy-start.1
Sparse Core Ops, SparseCore 0:
  13.1 266.1 all-gather.1
Sparse Core Ops, SparseCore 1:
  12.6 85.7 reduce-scatter.1
  531.0 851.8 all-reduce.2
where the time goes:
time: 1400 us; the launch traced here: 1390 us
  waiting for transfers between devices  1120 us (80%)
  blocking collectives  242 us (17%)
  between operations  15.6 us (1%)
    psum x1, waiting for transfers between devices, body(): lax.psum((local_self, local_neigh, local_bias), ('grp', 'blk'))  851 us
    all_gather x1, waiting for transfers between devices, body(): group_rows = lax.all_gather(node_feats, 'blk', axis=0, tiled=True)  267 us
    psum x1, blocking collectives, body(): lax.psum((local_self, local_neigh, local_bias), ('grp', 'blk'))  242 us
  transfers between devices with their start and end apart: 3, of which 2 were waited for; matrix products, arithmetic and copies ran while one was open for 0% of the time, Pallas kernels for 0%

commit v1 on v0

v1 whole, which is shorter than its diff:
```python
import functools

import jax
import jax.numpy as jnp
from jax import lax
from jax.experimental import pallas as pl
from jax.experimental.pallas import tpu as pltpu
from jax.sharding import Mesh, PartitionSpec as P

GRP = ("y", "x_lo", "core")
PLANE = ("y", "x_lo", "core", "x_hi")
BLK = ("x_hi", "z_far", "z_near")
ALL = GRP + BLK
SIZES = (4, 2, 2, 2, 8, 4)


def spread(value, axes):
    copies = lax.axis_size(axes)
    return lax.all_to_all(
        jnp.broadcast_to(value[None], (copies,) + value.shape), axes, 0, 0, tiled=True
    )


def layer_kernel(
    count_ref,
    pos_ref,
    place_ref,
    own_ref,
    adj_ref,
    rows_ref,
    stale_ref,
    feats_ref,
    w_self_ref,
    w_neigh_ref,
    bias_ref,
    cot_ref,
    part_ref,
    hidden_ref,
    grads_ref,
    acc_ref,
):
    tile = adj_ref.shape[1]
    groups, node_dev, width = part_ref.shape
    per_tile = tile // node_dev
    col_tiles = rows_ref.shape[0] // per_tile
    own = own_ref[0]
    acc_ref[...] = jnp.zeros_like(acc_ref)

    def add_tile(slot, carry):
        position = pos_ref[slot]
        row_tile = lax.div(position, col_tiles)
        first = lax.rem(position, col_tiles) * per_tile
        source = jnp.concatenate(
            [rows_ref[place_ref[first + j]] for j in range(per_tile)], axis=0
        )
        product = jnp.dot(adj_ref[slot], source, preferred_element_type=jnp.float32)
        rows = pl.ds(pl.multiple_of(row_tile * tile, tile), tile)
        acc_ref[rows, :] += product
        return carry

    lax.fori_loop(0, count_ref[0], add_tile, 0)
    part_ref[...] = acc_ref[...].reshape(part_ref.shape).astype(part_ref.dtype)
    total = acc_ref[pl.ds(pl.multiple_of(own * node_dev, node_dev), node_dev), :]
    stale = jnp.zeros((node_dev, width), jnp.float32)
    for source in range(groups):
        keep = jnp.where(source == own, jnp.float32(0.0), jnp.float32(1.0))
        stale += stale_ref[source].astype(jnp.float32) * keep
    aggregate = (total + stale).astype(jnp.bfloat16)
    feats = feats_ref[...]
    preact = jnp.dot(feats, w_self_ref[...], preferred_element_type=jnp.float32)
    preact += jnp.dot(aggregate, w_neigh_ref[...], preferred_element_type=jnp.float32)
    preact += bias_ref[...]
    gate = jax.nn.sigmoid(preact)
    hidden_ref[...] = (preact * gate).astype(hidden_ref.dtype)
    grad_pre = (
        cot_ref[...].astype(jnp.float32) * gate * (1.0 + preact * (1.0 - gate))
    ).astype(jnp.bfloat16)
    both = jnp.concatenate([feats, aggregate], axis=1)
    grads = lax.dot_general(
        both, grad_pre, (((0,), (0,)), ((), ())), preferred_element_type=jnp.float32
    )
    bias_grad = jnp.sum(grad_pre.astype(jnp.float32), axis=0, keepdims=True)
    pieces, piece_rows, _ = grads_ref.shape
    hid = grads.shape[1]
    grads_ref[:, :, :hid] = grads.reshape(pieces, piece_rows, hid)
    half = hid // 2
    tail = jnp.concatenate(
        [
            bias_grad[:, :half],
            bias_grad[:, half:],
            jnp.zeros((piece_rows - 2, half), jnp.float32),
        ],
        axis=0,
    )
    grads_ref[:, :, hid:] = jnp.broadcast_to(tail[None], (pieces, piece_rows, half))


def body(
    adj_tiles, tile_pos, tile_count, node_feats, stale_part, w_self, w_neigh, bias_vec, cotangent
):
    node_dev, width = node_feats.shape
    hid = cotangent.shape[1]
    groups = lax.axis_size(GRP)
    blocks = lax.axis_size(BLK)
    plane = lax.axis_size(PLANE)
    far, near, sides = SIZES[4], SIZES[5], SIZES[3]

    stale = lax.all_to_all(stale_part[0], GRP, 0, 0, tiled=True)
    rows = spread(node_feats, "z_far")
    rows = spread(rows, "z_near")
    rows = spread(rows, "x_hi").reshape(blocks, node_dev, width)
    index = jnp.arange(blocks, dtype=jnp.int32)
    side, line = index // (far * near), index % (far * near)
    place = side * (far * near) + (line % near) * far + line // near
    own = lax.axis_index(GRP).reshape(1).astype(jnp.int32)

    smem = pl.BlockSpec(memory_space=pltpu.SMEM)
    vmem = pl.BlockSpec(memory_space=pltpu.VMEM)
    piece_rows = 2 * width // plane
    new_part, hidden, grads = pl.pallas_call(
        layer_kernel,
        out_shape=(
            jax.ShapeDtypeStruct((groups, node_dev, width), jnp.bfloat16),
            jax.ShapeDtypeStruct((node_dev, hid), jnp.bfloat16),
            jax.ShapeDtypeStruct((plane, piece_rows, hid + hid // 2), jnp.float32),
        ),
        in_specs=[smem] * 4 + [vmem] * 8,
        out_specs=(vmem, vmem, vmem),
        scratch_shapes=[pltpu.VMEM((groups * node_dev, width), jnp.float32)],
        compiler_params=pltpu.CompilerParams(vmem_limit_bytes=32 * 1024 * 1024),
    )(
        tile_count,
        tile_pos,
        place,
        own,
        adj_tiles,
        rows,
        stale,
        node_feats,
        w_self,
        w_neigh,
        bias_vec[None],
        cotangent,
    )

    scaling = float(node_dev * groups * blocks) ** (-0.5)
    piece = jnp.sum(lax.all_to_all(grads, PLANE, 0, 0, tiled=True), axis=0)
    piece = jnp.sum(spread(piece, "z_far"), axis=0)
    piece = jnp.sum(spread(piece, "z_near"), axis=0) * scaling
    grad_bias = piece[:2, hid:].reshape(hid)
    whole = spread(piece[:, :hid], PLANE).reshape(2 * width, hid)
    return new_part[None], hidden, whole[:width], whole[width:], grad_bias


def solution(mesh):
    fine = Mesh(mesh.devices.reshape(SIZES), ALL)
    placed = (
        P(ALL, None, None),
        P(ALL),
        P(ALL),
        P(ALL, None),
        P(GRP, None, BLK, None),
        P(),
        P(),
        P(),
        P(ALL, None),
    )
    return jax.shard_map(
        body,
        mesh=fine,
        in_specs=placed,
        out_specs=(P(GRP, None, BLK, None), P(ALL, None), P(), P(), P()),
        check_vma=False,
    )
```

time: 1400 us -> 221 us (0.16)
  waiting for transfers between devices: 1120 us -> 31.2 us
  blocking collectives: 242 us -> 165 us
  between operations: 15.6 us -> 1.41 us
    psum x1 -> x0, waiting for transfers between devices: 851 us -> none  [body(): lax.psum((local_self, local_neigh, local_bias), ('grp', 'blk'))]
    all_gather x1 -> x0, waiting for transfers between devices: 267 us -> none  [body(): group_rows = lax.all_gather(node_feats, 'blk', axis=0, tiled=True)]
    psum x1 -> x0, blocking collectives: 242 us -> none  [body(): lax.psum((local_self, local_neigh, local_bias), ('grp', 'blk'))]
    all_to_all x0 -> x6, blocking collectives: none -> 165 us  [the longest x4 120 us: spread(): lax.all_to_all(jnp.broadcast_to(value[None], (copies,) + value.shape), ax...]
    all_to_all x0 -> x2, waiting for transfers between devices: none -> 31.2 us  [spread(): lax.all_to_all(jnp.broadcast_to(value[None], (copies,) + value.shape), ax...]
  transfers between devices with their start and end apart: 3 -> 2, of which waited for: 2 -> 2; matrix products, arithmetic and copies ran while one was open for 0% -> 0% of each run, Pallas kernels for 0% -> 0%
where the time goes in v1:
time: 221 us; the launch traced here: 220 us
  blocking collectives  165 us (75%)
  waiting for transfers between devices  31.2 us (14%)
  starting transfers between devices  13.4 us (6%)
  local copies, waits for them, and re-layouts  6.47 us (3%)
  Pallas kernels  2.95 us (1%)
    all_to_all x4, blocking collectives, spread(): lax.all_to_all(jnp.broadcast_to(value[None], (copies,) + value.shape), ax...  120 us
    all_to_all x2, waiting for transfers between devices, spread(): lax.all_to_all(jnp.broadcast_to(value[None], (copies,) + value.shape), ax...  31.2 us
    all_to_all x1, blocking collectives, body(): stale = lax.all_to_all(stale_part[0], GRP, 0, 0, tiled=True)  27.4 us
    all_to_all x1, blocking collectives, body(): piece = jnp.sum(lax.all_to_all(grads, PLANE, 0, 0, tiled=True), axis=0)  17.4 us
    all_to_all x2, starting transfers between devices, spread(): lax.all_to_all(jnp.broadcast_to(value[None], (copies,) + value.shape), ax...  13.4 us
  transfers between devices with their start and end apart: 2, of which 2 were waited for; matrix products, arithmetic and copies ran while one was open for 0% of the time, Pallas kernels for 0%

profile of v1, /device:TPU:1, one launch (start us, length us, event | category | flops | bytes accessed | tf_op | source)
XLA Modules:
  0.0 220.3 jit_solution(3587722228250731655)
XLA Ops:
  0.6 27.4 %all_to_all.40.stale_ref = bf16[16,128,128]{2,1,0:T(8,128)(2,1)S(1)} all-to-all(bf16[16,128,128]{2,1,0:T(8,128)(2,1)} %bitcast.13), channel_id=1, replica_groups=mesh['y'=4,'x_lo'=2,'core'=2,'x_hi'=2,'z_far'=8,'z_near'=4] {'y','x_lo',..., dimensions={0} | all-to-all | bytes 1048576 | tf_op jit(solution)/shard_map/all_to_all | solution.py:108
  28.0 0.8 broadcast_in_dim.16
  28.8 46.1 %all_to_all.41 = bf16[8,128,128]{2,1,0:T(8,128)(2,1)S(1)} all-to-all(bf16[8,128,128]{2,1,0:T(8,128)(2,1)S(1)} %broadcast_in_dim.16), channel_id=1, replica_groups=mesh['y'=4,'x_lo'=2,'core'=2,'x_hi'=2,'z_far'=8,'z_near'=4] {'z_far'}, dimensions={0} | all-to-all | bytes 524288 | tf_op jit(solution)/shard_map/all_to_all | solution.py:19
  74.9 0.2 broadcast_in_dim.17
  75.1 39.2 %all_to_all.42 = bf16[4,8,128,128]{3,2,1,0:T(8,128)(2,1)S(1)} all-to-all(bf16[4,8,128,128]{3,2,1,0:T(8,128)(2,1)S(1)} %broadcast_in_dim.17), channel_id=1, replica_groups=mesh['y'=4,'x_lo'=2,'core'=2,'x_hi'=2,'z_far'=8,'z_near'=4] {'z_near'}, dimensions={0} | all-to-all | bytes 2097152 | tf_op jit(solution)/shard_map/all_to_all | solution.py:19
  114.3 1.8 broadcast_in_dim.18
  116.2 0.0 copy-start.5
  116.2 0.0 copy-start.6
  116.2 3.9 %all-to-all-start.2 = ((bf16[2,4,8,128,128]{4,3,2,1,0:T(8,128)(2,1)}), bf16[2,4,8,128,128]{4,3,2,1,0:T(8,128)(2,1)S(1)}, u32[]{:S(2)}, u32[]{:S(2)}) async-start(bf16[2,4,8,128,128]{4,3,2,1,0:T(8,128)(2,1)} %broadcast_in_dim.18), calls=%async_computation.2 | async-start | bytes 4194304 | tf_op jit(solution)/shard_map/all_to_all | solution.py:19
  120.8 23.5 %all-to-all-done.2 = bf16[2,4,8,128,128]{4,3,2,1,0:T(8,128)(2,1)S(1)} async-done(((bf16[2,4,8,128,128]{4,3,2,1,0:T(8,128)(2,1)}), bf16[2,4,8,128,128]{4,3,2,1,0:T(8,128)(2,1)S(1)}, u32[]{:S(2)}, u32[]{:S(2)}) %all-to-all-start.2) | async-done | bytes 2097184 | tf_op jit(solution)/shard_map/all_to_all | solution.py:19
  144.3 0.0 copy-done.4
  144.4 0.0 copy-done.5
  144.4 0.0 copy-done.6
  144.4 0.0 copy-start
  144.4 1.6 copy-done
  146.0 2.9 %shard_map.128 = (bf16[16,128,128]{2,1,0:T(8,128)(2,1)}, bf16[128,256]{1,0:T(8,128)(2,1)}, f32[32,8,384]{2,1,0:T(8,128)S(1)}) custom-call(s32[1]{0:T(128)S(6)} %copy.14.count_ref, s32[16]{0:T(128)S(1)} %copy-done.6, s32[64]{0:T(128)S(1)} %fusion.2.place_ref, s32[1]{0:T(128)} %bitcast.own_ref, bf16[16,256,256]{2,1,0:T(8,128)(2,1)S(1)} %copy-done, ...), custom_call_target="tpu_custom_call" | custom-call | tf_op jit(solution)/shard_map/pallas_call | solution.py:120
  148.9 17.4 %all_to_all.43 = f32[32,8,384]{2,1,0:T(8,128)S(1)} all-to-all(f32[32,8,384]{2,1,0:T(8,128)S(1)} %get-tuple-element.10), channel_id=1, replica_groups=mesh['y'=4,'x_lo'=2,'core'=2,'x_hi'=2,'z_far'=8,'z_near'=4] {'y','x_lo',..., dimensions={0} | all-to-all | bytes 786432 | tf_op jit(solution)/shard_map/all_to_all | solution.py:147
  166.4 27.8 %all_to_all.44 = f32[8,8,384]{2,1,0:T(8,128)S(1)} all-to-all(f32[8,8,384]{2,1,0:T(8,128)S(1)} %broadcast_in_dim.21), channel_id=1, replica_groups=mesh['y'=4,'x_lo'=2,'core'=2,'x_hi'=2,'z_far'=8,'z_near'=4] {'z_far'}, dimensions={0} | all-to-all | bytes 196608 | tf_op jit(solution)/shard_map/all_to_all | solution.py:19
  194.2 6.9 %all_to_all.45 = f32[4,8,384]{2,1,0:T(8,128)S(1)} all-to-all(f32[4,8,384]{2,1,0:T(8,128)S(1)} %broadcast_in_dim.22), channel_id=1, replica_groups=mesh['y'=4,'x_lo'=2,'core'=2,'x_hi'=2,'z_far'=8,'z_near'=4] {'z_near'}, dimensions={0} | all-to-all | bytes 98304 | tf_op jit(solution)/shard_map/all_to_all | solution.py:19
  201.2 0.7 broadcast_in_dim.23
  201.9 9.5 %all-to-all-start.7 = ((f32[32,8,256]{2,1,0:T(8,128)}), f32[32,8,256]{2,1,0:T(8,128)S(1)}, u32[]{:S(2)}, u32[]{:S(2)}) async-start(f32[32,8,256]{2,1,0:T(8,128)} %broadcast_in_dim.23), calls=%async_computation.7 | async-start | bytes 524288 | tf_op jit(solution)/shard_map/all_to_all | solution.py:19
  211.3 0.6 slice_bitcast_fusion.2
  211.9 7.7 %all-to-all-done.7 = f32[32,8,256]{2,1,0:T(8,128)S(1)} async-done(((f32[32,8,256]{2,1,0:T(8,128)}), f32[32,8,256]{2,1,0:T(8,128)S(1)}, u32[]{:S(2)}, u32[]{:S(2)}) %all-to-all-start.7) | async-done | bytes 262176 | tf_op jit(solution)/shard_map/all_to_all | solution.py:19
  219.6 0.7 slice_bitcast_fusion
  (15 shorter events, 0.1 us)
Async XLA Ops:
  116.2 28.2 %copy-start.1 = (bf16[128,128]{1,0:T(8,128)(2,1)S(1)}, bf16[128,128]{1,0:T(8,128)(2,1)}, u32[]{:S(2)}) copy-start(bf16[128,128]{1,0:T(8,128)(2,1)} %feats_ref.1) | copy-start | bytes 98308
  116.2 28.2 %copy-start.2 = (bf16[128,256]{1,0:T(8,128)(2,1)S(1)}, bf16[128,256]{1,0:T(8,128)(2,1)}, u32[]{:S(2)}) copy-start(bf16[128,256]{1,0:T(8,128)(2,1)} %w_self_ref.1) | copy-start | bytes 196612
  116.2 28.2 %copy-start.3 = (bf16[128,256]{1,0:T(8,128)(2,1)S(1)}, bf16[128,256]{1,0:T(8,128)(2,1)}, u32[]{:S(2)}) copy-start(bf16[128,256]{1,0:T(8,128)(2,1)} %w_neigh_ref.1) | copy-start | bytes 196612
  116.2 28.2 %copy-start.4 = (bf16[128,256]{1,0:T(8,128)(2,1)S(1)}, bf16[128,256]{1,0:T(8,128)(2,1)}, u32[]{:S(2)}) copy-start(bf16[128,256]{1,0:T(8,128)(2,1)} %cot_ref.1) | copy-start | bytes 196612
  116.2 28.2 %copy-start.5 = (f32[256]{0:T(256)S(1)}, f32[256]{0:T(256)}, u32[]{:S(2)}) copy-start(f32[256]{0:T(256)} %param.16) | copy-start | bytes 3076
  116.2 28.2 %copy-start.6 = (s32[16]{0:T(128)S(1)}, s32[16]{0:T(128)}, u32[]{:S(2)}) copy-start(s32[16]{0:T(128)} %pos_ref.1) | copy-start | bytes 196
  116.2 28.1 %all-to-all-start.2 = ((bf16[2,4,8,128,128]{4,3,2,1,0:T(8,128)(2,1)}), bf16[2,4,8,128,128]{4,3,2,1,0:T(8,128)(2,1)S(1)}, u32[]{:S(2)}, u32[]{:S(2)}) async-start(bf16[2,4,8,128,128]{4,3,2,1,0:T(8,128)(2,1)} %broadcast_in_dim.18), calls=%async_computation.2 | async-start | bytes 4194304 | tf_op jit(solution)/shard_map/all_to_all | solution.py:19
  144.4 1.6 copy-start
  201.9 17.7 %all-to-all-start.7 = ((f32[32,8,256]{2,1,0:T(8,128)}), f32[32,8,256]{2,1,0:T(8,128)S(1)}, u32[]{:S(2)}, u32[]{:S(2)}) async-start(f32[32,8,256]{2,1,0:T(8,128)} %broadcast_in_dim.23), calls=%async_computation.7 | async-start | bytes 524288 | tf_op jit(solution)/shard_map/all_to_all | solution.py:19

commit v2 on v1

--- a/solution.py
+++ b/solution.py
@@ -9,9 +9,11 @@
 
 GRP = ("y", "x_lo", "core")
 PLANE = ("y", "x_lo", "core", "x_hi")
-BLK = ("x_hi", "z_far", "z_near")
+LINE = ("z_far", "z_mid", "z_near")
+EVERY_OTHER = ("z_far", "z_mid")
+BLK = ("x_hi",) + LINE
 ALL = GRP + BLK
-SIZES = (4, 2, 2, 2, 8, 4)
+SIZES = (4, 2, 2, 2, 8, 2, 2)
 
 
 def spread(value, axes):
@@ -27,7 +29,12 @@
     place_ref,
     own_ref,
     adj_ref,
-    rows_ref,
+    same_ref,
+    left_ref,
+    right_ref,
+    side_ref,
+    side_left_ref,
+    side_right_ref,
     stale_ref,
     feats_ref,
     w_self_ref,
@@ -38,11 +45,14 @@
     hidden_ref,
     grads_ref,
     acc_ref,
+    source_ref,
 ):
     tile = adj_ref.shape[1]
     groups, node_dev, width = part_ref.shape
     per_tile = tile // node_dev
-    col_tiles = rows_ref.shape[0] // per_tile
+    banks = (same_ref, left_ref, right_ref, side_ref, side_left_ref, side_right_ref)
+    slots = same_ref.shape[0]
+    col_tiles = place_ref.shape[0] // per_tile
     own = own_ref[0]
     acc_ref[...] = jnp.zeros_like(acc_ref)
 
@@ -50,10 +60,16 @@
         position = pos_ref[slot]
         row_tile = lax.div(position, col_tiles)
         first = lax.rem(position, col_tiles) * per_tile
-        source = jnp.concatenate(
-            [rows_ref[place_ref[first + j]] for j in range(per_tile)], axis=0
-        )
-        product = jnp.dot(adj_ref[slot], source, preferred_element_type=jnp.float32)
+        for j in range(per_tile):
+            place = place_ref[first + j]
+            bank, block = lax.div(place, slots), lax.rem(place, slots)
+            for choice, ref in enumerate(banks):
+
+                @pl.when(bank == choice)
+                def _():
+                    source_ref[j * node_dev : (j + 1) * node_dev, :] = ref[block]
+
+        product = jnp.dot(adj_ref[slot], source_ref[...], preferred_element_type=jnp.float32)
         rows = pl.ds(pl.multiple_of(row_tile * tile, tile), tile)
         acc_ref[rows, :] += product
         return carry
@@ -103,15 +119,29 @@
     groups = lax.axis_size(GRP)
     blocks = lax.axis_size(BLK)
     plane = lax.axis_size(PLANE)
-    far, near, sides = SIZES[4], SIZES[5], SIZES[3]
 
     stale = lax.all_to_all(stale_part[0], GRP, 0, 0, tiled=True)
-    rows = spread(node_feats, "z_far")
-    rows = spread(rows, "z_near")
-    rows = spread(rows, "x_hi").reshape(blocks, node_dev, width)
+    same = lax.all_gather(node_feats, EVERY_OTHER)
+    length = lax.axis_size(LINE)
+    up = [(i, (i + 1) % length) for i in range(length)]
+    down = [(i, (i - 1) % length) for i in range(length)]
+    half = same.shape[0] // 2
+    side = lax.ppermute(same, "x_hi", [(0, 1), (1, 0)])
+    banks = (
+        same,
+        lax.ppermute(same[:half], LINE, up),
+        lax.ppermute(same[half:], LINE, down),
+        side,
+        lax.ppermute(side[:half], LINE, up),
+        lax.ppermute(side[half:], LINE, down),
+    )
     index = jnp.arange(blocks, dtype=jnp.int32)
-    side, line = index // (far * near), index % (far * near)
-    place = side * (far * near) + (line % near) * far + line // near
+    other_side = index // length != lax.axis_index("x_hi")
+    other_parity = index % 2 != lax.axis_index("z_near")
+    slot = index % length // 2
+    slots = 2 * half
+    across = jnp.where(slot < half, slots + slot, 2 * slots + slot - half)
+    place = jnp.where(other_parity, across, slot) + jnp.where(other_side, 3 * slots, 0)
     own = lax.axis_index(GRP).reshape(1).astype(jnp.int32)
 
     smem = pl.BlockSpec(memory_space=pltpu.SMEM)
@@ -124,9 +154,12 @@
             jax.ShapeDtypeStruct((node_dev, hid), jnp.bfloat16),
             jax.ShapeDtypeStruct((plane, piece_rows, hid + hid // 2), jnp.float32),
         ),
-        in_specs=[smem] * 4 + [vmem] * 8,
+        in_specs=[smem] * 4 + [vmem] * 13,
         out_specs=(vmem, vmem, vmem),
-        scratch_shapes=[pltpu.VMEM((groups * node_dev, width), jnp.float32)],
+        scratch_shapes=[
+            pltpu.VMEM((groups * node_dev, width), jnp.float32),
+            pltpu.VMEM((adj_tiles.shape[1], width), jnp.bfloat16),
+        ],
         compiler_params=pltpu.CompilerParams(vmem_limit_bytes=32 * 1024 * 1024),
     )(
         tile_count,
@@ -134,7 +167,7 @@
         place,
         own,
         adj_tiles,
-        rows,
+        *banks,
         stale,
         node_feats,
         w_self,
@@ -145,8 +178,9 @@
 
     scaling = float(node_dev * groups * blocks) ** (-0.5)
     piece = jnp.sum(lax.all_to_all(grads, PLANE, 0, 0, tiled=True), axis=0)
-    piece = jnp.sum(spread(piece, "z_far"), axis=0)
-    piece = jnp.sum(spread(piece, "z_near"), axis=0) * scaling
+    piece = spread(piece.astype(jnp.bfloat16), "z_far")
+    piece = jnp.sum(piece.astype(jnp.float32), axis=0)
+    piece = jnp.sum(spread(piece, ("z_mid", "z_near")), axis=0) * scaling
     grad_bias = piece[:2, hid:].reshape(hid)
     whole = spread(piece[:, :hid], PLANE).reshape(2 * width, hid)
     return new_part[None], hidden, whole[:width], whole[width:], grad_bias

time: 221 us -> 167 us (0.76)
  blocking collectives: 165 us -> 106 us
  starting transfers between devices: 13.4 us -> 36.5 us
  waiting for transfers between devices: 31.2 us -> 14.1 us
    all_to_all x4 -> x2, blocking collectives: 120 us -> 40.9 us  [spread(): lax.all_to_all(jnp.broadcast_to(value[None], (copies,) + value.shape), ax...]
    all_gather x0 -> x1, blocking collectives: none -> 45.3 us  [body(): same = lax.all_gather(node_feats, EVERY_OTHER)]
    all_to_all x1 -> x0, blocking collectives: 27.4 us -> none  [body(): stale = lax.all_to_all(stale_part[0], GRP, 0, 0, tiled=True)]
    all_to_all x2 -> x1, waiting for transfers between devices: 31.2 us -> 7.79 us  [spread(): lax.all_to_all(jnp.broadcast_to(value[None], (copies,) + value.shape), ax...]
    ppermute x0 -> x5, starting transfers between devices: none -> 16.4 us  [the longest x1 4.6 us: body(): side = lax.ppermute(same, 'x_hi', [(0, 1), (1, 0)])]
    all_to_all x0 -> x1, starting transfers between devices: none -> 12 us  [body(): stale = lax.all_to_all(stale_part[0], GRP, 0, 0, tiled=True)]
    ppermute x0 -> x5, waiting for transfers between devices: none -> 6.3 us  [the longest x1 4.59 us: body(): lax.ppermute(side[half:], LINE, down)]
    all_to_all x2 -> x1, starting transfers between devices: 13.4 us -> 8.16 us  [spread(): lax.all_to_all(jnp.broadcast_to(value[None], (copies,) + value.shape), ax...]
  transfers between devices with their start and end apart: 2 -> 7, of which waited for: 2 -> 3; matrix products, arithmetic and copies ran while one was open for 0% -> 1% of each run, Pallas kernels for 0% -> 0%
where the time goes in v2:
time: 167 us
  blocking collectives  106 us (63%)
  starting transfers between devices  36.5 us (22%)
  waiting for transfers between devices  14.1 us (8%)
  local copies, waits for them, and re-layouts  5.37 us (3%)
  Pallas kernels  3.12 us (2%)
    all_gather x1, blocking collectives, body(): same = lax.all_gather(node_feats, EVERY_OTHER)  45.3 us
    all_to_all x2, blocking collectives, spread(): lax.all_to_all(jnp.broadcast_to(value[None], (copies,) + value.shape), ax...  40.9 us
    all_to_all x1, blocking collectives, body(): piece = jnp.sum(lax.all_to_all(grads, PLANE, 0, 0, tiled=True), axis=0)  19.7 us
    all_to_all x1, starting transfers between devices, body(): stale = lax.all_to_all(stale_part[0], GRP, 0, 0, tiled=True)  12 us
    all_to_all x1, starting transfers between devices, spread(): lax.all_to_all(jnp.broadcast_to(value[None], (copies,) + value.shape), ax...  8.16 us
    all_to_all x1, waiting for transfers between devices, spread(): lax.all_to_all(jnp.broadcast_to(value[None], (copies,) + value.shape), ax...  7.79 us
    ppermute x1, starting transfers between devices, body(): side = lax.ppermute(same, 'x_hi', [(0, 1), (1, 0)])  4.6 us
    ppermute x1, waiting for transfers between devices, body(): lax.ppermute(side[half:], LINE, down)  4.59 us
  transfers between devices with their start and end apart: 7, of which 3 were waited for; matrix products, arithmetic and copies ran while one was open for 1% of the time, Pallas kernels for 0%

profile of v2, /device:TPU:1, one launch (start us, length us, event | category | flops | bytes accessed | tf_op | source)
XLA Modules:
  0.0 166.6 jit_solution(14858883804596914232)
XLA Ops:
  0.7 45.3 %all-gather = bf16[2048,128]{1,0:T(8,128)(2,1)S(1)} all-gather(bf16[128,128]{1,0:T(8,128)(2,1)} %feats_ref.1), channel_id=2, replica_groups=mesh['y'=4,'x_lo'=2,'core'=2,'x_hi'=2,'z_far'=8,'z_mid'=2,'z_near'=2] {'..., dimensions={0}, use_global_device_ids=true | all-gather | bytes 557056 | tf_op jit(solution)/shard_map/all_gather | solution.py:124
  46.0 4.6 %collective-permute-start.2 = (bf16[16,128,128]{2,1,0:T(8,128)(2,1)S(1)}, bf16[16,128,128]{2,1,0:T(8,128)(2,1)S(1)}, u32[]{:S(2)}, u32[]{:S(2)}) collective-permute-start(bf16[16,128,128]{2,1,0:T(8,128)(2,1)S(1)} %bitcast.13), channel_id=1, source_target_pairs={{0,32},{32,0},{1,33},{33,1},{2,34},{34,2},{3,35},{35,3},{4,36},{36... | collective-permute-start | bytes 1572872 | tf_op jit(solution)/shard_map/ppermute | solution.py:129
  50.6 12.0 %all-to-all-start = ((bf16[16,128,128]{2,1,0:T(8,128)(2,1)}), bf16[16,128,128]{2,1,0:T(8,128)(2,1)}, u32[]{:S(2)}, u32[]{:S(2)}) async-start(bf16[16,128,128]{2,1,0:T(8,128)(2,1)} %bitcast.16), calls=%async_computation | async-start | bytes 1048576 | tf_op jit(solution)/shard_map/all_to_all | solution.py:123
  62.6 0.8 fusion.2
  63.4 2.6 %collective-permute-start = (bf16[8,128,128]{2,1,0:T(8,128)(2,1)}, bf16[8,128,128]{2,1,0:T(8,128)(2,1)S(1)}, u32[]{:S(2)}, u32[]{:S(2)}) collective-permute-start(bf16[8,128,128]{2,1,0:T(8,128)(2,1)} %bitcast.2), channel_id=1, source_target_pairs={{0,1},{1,2},{2,3},{3,4},{4,5},{5,6},{6,7},{7,8},{8,9},{9,10},{10,1... | collective-permute-start | bytes 786440 | tf_op jit(solution)/shard_map/ppermute | solution.py:132
  66.0 3.9 %collective-permute-start.1 = (bf16[8,128,128]{2,1,0:T(8,128)(2,1)}, bf16[8,128,128]{2,1,0:T(8,128)(2,1)}, u32[]{:S(2)}, u32[]{:S(2)}) collective-permute-start(bf16[8,128,128]{2,1,0:T(8,128)(2,1)} %bitcast.3), channel_id=1, source_target_pairs={{0,31},{1,0},{2,1},{3,2},{4,3},{5,4},{6,5},{7,6},{8,7},{9,8},{10,9... | collective-permute-start | bytes 786440 | tf_op jit(solution)/shard_map/ppermute | solution.py:133
  69.9 0.0 collective-permute-done.2.side_ref
  69.9 0.8 fusion.1
  70.8 2.1 %collective-permute-start.4 = (bf16[8,128,128]{2,1,0:T(8,128)(2,1)}, bf16[8,128,128]{2,1,0:T(8,128)(2,1)}, u32[]{:S(2)}, u32[]{:S(2)}) collective-permute-start(bf16[8,128,128]{2,1,0:T(8,128)(2,1)} %get-tuple-element.11), channel_id=1, source_target_pairs={{0,31},{1,0},{2,1},{3,2},{4,3},{5,4},{6,5},{7,6},{8,7},{9,8},{10,9... | collective-permute-start | bytes 786440 | tf_op jit(solution)/shard_map/ppermute | solution.py:136
  72.8 3.2 %collective-permute-start.3 = (bf16[8,128,128]{2,1,0:T(8,128)(2,1)}, bf16[8,128,128]{2,1,0:T(8,128)(2,1)}, u32[]{:S(2)}, u32[]{:S(2)}) collective-permute-start(bf16[8,128,128]{2,1,0:T(8,128)(2,1)} %get-tuple-element.12), channel_id=1, source_target_pairs={{0,1},{1,2},{2,3},{3,4},{4,5},{5,6},{6,7},{7,8},{8,9},{9,10},{10,1... | collective-permute-start | bytes 786440 | tf_op jit(solution)/shard_map/ppermute | solution.py:135
  76.8 4.6 %collective-permute-done.4.side_right_ref = bf16[8,128,128]{2,1,0:T(8,128)(2,1)} collective-permute-done((bf16[8,128,128]{2,1,0:T(8,128)(2,1)}, bf16[8,128,128]{2,1,0:T(8,128)(2,1)}, u32[]{:S(2)}, u32[]{:S(2)}) %collective-permute-start.4) | collective-permute-done | bytes 262176 | tf_op jit(solution)/shard_map/ppermute | solution.py:136
  81.4 1.7 %collective-permute-done.3.side_left_ref = bf16[8,128,128]{2,1,0:T(8,128)(2,1)} collective-permute-done((bf16[8,128,128]{2,1,0:T(8,128)(2,1)}, bf16[8,128,128]{2,1,0:T(8,128)(2,1)}, u32[]{:S(2)}, u32[]{:S(2)}) %collective-permute-start.3) | collective-permute-done | bytes 262176 | tf_op jit(solution)/shard_map/ppermute | solution.py:135
  83.1 0.0 copy-start.3
  83.1 0.8 copy-done.3
  83.9 0.8 copy-done.4
  84.8 3.1 %shard_map.128 = (bf16[16,128,128]{2,1,0:T(8,128)(2,1)}, bf16[128,256]{1,0:T(8,128)(2,1)}, f32[32,8,384]{2,1,0:T(8,128)S(1)}) custom-call(s32[1]{0:T(128)S(6)} %copy.14.count_ref, s32[16]{0:T(128)S(1)} %copy-done.6, s32[64]{0:T(128)S(1)} %fusion.place_ref, s32[1]{0:T(128)} %bitcast.own_ref, bf16[16,256,256]{2,1,0:T(8,128)(2,1)S(1)} %copy-done, ...), custom_call_target="tpu_custom_call" | custom-call | tf_op jit(solution)/shard_map/pallas_call | solution.py:150
  87.9 19.7 %all_to_all.25 = f32[32,8,384]{2,1,0:T(8,128)S(1)} all-to-all(f32[32,8,384]{2,1,0:T(8,128)S(1)} %get-tuple-element.10), channel_id=1, replica_groups=mesh['y'=4,'x_lo'=2,'core'=2,'x_hi'=2,'z_far'=8,'z_mid'=2,'z_near'=2] {'..., dimensions={0} | all-to-all | bytes 786432 | tf_op jit(solution)/shard_map/all_to_all | solution.py:180
  107.7 33.8 %all_to_all.26 = bf16[8,8,384]{2,1,0:T(8,128)(2,1)S(1)} all-to-all(bf16[8,8,384]{2,1,0:T(8,128)(2,1)S(1)} %broadcast_in_dim.33), channel_id=1, replica_groups=mesh['y'=4,'x_lo'=2,'core'=2,'x_hi'=2,'z_far'=8,'z_mid'=2,'z_near'=2] {'..., dimensions={0} | all-to-all | bytes 98304 | tf_op jit(solution)/shard_map/all_to_all | solution.py:21
  141.6 7.1 %all_to_all.27 = f32[4,8,384]{2,1,0:T(8,128)S(1)} all-to-all(f32[4,8,384]{2,1,0:T(8,128)S(1)} %broadcast_in_dim.34), channel_id=1, replica_groups=mesh['y'=4,'x_lo'=2,'core'=2,'x_hi'=2,'z_far'=8,'z_mid'=2,'z_near'=2] {'..., dimensions={0} | all-to-all | bytes 98304 | tf_op jit(solution)/shard_map/all_to_all | solution.py:21
  148.7 0.7 broadcast_in_dim.35
  149.4 8.2 %all-to-all-start.4 = ((f32[32,8,256]{2,1,0:T(8,128)}), f32[32,8,256]{2,1,0:T(8,128)S(1)}, u32[]{:S(2)}, u32[]{:S(2)}) async-start(f32[32,8,256]{2,1,0:T(8,128)} %broadcast_in_dim.35), calls=%async_computation.4 | async-start | bytes 524288 | tf_op jit(solution)/shard_map/all_to_all | solution.py:21
  157.6 0.6 slice_bitcast_fusion.2
  158.1 7.8 %all-to-all-done.4 = f32[32,8,256]{2,1,0:T(8,128)S(1)} async-done(((f32[32,8,256]{2,1,0:T(8,128)}), f32[32,8,256]{2,1,0:T(8,128)S(1)}, u32[]{:S(2)}, u32[]{:S(2)}) %all-to-all-start.4) | async-done | bytes 262176 | tf_op jit(solution)/shard_map/all_to_all | solution.py:21
  165.9 0.7 slice_bitcast_fusion
  (22 shorter events, 0.1 us)
Async XLA Ops:
  0.6 82.4 %copy-start.1 = (bf16[128,128]{1,0:T(8,128)(2,1)S(1)}, bf16[128,128]{1,0:T(8,128)(2,1)}, u32[]{:S(2)}) copy-start(bf16[128,128]{1,0:T(8,128)(2,1)} %feats_ref.1) | copy-start | bytes 98308
  0.6 82.4 %copy-start.5 = (f32[256]{0:T(256)S(1)}, f32[256]{0:T(256)}, u32[]{:S(2)}) copy-start(f32[256]{0:T(256)} %param.16) | copy-start | bytes 3076
  0.7 82.4 %copy-start.2 = (bf16[128,256]{1,0:T(8,128)(2,1)S(1)}, bf16[128,256]{1,0:T(8,128)(2,1)}, u32[]{:S(2)}) copy-start(bf16[128,256]{1,0:T(8,128)(2,1)} %w_self_ref.1) | copy-start | bytes 196612
  0.7 82.4 %copy-start.6 = (s32[16]{0:T(128)S(1)}, s32[16]{0:T(128)}, u32[]{:S(2)}) copy-start(s32[16]{0:T(128)} %pos_ref.1) | copy-start | bytes 196
  0.7 82.4 %copy-start = (bf16[16,256,256]{2,1,0:T(8,128)(2,1)S(1)}, bf16[16,256,256]{2,1,0:T(8,128)(2,1)}, u32[]{:S(2)}) copy-start(bf16[16,256,256]{2,1,0:T(8,128)(2,1)} %adj_ref.1) | copy-start | bytes 6291460
  46.0 23.9 %collective-permute-start.2 = (bf16[16,128,128]{2,1,0:T(8,128)(2,1)S(1)}, bf16[16,128,128]{2,1,0:T(8,128)(2,1)S(1)}, u32[]{:S(2)}, u32[]{:S(2)}) collective-permute-start(bf16[16,128,128]{2,1,0:T(8,128)(2,1)S(1)} %bitcast.13), channel_id=1, source_target_pairs={{0,32},{32,0},{1,33},{33,1},{2,34},{34,2},{3,35},{35,3},{4,36},{36... | collective-permute-start | bytes 1572872 | tf_op jit(solution)/shard_map/ppermute | solution.py:129
  50.6 26.1 %all-to-all-start = ((bf16[16,128,128]{2,1,0:T(8,128)(2,1)}), bf16[16,128,128]{2,1,0:T(8,128)(2,1)}, u32[]{:S(2)}, u32[]{:S(2)}) async-start(bf16[16,128,128]{2,1,0:T(8,128)(2,1)} %bitcast.16), calls=%async_computation | async-start | bytes 1048576 | tf_op jit(solution)/shard_map/all_to_all | solution.py:123
  63.4 13.3 %collective-permute-start = (bf16[8,128,128]{2,1,0:T(8,128)(2,1)}, bf16[8,128,128]{2,1,0:T(8,128)(2,1)S(1)}, u32[]{:S(2)}, u32[]{:S(2)}) collective-permute-start(bf16[8,128,128]{2,1,0:T(8,128)(2,1)} %bitcast.2), channel_id=1, source_target_pairs={{0,1},{1,2},{2,3},{3,4},{4,5},{5,6},{6,7},{7,8},{8,9},{9,10},{10,1... | collective-permute-start | bytes 786440 | tf_op jit(solution)/shard_map/ppermute | solution.py:132
  66.0 10.8 %collective-permute-start.1 = (bf16[8,128,128]{2,1,0:T(8,128)(2,1)}, bf16[8,128,128]{2,1,0:T(8,128)(2,1)}, u32[]{:S(2)}, u32[]{:S(2)}) collective-permute-start(bf16[8,128,128]{2,1,0:T(8,128)(2,1)} %bitcast.3), channel_id=1, source_target_pairs={{0,31},{1,0},{2,1},{3,2},{4,3},{5,4},{6,5},{7,6},{8,7},{9,8},{10,9... | collective-permute-start | bytes 786440 | tf_op jit(solution)/shard_map/ppermute | solution.py:133
  70.8 10.6 %collective-permute-start.4 = (bf16[8,128,128]{2,1,0:T(8,128)(2,1)}, bf16[8,128,128]{2,1,0:T(8,128)(2,1)}, u32[]{:S(2)}, u32[]{:S(2)}) collective-permute-start(bf16[8,128,128]{2,1,0:T(8,128)(2,1)} %get-tuple-element.11), channel_id=1, source_target_pairs={{0,31},{1,0},{2,1},{3,2},{4,3},{5,4},{6,5},{7,6},{8,7},{9,8},{10,9... | collective-permute-start | bytes 786440 | tf_op jit(solution)/shard_map/ppermute | solution.py:136
  72.8 10.2 %collective-permute-start.3 = (bf16[8,128,128]{2,1,0:T(8,128)(2,1)}, bf16[8,128,128]{2,1,0:T(8,128)(2,1)}, u32[]{:S(2)}, u32[]{:S(2)}) collective-permute-start(bf16[8,128,128]{2,1,0:T(8,128)(2,1)} %get-tuple-element.12), channel_id=1, source_target_pairs={{0,1},{1,2},{2,3},{3,4},{4,5},{5,6},{6,7},{7,8},{8,9},{9,10},{10,1... | collective-permute-start | bytes 786440 | tf_op jit(solution)/shard_map/ppermute | solution.py:135
  83.1 0.8 copy-start.3
  83.9 0.8 copy-start.4
  149.4 16.5 %all-to-all-start.4 = ((f32[32,8,256]{2,1,0:T(8,128)}), f32[32,8,256]{2,1,0:T(8,128)S(1)}, u32[]{:S(2)}, u32[]{:S(2)}) async-start(f32[32,8,256]{2,1,0:T(8,128)} %broadcast_in_dim.35), calls=%async_computation.4 | async-start | bytes 524288 | tf_op jit(solution)/shard_map/all_to_all | solution.py:21

commit v3 on v1

v3 whole, which is shorter than its diff:
```python
import jax
import jax.numpy as jnp
from jax import lax
from jax.experimental import pallas as pl
from jax.experimental.pallas import tpu as pltpu
from jax.sharding import Mesh, PartitionSpec as P

GRP = ("y", "x_lo", "core")
PLANE = ("y", "x_lo", "core", "x_hi")
LINE = ("z_far", "z_mid", "z_near")
EVERY_OTHER = ("z_far", "z_mid")
BLK = ("x_hi",) + LINE
ALL = GRP + BLK
SIZES = (4, 2, 2, 2, 8, 2, 2)


def spread(value, axes):
    copies = lax.axis_size(axes)
    return lax.all_to_all(
        jnp.broadcast_to(value[None], (copies,) + value.shape), axes, 0, 0, tiled=True
    )


def split_position(position, col_tiles, per_tile):
    return lax.div(position, col_tiles), lax.rem(position, col_tiles) * per_tile


def layer_kernel(
    count_ref,
    pos_ref,
    place_ref,
    own_ref,
    adj_ref,
    bank_refs,
    stale_ref,
    feats_ref,
    w_self_ref,
    w_neigh_ref,
    bias_ref,
    cot_ref,
    hidden_ref,
    grads_ref,
    pos_out_ref,
    tiles_ref,
    sources_ref,
    stale_vmem,
    feats_vmem,
    w_self_vmem,
    w_neigh_vmem,
    cot_vmem,
    tile_sem,
    source_sem,
    dense_sem,
):
    tile = adj_ref.shape[1]
    groups, node_dev, width = stale_ref.shape
    per_tile = tile // node_dev
    bank_slots = bank_refs[0].shape[0]
    col_tiles = place_ref.shape[0] // per_tile
    own = own_ref[0]
    own_tile, own_part = lax.div(own, per_tile), lax.rem(own, per_tile)
    count = count_ref[0]

    dense = [
        pltpu.make_async_copy(src, dst, dense_sem.at[i])
        for i, (src, dst) in enumerate(
            (
                (stale_ref, stale_vmem),
                (feats_ref, feats_vmem),
                (w_self_ref, w_self_vmem),
                (w_neigh_ref, w_neigh_vmem),
                (cot_ref, cot_vmem),
            )
        )
    ]

    def tile_copy(slot):
        rows = pl.ds(pl.multiple_of(own_part * node_dev, node_dev), node_dev)
        return pltpu.make_async_copy(
            adj_ref.at[slot, rows, :], tiles_ref.at[slot], tile_sem.at[slot]
        )

    def source_copy(slot, j, bank, block):
        return pltpu.make_async_copy(
            bank.at[block],
            sources_ref.at[slot, pl.ds(j * node_dev, node_dev), :],
            source_sem.at[slot, j],
        )

    def fetch(slot, carry):
        pos_out_ref[slot] = pos_ref[slot]
        row_tile, first = split_position(pos_ref[slot], col_tiles, per_tile)

        @pl.when((row_tile == own_tile) & (slot < count))
        def _():
            tile_copy(slot).start()
            for j in range(per_tile):
                place = place_ref[first + j]
                bank, block = lax.div(place, bank_slots), lax.rem(place, bank_slots)
                for choice, ref in enumerate(bank_refs):

                    @pl.when(bank == choice)
                    def _():
                        source_copy(slot, j, ref, block).start()

        return carry

    lax.fori_loop(0, pos_ref.shape[0], fetch, 0)
    for copy in dense:
        copy.start()

    def add_tile(slot, fresh):
        row_tile, _ = split_position(pos_ref[slot], col_tiles, per_tile)

        def add():
            tile_copy(slot).wait()
            for j in range(per_tile):
                source_copy(slot, j, bank_refs[0], 0).wait()
            return fresh + jnp.dot(
                tiles_ref[slot], sources_ref[slot], preferred_element_type=jnp.float32
            )

        return lax.cond(row_tile == own_tile, add, lambda: fresh)

    fresh = lax.fori_loop(0, count, add_tile, jnp.zeros((node_dev, width), jnp.float32))
    for copy in dense:
        copy.wait()
    stale = jnp.zeros((node_dev, width), jnp.float32)
    for source in range(groups):
        keep = jnp.where(source == own, jnp.float32(0.0), jnp.float32(1.0))
        stale += stale_vmem[source].astype(jnp.float32) * keep
    aggregate = (fresh + stale).astype(jnp.bfloat16)
    feats = feats_vmem[...]
    preact = jnp.dot(feats, w_self_vmem[...], preferred_element_type=jnp.float32)
    preact += jnp.dot(aggregate, w_neigh_vmem[...], preferred_element_type=jnp.float32)
    preact += bias_ref[...]
    gate = jax.nn.sigmoid(preact)
    hidden_ref[...] = (preact * gate).astype(hidden_ref.dtype)
    grad_pre = (
        cot_vmem[...].astype(jnp.float32) * gate * (1.0 + preact * (1.0 - gate))
    ).astype(jnp.bfloat16)
    both = jnp.concatenate([feats, aggregate], axis=1)
    grads = lax.dot_general(
        both, grad_pre, (((0,), (0,)), ((), ())), preferred_element_type=jnp.float32
    )
    bias_grad = jnp.sum(grad_pre.astype(jnp.float32), axis=0, keepdims=True)
    pieces, piece_rows, _ = grads_ref.shape
    hid = grads.shape[1]
    grads_ref[:, :, :hid] = grads.reshape(pieces, piece_rows, hid).astype(grads_ref.dtype)
    half = hid // 2
    tail = jnp.concatenate(
        [
            bias_grad[:, :half],
            bias_grad[:, half:],
            jnp.zeros((piece_rows - 2, half), jnp.float32),
        ],
        axis=0,
    )
    grads_ref[:, :, hid:] = jnp.broadcast_to(tail[None], (pieces, piece_rows, half)).astype(
        grads_ref.dtype
    )


def partial_kernel(
    count_ref, pos_ref, place_ref, adj_ref, bank_refs, part_ref, acc_ref, source_ref
):
    tile = adj_ref.shape[1]
    _, node_dev, _ = part_ref.shape
    per_tile = tile // node_dev
    bank_slots = bank_refs[0].shape[0]
    col_tiles = place_ref.shape[0] // per_tile
    acc_ref[...] = jnp.zeros_like(acc_ref)

    def add_tile(slot, carry):
        row_tile, first = split_position(pos_ref[slot], col_tiles, per_tile)
        for j in range(per_tile):
            place = place_ref[first + j]
            bank, block = lax.div(place, bank_slots), lax.rem(place, bank_slots)
            for choice, ref in enumerate(bank_refs):

                @pl.when(bank == choice)
                def _():
                    source_ref[j * node_dev : (j + 1) * node_dev, :] = ref[block]

        product = jnp.dot(adj_ref[slot], source_ref[...], preferred_element_type=jnp.float32)
        rows = pl.ds(pl.multiple_of(row_tile * tile, tile), tile)
        acc_ref[rows, :] += product
        return carry

    lax.fori_loop(0, count_ref[0], add_tile, 0)
    part_ref[...] = acc_ref[...].reshape(part_ref.shape).astype(part_ref.dtype)


def body(
    adj_tiles, tile_pos, tile_count, node_feats, stale_part, w_self, w_neigh, bias_vec, cotangent
):
    node_dev, width = node_feats.shape
    hid = cotangent.shape[1]
    groups = lax.axis_size(GRP)
    blocks = lax.axis_size(BLK)
    plane = lax.axis_size(PLANE)

    stale = lax.all_to_all(stale_part[0], GRP, 0, 0, tiled=True)
    same = lax.all_gather(node_feats, EVERY_OTHER)
    length = lax.axis_size(LINE)
    up = [(i, (i + 1) % length) for i in range(length)]
    down = [(i, (i - 1) % length) for i in range(length)]
    half = same.shape[0] // 2
    low, high = same[:half], same[half:]
    swap = [(0, 1), (1, 0)]
    side_low, side_high = lax.ppermute(low, "x_hi", swap), lax.ppermute(high, "x_hi", swap)
    banks = (
        low,
        high,
        lax.ppermute(low, LINE, up),
        lax.ppermute(high, LINE, down),
        side_low,
        side_high,
        lax.ppermute(side_low, LINE, up),
        lax.ppermute(side_high, LINE, down),
    )
    index = jnp.arange(blocks, dtype=jnp.int32)
    other_side = index // length != lax.axis_index("x_hi")
    other_parity = index % 2 != lax.axis_index("z_near")
    slot = index % length // 2
    place = slot + length // 2 * (other_parity.astype(jnp.int32) + 2 * other_side)
    own = lax.axis_index(GRP).reshape(1).astype(jnp.int32)

    smem = pl.BlockSpec(memory_space=pltpu.SMEM)
    vmem = pl.BlockSpec(memory_space=pltpu.VMEM)
    piece_rows = 2 * width // plane
    tile, slots = adj_tiles.shape[1], adj_tiles.shape[0]
    whole = pl.BlockSpec(memory_space=pl.ANY)
    bf16, f32 = jnp.bfloat16, jnp.float32
    limit = pltpu.CompilerParams(vmem_limit_bytes=32 * 1024 * 1024)
    hidden, grads, positions = pl.pallas_call(
        layer_kernel,
        out_shape=(
            jax.ShapeDtypeStruct((node_dev, hid), bf16),
            jax.ShapeDtypeStruct((plane, piece_rows, hid + hid // 2), bf16),
            jax.ShapeDtypeStruct(tile_pos.shape, jnp.int32),
        ),
        in_specs=[smem] * 4 + [whole, [whole] * len(banks)] + [whole] * 4 + [vmem, whole],
        out_specs=(vmem, vmem, smem),
        scratch_shapes=[
            pltpu.VMEM((slots, node_dev, tile), bf16),
            pltpu.VMEM((slots, tile, width), bf16),
            pltpu.VMEM((groups, node_dev, width), bf16),
            pltpu.VMEM((node_dev, width), bf16),
            pltpu.VMEM((width, hid), bf16),
            pltpu.VMEM((width, hid), bf16),
            pltpu.VMEM((node_dev, hid), bf16),
            pltpu.SemaphoreType.DMA((slots,)),
            pltpu.SemaphoreType.DMA((slots, tile // node_dev)),
            pltpu.SemaphoreType.DMA((5,)),
        ],
        compiler_params=limit,
        cost_estimate=pl.CostEstimate(
            flops=10 * node_dev * width * hid, bytes_accessed=2**20, transcendentals=0
        ),
    )(
        tile_count,
        tile_pos,
        place,
        own,
        adj_tiles,
        list(banks),
        stale,
        node_feats,
        w_self,
        w_neigh,
        bias_vec[None],
        cotangent,
    )
    new_part = pl.pallas_call(
        partial_kernel,
        out_shape=jax.ShapeDtypeStruct((groups, node_dev, width), bf16),
        in_specs=[smem] * 3 + [vmem, [vmem] * len(banks)],
        out_specs=vmem,
        scratch_shapes=[
            pltpu.VMEM((groups * node_dev, width), f32),
            pltpu.VMEM((tile, width), bf16),
        ],
        compiler_params=limit,
        cost_estimate=pl.CostEstimate(
            flops=2 * slots * tile * tile * width, bytes_accessed=8 * 2**20, transcendentals=0
        ),
    )(tile_count, positions, place, adj_tiles, list(banks))

    scaling = float(node_dev * groups * blocks) ** (-0.5)
    piece = lax.all_to_all(grads, PLANE, 0, 0, tiled=True).astype(f32)
    piece = spread(jnp.sum(piece, axis=0).astype(bf16), "z_far").astype(f32)
    piece = jnp.sum(spread(jnp.sum(piece, axis=0), ("z_mid", "z_near")), axis=0) * scaling
    grad_bias = piece[:2, hid:].reshape(hid)
    both = spread(piece[:, :hid].astype(bf16), PLANE).astype(f32).reshape(2 * width, hid)
    return new_part[None], hidden, both[:width], both[width:], grad_bias


def solution(mesh):
    fine = Mesh(mesh.devices.reshape(SIZES), ALL)
    placed = (
        P(ALL, None, None),
        P(ALL),
        P(ALL),
        P(ALL, None),
        P(GRP, None, BLK, None),
        P(),
        P(),
        P(),
        P(ALL, None),
    )
    return jax.shard_map(
        body,
        mesh=fine,
        in_specs=placed,
        out_specs=(P(GRP, None, BLK, None), P(ALL, None), P(), P(), P()),
        check_vma=False,
    )
```

time: 221 us -> 167 us (0.76)
  blocking collectives: 165 us -> 96.6 us
  starting transfers between devices: 13.4 us -> 44.6 us
  waiting for transfers between devices: 31.2 us -> 12.2 us
  Pallas kernels: 2.95 us -> 6.69 us
    all_to_all x4 -> x1, blocking collectives: 120 us -> 34.5 us  [spread(): lax.all_to_all(jnp.broadcast_to(value[None], (copies,) + value.shape), ax...]
    all_gather x0 -> x1, blocking collectives: none -> 45.3 us  [body(): same = lax.all_gather(node_feats, EVERY_OTHER)]
    all_to_all x2 -> x1, blocking collectives: 44.8 us -> 16.8 us  [body(): piece = lax.all_to_all(grads, PLANE, 0, 0, tiled=True).astype(f32)]
    all_to_all x2, waiting for transfers between devices: 31.2 us -> 7.9 us  [spread(): lax.all_to_all(jnp.broadcast_to(value[None], (copies,) + value.shape), ax...]
    ppermute x0 -> x6, starting transfers between devices: none -> 19.8 us  [the longest x1 4.61 us: body(): lax.ppermute(low, 'x_hi', swap)]
    all_to_all x0 -> x1, starting transfers between devices: none -> 13.1 us  [body(): stale = lax.all_to_all(stale_part[0], GRP, 0, 0, tiled=True)]
    ppermute x0 -> x6, waiting for transfers between devices: none -> 4.29 us  [the longest x1 3.2 us: body(): lax.ppermute(side_low, LINE, up)]
    pallas_call x1 -> x2, Pallas kernels: 2.95 us -> 6.69 us  [the longest x1 3.55 us: body(): pl.pallas_call(partial_kernel, out_shape=jax.ShapeDtypeStruct((groups, no...]
  transfers between devices with their start and end apart: 2 -> 9, of which waited for: 2 -> 4; matrix products, arithmetic and copies ran while one was open for 0% -> 0% of each run, Pallas kernels for 0% -> 2%
where the time goes in v3:
time: 167 us; the launch traced here: 166 us
  blocking collectives  96.6 us (58%)
  starting transfers between devices  44.6 us (27%)
  waiting for transfers between devices  12.2 us (7%)
  Pallas kernels  6.69 us (4%)
  local copies, waits for them, and re-layouts  4.31 us (3%)
    all_gather x1, blocking collectives, body(): same = lax.all_gather(node_feats, EVERY_OTHER)  45.3 us
    all_to_all x1, blocking collectives, spread(): lax.all_to_all(jnp.broadcast_to(value[None], (copies,) + value.shape), ax...  34.5 us
    all_to_all x1, blocking collectives, body(): piece = lax.all_to_all(grads, PLANE, 0, 0, tiled=True).astype(f32)  16.8 us
    all_to_all x1, starting transfers between devices, body(): stale = lax.all_to_all(stale_part[0], GRP, 0, 0, tiled=True)  13.1 us
    all_to_all x2, starting transfers between devices, spread(): lax.all_to_all(jnp.broadcast_to(value[None], (copies,) + value.shape), ax...  11.7 us
    all_to_all x2, waiting for transfers between devices, spread(): lax.all_to_all(jnp.broadcast_to(value[None], (copies,) + value.shape), ax...  7.9 us
    ppermute x1, starting transfers between devices, body(): lax.ppermute(low, 'x_hi', swap)  4.61 us
    ppermute x1, starting transfers between devices, body(): lax.ppermute(side_high, LINE, down)  4.57 us
  transfers between devices with their start and end apart: 9, of which 4 were waited for; matrix products, arithmetic and copies ran while one was open for 0% of the time, Pallas kernels for 2%

profile of v3, /device:TPU:1, one launch (start us, length us, event | category | flops | bytes accessed | tf_op | source)
XLA Modules:
  0.0 166.0 jit_solution(4996889500137783077)
XLA Ops:
  0.7 45.3 %all-gather = bf16[2048,128]{1,0:T(8,128)(2,1)S(1)} all-gather(bf16[128,128]{1,0:T(8,128)(2,1)} %feats_ref.1), channel_id=2, replica_groups=mesh['y'=4,'x_lo'=2,'core'=2,'x_hi'=2,'z_far'=8,'z_mid'=2,'z_near'=2] {'..., dimensions={0}, use_global_device_ids=true | all-gather | bytes 557056 | tf_op jit(solution)/shard_map/all_gather | solution.py:204
  46.1 4.6 %collective-permute-start.2 = (bf16[8,128,128]{2,1,0:T(8,128)(2,1)S(1)}, bf16[8,128,128]{2,1,0:T(8,128)(2,1)S(1)}, u32[]{:S(2)}, u32[]{:S(2)}) collective-permute-start(bf16[8,128,128]{2,1,0:T(8,128)(2,1)S(1)} %bitcast.16), channel_id=1, source_target_pairs={{0,32},{32,0},{1,33},{33,1},{2,34},{34,2},{3,35},{35,3},{4,36},{36... | collective-permute-start | bytes 786440 | tf_op jit(solution)/shard_map/ppermute | solution.py:211
  50.7 2.2 %collective-permute-start.3 = (bf16[8,128,128]{2,1,0:T(8,128)(2,1)S(1)}, bf16[8,128,128]{2,1,0:T(8,128)(2,1)}, u32[]{:S(2)}, u32[]{:S(2)}) collective-permute-start(bf16[8,128,128]{2,1,0:T(8,128)(2,1)S(1)} %bitcast.12), channel_id=1, source_target_pairs={{0,32},{32,0},{1,33},{33,1},{2,34},{34,2},{3,35},{35,3},{4,36},{36... | collective-permute-start | bytes 786440 | tf_op jit(solution)/shard_map/ppermute | solution.py:211
  52.9 13.1 %all-to-all-start = ((bf16[16,128,128]{2,1,0:T(8,128)(2,1)}), bf16[16,128,128]{2,1,0:T(8,128)(2,1)S(1)}, u32[]{:S(2)}, u32[]{:S(2)}) async-start(bf16[16,128,128]{2,1,0:T(8,128)(2,1)} %bitcast.21), calls=%async_computation | async-start | bytes 1048576 | tf_op jit(solution)/shard_map/all_to_all | solution.py:203
  66.0 2.6 %collective-permute-start = (bf16[8,128,128]{2,1,0:T(8,128)(2,1)S(1)}, bf16[8,128,128]{2,1,0:T(8,128)(2,1)}, u32[]{:S(2)}, u32[]{:S(2)}) collective-permute-start(bf16[8,128,128]{2,1,0:T(8,128)(2,1)S(1)} %bitcast.17), channel_id=1, source_target_pairs={{0,1},{1,2},{2,3},{3,4},{4,5},{5,6},{6,7},{7,8},{8,9},{9,10},{10,1... | collective-permute-start | bytes 786440 | tf_op jit(solution)/shard_map/ppermute | solution.py:215
  68.6 3.9 %collective-permute-start.1 = (bf16[8,128,128]{2,1,0:T(8,128)(2,1)S(1)}, bf16[8,128,128]{2,1,0:T(8,128)(2,1)}, u32[]{:S(2)}, u32[]{:S(2)}) collective-permute-start(bf16[8,128,128]{2,1,0:T(8,128)(2,1)S(1)} %bitcast.13), channel_id=1, source_target_pairs={{0,31},{1,0},{2,1},{3,2},{4,3},{5,4},{6,5},{7,6},{8,7},{9,8},{10,9... | collective-permute-start | bytes 786440 | tf_op jit(solution)/shard_map/ppermute | solution.py:216
  72.5 1.9 %collective-permute-start.4 = (bf16[8,128,128]{2,1,0:T(8,128)(2,1)S(1)}, bf16[8,128,128]{2,1,0:T(8,128)(2,1)}, u32[]{:S(2)}, u32[]{:S(2)}) collective-permute-start(bf16[8,128,128]{2,1,0:T(8,128)(2,1)S(1)} %collective-permute-done.2.bank_refs_4_), channel_id=1, source_target_pairs={{0,1},{1,2},{2,3},{3,4},{4,5},{5,6},{6,7},{7,8},{8,9},{9,10},{10,1... | collective-permute-start | bytes 786440 | tf_op jit(solution)/shard_map/ppermute | solution.py:219
  74.5 4.6 %collective-permute-start.5 = (bf16[8,128,128]{2,1,0:T(8,128)(2,1)}, bf16[8,128,128]{2,1,0:T(8,128)(2,1)}, u32[]{:S(2)}, u32[]{:S(2)}) collective-permute-start(bf16[8,128,128]{2,1,0:T(8,128)(2,1)} %collective-permute-done.3.bank_refs_5_), channel_id=1, source_target_pairs={{0,31},{1,0},{2,1},{3,2},{4,3},{5,4},{6,5},{7,6},{8,7},{9,8},{10,9... | collective-permute-start | bytes 786440 | tf_op jit(solution)/shard_map/ppermute | solution.py:220
  79.7 3.2 %collective-permute-done.4.bank_refs_6_ = bf16[8,128,128]{2,1,0:T(8,128)(2,1)} collective-permute-done((bf16[8,128,128]{2,1,0:T(8,128)(2,1)S(1)}, bf16[8,128,128]{2,1,0:T(8,128)(2,1)}, u32[]{:S(2)}, u32[]{:S(2)}) %collective-permute-start.4) | collective-permute-done | bytes 262176 | tf_op jit(solution)/shard_map/ppermute | solution.py:219
  82.9 1.1 collective-permute-done.5.bank_refs_7_
  84.1 0.8 copy-done.3
  84.9 0.8 copy-done.4
  85.7 3.1 %shard_map.128 = (bf16[128,256]{1,0:T(8,128)(2,1)}, bf16[32,8,384]{2,1,0:T(8,128)(2,1)S(1)}, s32[16]{0:T(128)S(1)}) custom-call(s32[1]{0:T(128)S(6)} %copy.14.count_ref, s32[16]{0:T(128)S(1)} %copy-done.6, s32[64]{0:T(128)S(1)} %multiply_add_fusion.place_ref, s32[1]{0:T(128)} %bitcast.own_ref, bf16[16,256,256]{2,1,0:T(8,128)(2,1)S(1)} %copy-done, ...), custom_call_target="tpu_custom_call" | custom-call | flops 41943040 | bytes 1048576 | tf_op jit(solution)/shard_map/pallas_call | solution.py:236
  88.9 16.8 %all_to_all.25 = bf16[32,8,384]{2,1,0:T(8,128)(2,1)S(1)} all-to-all(bf16[32,8,384]{2,1,0:T(8,128)(2,1)S(1)} %get-tuple-element.10), channel_id=1, replica_groups=mesh['y'=4,'x_lo'=2,'core'=2,'x_hi'=2,'z_far'=8,'z_mid'=2,'z_near'=2] {'..., dimensions={0} | all-to-all | bytes 393216 | tf_op jit(solution)/shard_map/all_to_all | solution.py:291
  105.7 34.5 %all_to_all.26 = bf16[8,8,384]{2,1,0:T(8,128)(2,1)S(1)} all-to-all(bf16[8,8,384]{2,1,0:T(8,128)(2,1)S(1)} %broadcast_in_dim.12), channel_id=1, replica_groups=mesh['y'=4,'x_lo'=2,'core'=2,'x_hi'=2,'z_far'=8,'z_mid'=2,'z_near'=2] {'..., dimensions={0} | all-to-all | bytes 98304 | tf_op jit(solution)/shard_map/all_to_all | solution.py:19
  140.2 0.6 broadcast_in_dim.13
  140.8 4.5 %all-to-all-start.3 = ((f32[4,8,384]{2,1,0:T(8,128)}), f32[4,8,384]{2,1,0:T(8,128)S(1)}, u32[]{:S(2)}, u32[]{:S(2)}) async-start(f32[4,8,384]{2,1,0:T(8,128)} %broadcast_in_dim.13), calls=%async_computation.3 | async-start | bytes 98304 | tf_op jit(solution)/shard_map/all_to_all | solution.py:19
  145.3 3.6 %shard_map.129 = bf16[16,128,128]{2,1,0:T(8,128)(2,1)} custom-call(s32[1]{0:T(128)S(6)} %copy.14.count_ref, s32[16]{0:T(128)S(1)} %get-tuple-element.8.pos_ref, s32[64]{0:T(128)S(1)} %multiply_add_fusion.place_ref, bf16[16,256,256]{2,1,0:T(8,128)(2,1)S(1)} %copy-done, bf16[8,128,128]{2,1,0:T(8,128)(2,1)S(1)} %bitcast.19, bf16[8,128,128]{2,1,0:T(8,128)(2,1)S(1)} %bitcast.15, ...), custom_call_target="tpu_custom_call" | custom-call | flops 268435456 | bytes 8388608 | tf_op jit(solution)/shard_map/pallas_call | solution.py:275
  148.9 1.0 all-to-all-done.3
  149.9 0.7 broadcast_in_dim.28
  150.6 7.2 %all-to-all-start.4 = ((bf16[32,8,256]{2,1,0:T(8,128)(2,1)}), bf16[32,8,256]{2,1,0:T(8,128)(2,1)S(1)}, u32[]{:S(2)}, u32[]{:S(2)}) async-start(bf16[32,8,256]{2,1,0:T(8,128)(2,1)} %broadcast_in_dim.28), calls=%async_computation.4 | async-start | bytes 262144 | tf_op jit(solution)/shard_map/all_to_all | solution.py:19
  157.8 0.6 slice_bitcast_fusion.2
  158.4 6.9 %all-to-all-done.4 = bf16[32,8,256]{2,1,0:T(8,128)(2,1)S(1)} async-done(((bf16[32,8,256]{2,1,0:T(8,128)(2,1)}), bf16[32,8,256]{2,1,0:T(8,128)(2,1)S(1)}, u32[]{:S(2)}, u32[]{:S(2)}) %all-to-all-start.4) | async-done | bytes 131104 | tf_op jit(solution)/shard_map/all_to_all | solution.py:19
  165.3 0.7 slice_bitcast_fusion
  (26 shorter events, 0.2 us)
Async XLA Ops:
  0.6 83.4 %copy-start.1 = (bf16[128,128]{1,0:T(8,128)(2,1)S(1)}, bf16[128,128]{1,0:T(8,128)(2,1)}, u32[]{:S(2)}) copy-start(bf16[128,128]{1,0:T(8,128)(2,1)} %feats_ref.1) | copy-start | bytes 98308
  0.6 83.4 %copy-start = (bf16[16,256,256]{2,1,0:T(8,128)(2,1)S(1)}, bf16[16,256,256]{2,1,0:T(8,128)(2,1)}, u32[]{:S(2)}) copy-start(bf16[16,256,256]{2,1,0:T(8,128)(2,1)} %adj_ref.3) | copy-start | bytes 6291460
  0.7 83.4 %copy-start.5 = (f32[256]{0:T(256)S(1)}, f32[256]{0:T(256)}, u32[]{:S(2)}) copy-start(f32[256]{0:T(256)} %param.16) | copy-start | bytes 3076
  0.7 83.4 %copy-start.2 = (bf16[128,256]{1,0:T(8,128)(2,1)S(1)}, bf16[128,256]{1,0:T(8,128)(2,1)}, u32[]{:S(2)}) copy-start(bf16[128,256]{1,0:T(8,128)(2,1)} %w_self_ref.1) | copy-start | bytes 196612
  0.7 83.4 %copy-start.6 = (s32[16]{0:T(128)S(1)}, s32[16]{0:T(128)}, u32[]{:S(2)}) copy-start(s32[16]{0:T(128)} %pos_ref.1) | copy-start | bytes 196
  46.1 26.4 %collective-permute-start.2 = (bf16[8,128,128]{2,1,0:T(8,128)(2,1)S(1)}, bf16[8,128,128]{2,1,0:T(8,128)(2,1)S(1)}, u32[]{:S(2)}, u32[]{:S(2)}) collective-permute-start(bf16[8,128,128]{2,1,0:T(8,128)(2,1)S(1)} %bitcast.16), channel_id=1, source_target_pairs={{0,32},{32,0},{1,33},{33,1},{2,34},{34,2},{3,35},{35,3},{4,36},{36... | collective-permute-start | bytes 786440 | tf_op jit(solution)/shard_map/ppermute | solution.py:211
  50.7 23.8 %collective-permute-start.3 = (bf16[8,128,128]{2,1,0:T(8,128)(2,1)S(1)}, bf16[8,128,128]{2,1,0:T(8,128)(2,1)}, u32[]{:S(2)}, u32[]{:S(2)}) collective-permute-start(bf16[8,128,128]{2,1,0:T(8,128)(2,1)S(1)} %bitcast.12), channel_id=1, source_target_pairs={{0,32},{32,0},{1,33},{33,1},{2,34},{34,2},{3,35},{35,3},{4,36},{36... | collective-permute-start | bytes 786440 | tf_op jit(solution)/shard_map/ppermute | solution.py:211
  52.9 26.9 %all-to-all-start = ((bf16[16,128,128]{2,1,0:T(8,128)(2,1)}), bf16[16,128,128]{2,1,0:T(8,128)(2,1)S(1)}, u32[]{:S(2)}, u32[]{:S(2)}) async-start(bf16[16,128,128]{2,1,0:T(8,128)(2,1)} %bitcast.21), calls=%async_computation | async-start | bytes 1048576 | tf_op jit(solution)/shard_map/all_to_all | solution.py:203
  66.0 13.7 %collective-permute-start = (bf16[8,128,128]{2,1,0:T(8,128)(2,1)S(1)}, bf16[8,128,128]{2,1,0:T(8,128)(2,1)}, u32[]{:S(2)}, u32[]{:S(2)}) collective-permute-start(bf16[8,128,128]{2,1,0:T(8,128)(2,1)S(1)} %bitcast.17), channel_id=1, source_target_pairs={{0,1},{1,2},{2,3},{3,4},{4,5},{5,6},{6,7},{7,8},{8,9},{9,10},{10,1... | collective-permute-start | bytes 786440 | tf_op jit(solution)/shard_map/ppermute | solution.py:215
  68.6 11.1 %collective-permute-start.1 = (bf16[8,128,128]{2,1,0:T(8,128)(2,1)S(1)}, bf16[8,128,128]{2,1,0:T(8,128)(2,1)}, u32[]{:S(2)}, u32[]{:S(2)}) collective-permute-start(bf16[8,128,128]{2,1,0:T(8,128)(2,1)S(1)} %bitcast.13), channel_id=1, source_target_pairs={{0,31},{1,0},{2,1},{3,2},{4,3},{5,4},{6,5},{7,6},{8,7},{9,8},{10,9... | collective-permute-start | bytes 786440 | tf_op jit(solution)/shard_map/ppermute | solution.py:216
  72.5 10.4 %collective-permute-start.4 = (bf16[8,128,128]{2,1,0:T(8,128)(2,1)S(1)}, bf16[8,128,128]{2,1,0:T(8,128)(2,1)}, u32[]{:S(2)}, u32[]{:S(2)}) collective-permute-start(bf16[8,128,128]{2,1,0:T(8,128)(2,1)S(1)} %collective-permute-done.2.bank_refs_4_), channel_id=1, source_target_pairs={{0,1},{1,2},{2,3},{3,4},{4,5},{5,6},{6,7},{7,8},{8,9},{9,10},{10,1... | collective-permute-start | bytes 786440 | tf_op jit(solution)/shard_map/ppermute | solution.py:219
  74.5 9.6 %collective-permute-start.5 = (bf16[8,128,128]{2,1,0:T(8,128)(2,1)}, bf16[8,128,128]{2,1,0:T(8,128)(2,1)}, u32[]{:S(2)}, u32[]{:S(2)}) collective-permute-start(bf16[8,128,128]{2,1,0:T(8,128)(2,1)} %collective-permute-done.3.bank_refs_5_), channel_id=1, source_target_pairs={{0,31},{1,0},{2,1},{3,2},{4,3},{5,4},{6,5},{7,6},{8,7},{9,8},{10,9... | collective-permute-start | bytes 786440 | tf_op jit(solution)/shard_map/ppermute | solution.py:220
  84.1 0.8 copy-start.3
  84.9 0.8 copy-start.4
  140.8 9.0 %all-to-all-start.3 = ((f32[4,8,384]{2,1,0:T(8,128)}), f32[4,8,384]{2,1,0:T(8,128)S(1)}, u32[]{:S(2)}, u32[]{:S(2)}) async-start(f32[4,8,384]{2,1,0:T(8,128)} %broadcast_in_dim.13), calls=%async_computation.3 | async-start | bytes 98304 | tf_op jit(solution)/shard_map/all_to_all | solution.py:19
  150.6 14.7 %all-to-all-start.4 = ((bf16[32,8,256]{2,1,0:T(8,128)(2,1)}), bf16[32,8,256]{2,1,0:T(8,128)(2,1)S(1)}, u32[]{:S(2)}, u32[]{:S(2)}) async-start(bf16[32,8,256]{2,1,0:T(8,128)(2,1)} %broadcast_in_dim.28), calls=%async_computation.4 | async-start | bytes 262144 | tf_op jit(solution)/shard_map/all_to_all | solution.py:19

commit v4 on v3

--- a/solution.py
+++ b/solution.py
@@ -23,6 +23,23 @@
 
 def split_position(position, col_tiles, per_tile):
     return lax.div(position, col_tiles), lax.rem(position, col_tiles) * per_tile
+
+
+def early_kernel(
+    own_ref, stale_ref, feats_ref, w_self_ref, w_neigh_ref, cot_ref,
+    sum_ref, base_ref, w_neigh_out, cot_out,
+):
+    groups = stale_ref.shape[0]
+    own = own_ref[0]
+    stale = jnp.zeros(sum_ref.shape, jnp.float32)
+    for source in range(groups):
+        keep = jnp.where(source == own, jnp.float32(0.0), jnp.float32(1.0))
+        stale += stale_ref[source].astype(jnp.float32) * keep
+    sum_ref[...] = stale
+    preact = jnp.dot(feats_ref[...], w_self_ref[...], preferred_element_type=jnp.float32)
+    base_ref[...] = preact
+    w_neigh_out[...] = w_neigh_ref[...]
+    cot_out[...] = cot_ref[...]
 
 
 def layer_kernel(
@@ -33,8 +50,8 @@
     adj_ref,
     bank_refs,
     stale_ref,
+    base_ref,
     feats_ref,
-    w_self_ref,
     w_neigh_ref,
     bias_ref,
     cot_ref,
@@ -43,36 +60,17 @@
     pos_out_ref,
     tiles_ref,
     sources_ref,
-    stale_vmem,
-    feats_vmem,
-    w_self_vmem,
-    w_neigh_vmem,
-    cot_vmem,
     tile_sem,
     source_sem,
-    dense_sem,
 ):
     tile = adj_ref.shape[1]
-    groups, node_dev, width = stale_ref.shape
+    node_dev, width = stale_ref.shape
     per_tile = tile // node_dev
     bank_slots = bank_refs[0].shape[0]
     col_tiles = place_ref.shape[0] // per_tile
     own = own_ref[0]
     own_tile, own_part = lax.div(own, per_tile), lax.rem(own, per_tile)
     count = count_ref[0]
-
-    dense = [
-        pltpu.make_async_copy(src, dst, dense_sem.at[i])
-        for i, (src, dst) in enumerate(
-            (
-                (stale_ref, stale_vmem),
-                (feats_ref, feats_vmem),
-                (w_self_ref, w_self_vmem),
-                (w_neigh_ref, w_neigh_vmem),
-                (cot_ref, cot_vmem),
-            )
-        )
-    ]
 
     def tile_copy(slot):
         rows = pl.ds(pl.multiple_of(own_part * node_dev, node_dev), node_dev)
@@ -106,8 +104,6 @@
         return carry
 
     lax.fori_loop(0, pos_ref.shape[0], fetch, 0)
-    for copy in dense:
-        copy.start()
 
     def add_tile(slot, fresh):
         row_tile, _ = split_position(pos_ref[slot], col_tiles, per_tile)
@@ -123,21 +119,15 @@
         return lax.cond(row_tile == own_tile, add, lambda: fresh)
 
     fresh = lax.fori_loop(0, count, add_tile, jnp.zeros((node_dev, width), jnp.float32))
-    for copy in dense:
-        copy.wait()
-    stale = jnp.zeros((node_dev, width), jnp.float32)
-    for source in range(groups):
-        keep = jnp.where(source == own, jnp.float32(0.0), jnp.float32(1.0))
-        stale += stale_vmem[source].astype(jnp.float32) * keep
-    aggregate = (fresh + stale).astype(jnp.bfloat16)
-    feats = feats_vmem[...]
-    preact = jnp.dot(feats, w_self_vmem[...], preferred_element_type=jnp.float32)
-    preact += jnp.dot(aggregate, w_neigh_vmem[...], preferred_element_type=jnp.float32)
+    aggregate = (fresh + stale_ref[...]).astype(jnp.bfloat16)
+    feats = feats_ref[...]
+    preact = base_ref[...]
+    preact += jnp.dot(aggregate, w_neigh_ref[...], preferred_element_type=jnp.float32)
     preact += bias_ref[...]
     gate = jax.nn.sigmoid(preact)
     hidden_ref[...] = (preact * gate).astype(hidden_ref.dtype)
     grad_pre = (
-        cot_vmem[...].astype(jnp.float32) * gate * (1.0 + preact * (1.0 - gate))
+        cot_ref[...].astype(jnp.float32) * gate * (1.0 + preact * (1.0 - gate))
     ).astype(jnp.bfloat16)
     both = jnp.concatenate([feats, aggregate], axis=1)
     grads = lax.dot_general(
@@ -233,6 +223,21 @@
     whole = pl.BlockSpec(memory_space=pl.ANY)
     bf16, f32 = jnp.bfloat16, jnp.float32
     limit = pltpu.CompilerParams(vmem_limit_bytes=32 * 1024 * 1024)
+    stale_sum, base, w_neigh, cotangent = pl.pallas_call(
+        early_kernel,
+        out_shape=(
+            jax.ShapeDtypeStruct((node_dev, width), f32),
+            jax.ShapeDtypeStruct((node_dev, hid), f32),
+            jax.ShapeDtypeStruct(w_neigh.shape, bf16),
+            jax.ShapeDtypeStruct(cotangent.shape, bf16),
+        ),
+        in_specs=[smem] + [vmem] * 5,
+        out_specs=(vmem,) * 4,
+        compiler_params=limit,
+        cost_estimate=pl.CostEstimate(
+            flops=2 * node_dev * width * hid, bytes_accessed=2**20, transcendentals=0
+        ),
+    )(own, stale, node_feats, w_self, w_neigh, cotangent)
     hidden, grads, positions = pl.pallas_call(
         layer_kernel,
         out_shape=(
@@ -240,23 +245,17 @@
             jax.ShapeDtypeStruct((plane, piece_rows, hid + hid // 2), bf16),
             jax.ShapeDtypeStruct(tile_pos.shape, jnp.int32),
         ),
-        in_specs=[smem] * 4 + [whole, [whole] * len(banks)] + [whole] * 4 + [vmem, whole],
+        in_specs=[smem] * 4 + [whole, [whole] * len(banks)] + [vmem] * 6,
         out_specs=(vmem, vmem, smem),
         scratch_shapes=[
             pltpu.VMEM((slots, node_dev, tile), bf16),
             pltpu.VMEM((slots, tile, width), bf16),
-            pltpu.VMEM((groups, node_dev, width), bf16),
-            pltpu.VMEM((node_dev, width), bf16),
-            pltpu.VMEM((width, hid), bf16),
-            pltpu.VMEM((width, hid), bf16),
-            pltpu.VMEM((node_dev, hid), bf16),
             pltpu.SemaphoreType.DMA((slots,)),
             pltpu.SemaphoreType.DMA((slots, tile // node_dev)),
-            pltpu.SemaphoreType.DMA((5,)),
         ],
         compiler_params=limit,
         cost_estimate=pl.CostEstimate(
-            flops=10 * node_dev * width * hid, bytes_accessed=2**20, transcendentals=0
+            flops=8 * node_dev * width * hid, bytes_accessed=2**20, transcendentals=0
         ),
     )(
         tile_count,
@@ -265,9 +264,9 @@
         own,
         adj_tiles,
         list(banks),
-        stale,
+        stale_sum,
+        base,
         node_feats,
-        w_self,
         w_neigh,
         bias_vec[None],
         cotangent,
@@ -289,8 +288,9 @@
 
     scaling = float(node_dev * groups * blocks) ** (-0.5)
     piece = lax.all_to_all(grads, PLANE, 0, 0, tiled=True).astype(f32)
-    piece = spread(jnp.sum(piece, axis=0).astype(bf16), "z_far").astype(f32)
-    piece = jnp.sum(spread(jnp.sum(piece, axis=0), ("z_mid", "z_near")), axis=0) * scaling
+    piece = lax.all_gather(jnp.sum(piece, axis=0).astype(bf16), EVERY_OTHER).astype(f32)
+    piece = jnp.sum(piece, axis=0)
+    piece = (piece + lax.ppermute(piece, "z_near", swap)) * scaling
     grad_bias = piece[:2, hid:].reshape(hid)
     both = spread(piece[:, :hid].astype(bf16), PLANE).astype(f32).reshape(2 * width, hid)
     return new_part[None], hidden, both[:width], both[width:], grad_bias

time: 167 us -> 161 us (0.964)
  blocking collectives: 96.6 us -> 88.5 us
  starting transfers between devices: 44.6 us -> 52.5 us
  waiting for transfers between devices: 12.2 us -> 9.43 us
  Pallas kernels: 6.69 us -> 4.77 us
    all_to_all x1 -> x0, blocking collectives: 34.5 us -> none  [spread(): lax.all_to_all(jnp.broadcast_to(value[None], (copies,) + value.shape), ax...]
    all_gather x0 -> x1, blocking collectives: none -> 25.2 us  [body(): lax.all_gather(jnp.sum(piece, axis=0).astype(bf16), EVERY_OTHER).astype(f32)]
    ppermute x0 -> x1, starting transfers between devices: none -> 4.22 us  [body(): piece = (piece + lax.ppermute(piece, 'z_near', swap)) * scaling]
    all_to_all x2 -> x1, starting transfers between devices: 11.7 us -> 15.3 us  [spread(): lax.all_to_all(jnp.broadcast_to(value[None], (copies,) + value.shape), ax...]
    ppermute x1, waiting for transfers between devices: 3.2 us -> 1.33 us  [body(): lax.ppermute(side_low, LINE, up)]
    all_to_all x2 -> x1, waiting for transfers between devices: 7.9 us -> 7 us  [spread(): lax.all_to_all(jnp.broadcast_to(value[None], (copies,) + value.shape), ax...]
  transfers between devices with their start and end apart: 9 -> 9, of which waited for: 4 -> 3; matrix products, arithmetic and copies ran while one was open for 0% -> 0% of each run, Pallas kernels for 2% -> 2%
where the time goes in v4:
time: 161 us; the launch traced here: 160 us
  blocking collectives  88.5 us (55%)
  starting transfers between devices  52.5 us (33%)
  waiting for transfers between devices  9.43 us (6%)
  Pallas kernels  4.77 us (3%)
  local copies, waits for them, and re-layouts  3.68 us (2%)
    all_gather x1, blocking collectives, body(): same = lax.all_gather(node_feats, EVERY_OTHER)  45.3 us
    all_gather x1, blocking collectives, body(): lax.all_gather(jnp.sum(piece, axis=0).astype(bf16), EVERY_OTHER).astype(f32)  25.2 us
    all_to_all x1, blocking collectives, body(): piece = lax.all_to_all(grads, PLANE, 0, 0, tiled=True).astype(f32)  18 us
    all_to_all x1, starting transfers between devices, spread(): lax.all_to_all(jnp.broadcast_to(value[None], (copies,) + value.shape), ax...  15.3 us
    all_to_all x1, starting transfers between devices, body(): stale = lax.all_to_all(stale_part[0], GRP, 0, 0, tiled=True)  13.1 us
    all_to_all x1, waiting for transfers between devices, spread(): lax.all_to_all(jnp.broadcast_to(value[None], (copies,) + value.shape), ax...  7 us
    ppermute x1, starting transfers between devices, body(): lax.ppermute(low, 'x_hi', swap)  4.61 us
    ppermute x1, starting transfers between devices, body(): lax.ppermute(side_high, LINE, down)  4.57 us
  transfers between devices with their start and end apart: 9, of which 3 were waited for; matrix products, arithmetic and copies ran while one was open for 0% of the time, Pallas kernels for 2%

profile of v4, /device:TPU:1, one launch (start us, length us, event | category | flops | bytes accessed | tf_op | source)
XLA Modules:
  0.0 160.4 jit_solution(475093302881320812)
XLA Ops:
  0.7 45.3 %all-gather = bf16[2048,128]{1,0:T(8,128)(2,1)S(1)} all-gather(bf16[128,128]{1,0:T(8,128)(2,1)} %feats_ref.3), channel_id=2, replica_groups=mesh['y'=4,'x_lo'=2,'core'=2,'x_hi'=2,'z_far'=8,'z_mid'=2,'z_near'=2] {'..., dimensions={0}, use_global_device_ids=true | all-gather | bytes 557056 | tf_op jit(solution)/shard_map/all_gather | solution.py:194
  46.1 4.6 %collective-permute-start.2 = (bf16[8,128,128]{2,1,0:T(8,128)(2,1)S(1)}, bf16[8,128,128]{2,1,0:T(8,128)(2,1)S(1)}, u32[]{:S(2)}, u32[]{:S(2)}) collective-permute-start(bf16[8,128,128]{2,1,0:T(8,128)(2,1)S(1)} %bitcast.19), channel_id=1, source_target_pairs={{0,32},{32,0},{1,33},{33,1},{2,34},{34,2},{3,35},{35,3},{4,36},{36... | collective-permute-start | bytes 786440 | tf_op jit(solution)/shard_map/ppermute | solution.py:201
  50.7 2.2 %collective-permute-start.3 = (bf16[8,128,128]{2,1,0:T(8,128)(2,1)S(1)}, bf16[8,128,128]{2,1,0:T(8,128)(2,1)}, u32[]{:S(2)}, u32[]{:S(2)}) collective-permute-start(bf16[8,128,128]{2,1,0:T(8,128)(2,1)S(1)} %bitcast.15), channel_id=1, source_target_pairs={{0,32},{32,0},{1,33},{33,1},{2,34},{34,2},{3,35},{35,3},{4,36},{36... | collective-permute-start | bytes 786440 | tf_op jit(solution)/shard_map/ppermute | solution.py:201
  52.9 13.1 %all-to-all-start = ((bf16[16,128,128]{2,1,0:T(8,128)(2,1)}), bf16[16,128,128]{2,1,0:T(8,128)(2,1)S(1)}, u32[]{:S(2)}, u32[]{:S(2)}) async-start(bf16[16,128,128]{2,1,0:T(8,128)(2,1)} %bitcast.24), calls=%async_computation | async-start | bytes 1048576 | tf_op jit(solution)/shard_map/all_to_all | solution.py:193
  66.0 2.6 %collective-permute-start = (bf16[8,128,128]{2,1,0:T(8,128)(2,1)S(1)}, bf16[8,128,128]{2,1,0:T(8,128)(2,1)}, u32[]{:S(2)}, u32[]{:S(2)}) collective-permute-start(bf16[8,128,128]{2,1,0:T(8,128)(2,1)S(1)} %bitcast.20), channel_id=1, source_target_pairs={{0,1},{1,2},{2,3},{3,4},{4,5},{5,6},{6,7},{7,8},{8,9},{9,10},{10,1... | collective-permute-start | bytes 786440 | tf_op jit(solution)/shard_map/ppermute | solution.py:205
  68.6 3.9 %collective-permute-start.1 = (bf16[8,128,128]{2,1,0:T(8,128)(2,1)S(1)}, bf16[8,128,128]{2,1,0:T(8,128)(2,1)}, u32[]{:S(2)}, u32[]{:S(2)}) collective-permute-start(bf16[8,128,128]{2,1,0:T(8,128)(2,1)S(1)} %bitcast.16), channel_id=1, source_target_pairs={{0,31},{1,0},{2,1},{3,2},{4,3},{5,4},{6,5},{7,6},{8,7},{9,8},{10,9... | collective-permute-start | bytes 786440 | tf_op jit(solution)/shard_map/ppermute | solution.py:206
  72.5 1.9 %collective-permute-start.4 = (bf16[8,128,128]{2,1,0:T(8,128)(2,1)S(1)}, bf16[8,128,128]{2,1,0:T(8,128)(2,1)}, u32[]{:S(2)}, u32[]{:S(2)}) collective-permute-start(bf16[8,128,128]{2,1,0:T(8,128)(2,1)S(1)} %collective-permute-done.2.bank_refs_4_), channel_id=1, source_target_pairs={{0,1},{1,2},{2,3},{3,4},{4,5},{5,6},{6,7},{7,8},{8,9},{9,10},{10,1... | collective-permute-start | bytes 786440 | tf_op jit(solution)/shard_map/ppermute | solution.py:209
  74.5 4.6 %collective-permute-start.5 = (bf16[8,128,128]{2,1,0:T(8,128)(2,1)}, bf16[8,128,128]{2,1,0:T(8,128)(2,1)}, u32[]{:S(2)}, u32[]{:S(2)}) collective-permute-start(bf16[8,128,128]{2,1,0:T(8,128)(2,1)} %collective-permute-done.3.bank_refs_5_), channel_id=1, source_target_pairs={{0,31},{1,0},{2,1},{3,2},{4,3},{5,4},{6,5},{7,6},{8,7},{9,8},{10,9... | collective-permute-start | bytes 786440 | tf_op jit(solution)/shard_map/ppermute | solution.py:210
  79.7 0.0 copy-start.3
  79.8 0.8 copy-done.3
  80.6 0.8 copy-done.4
  81.4 0.2 shard_map.128
  81.6 1.3 collective-permute-done.4.bank_refs_6_
  82.9 1.1 collective-permute-done.5.bank_refs_7_
  84.0 2.1 %shard_map.129 = (bf16[128,256]{1,0:T(8,128)(2,1)}, bf16[32,8,384]{2,1,0:T(8,128)(2,1)S(1)}, s32[16]{0:T(128)S(1)}) custom-call(s32[1]{0:T(128)S(6)} %copy.14.count_ref, s32[16]{0:T(128)S(1)} %copy-done.6, s32[64]{0:T(128)S(1)} %multiply_add_fusion.place_ref, s32[1]{0:T(128)} %bitcast.own_ref, bf16[16,256,256]{2,1,0:T(8,128)(2,1)S(1)} %copy-done, ...), custom_call_target="tpu_custom_call" | custom-call | flops 33554432 | bytes 1048576 | tf_op jit(solution)/shard_map/pallas_call | solution.py:241
  86.2 18.0 %all_to_all.15 = bf16[32,8,384]{2,1,0:T(8,128)(2,1)S(1)} all-to-all(bf16[32,8,384]{2,1,0:T(8,128)(2,1)S(1)} %get-tuple-element.18), channel_id=1, replica_groups=mesh['y'=4,'x_lo'=2,'core'=2,'x_hi'=2,'z_far'=8,'z_mid'=2,'z_near'=2] {'..., dimensions={0} | all-to-all | bytes 393216 | tf_op jit(solution)/shard_map/all_to_all | solution.py:290
  104.2 25.2 %all-gather.1 = bf16[128,384]{1,0:T(8,128)(2,1)S(1)} all-gather(bf16[8,384]{1,0:T(8,128)(2,1)S(1)} %reduce_sum.21), channel_id=3, replica_groups=mesh['y'=4,'x_lo'=2,'core'=2,'x_hi'=2,'z_far'=8,'z_mid'=2,'z_near'=2] {'..., dimensions={0}, use_global_device_ids=true | all-gather | bytes 104448 | tf_op jit(solution)/shard_map/all_gather | solution.py:291
  129.4 4.2 %collective-permute-start.6 = (f32[8,384]{1,0:T(8,128)S(1)}, f32[8,384]{1,0:T(8,128)S(1)}, u32[]{:S(2)}, u32[]{:S(2)}) collective-permute-start(f32[8,384]{1,0:T(8,128)S(1)} %convert_reduce_fusion), channel_id=1, source_target_pairs={{0,1},{1,0},{2,3},{3,2},{4,5},{5,4},{6,7},{7,6},{8,9},{9,8},{10,11... | collective-permute-start | bytes 36872 | tf_op jit(solution)/shard_map/ppermute | solution.py:293
  133.6 2.5 %shard_map.130 = bf16[16,128,128]{2,1,0:T(8,128)(2,1)} custom-call(s32[1]{0:T(128)S(6)} %copy.14.count_ref, s32[16]{0:T(128)S(1)} %get-tuple-element.16.pos_ref, s32[64]{0:T(128)S(1)} %multiply_add_fusion.place_ref, bf16[16,256,256]{2,1,0:T(8,128)(2,1)S(1)} %copy-done, bf16[8,128,128]{2,1,0:T(8,128)(2,1)S(1)} %bitcast.22, bf16[8,128,128]{2,1,0:T(8,128)(2,1)S(1)} %bitcast.18, ...), custom_call_target="tpu_custom_call" | custom-call | flops 268435456 | bytes 8388608 | tf_op jit(solution)/shard_map/pallas_call | solution.py:274
  136.1 0.7 broadcast_in_dim.14
  136.8 15.3 %all-to-all-start.2 = ((bf16[32,8,256]{2,1,0:T(8,128)(2,1)}), bf16[32,8,256]{2,1,0:T(8,128)(2,1)S(1)}, u32[]{:S(2)}, u32[]{:S(2)}) async-start(bf16[32,8,256]{2,1,0:T(8,128)(2,1)} %broadcast_in_dim.14), calls=%async_computation.2 | async-start | bytes 262144 | tf_op jit(solution)/shard_map/all_to_all | solution.py:19
  152.1 0.6 slice_bitcast_fusion.2
  152.7 7.0 %all-to-all-done.2 = bf16[32,8,256]{2,1,0:T(8,128)(2,1)S(1)} async-done(((bf16[32,8,256]{2,1,0:T(8,128)(2,1)}), bf16[32,8,256]{2,1,0:T(8,128)(2,1)S(1)}, u32[]{:S(2)}, u32[]{:S(2)}) %all-to-all-start.2) | async-done | bytes 131104 | tf_op jit(solution)/shard_map/all_to_all | solution.py:19
  159.7 0.7 slice_bitcast_fusion
  (24 shorter events, 0.2 us)
Async XLA Ops:
  0.6 79.1 %copy-start.1 = (bf16[128,128]{1,0:T(8,128)(2,1)S(1)}, bf16[128,128]{1,0:T(8,128)(2,1)}, u32[]{:S(2)}) copy-start(bf16[128,128]{1,0:T(8,128)(2,1)} %feats_ref.3) | copy-start | bytes 98308
  0.6 79.1 %copy-start.2 = (bf16[128,256]{1,0:T(8,128)(2,1)S(1)}, bf16[128,256]{1,0:T(8,128)(2,1)}, u32[]{:S(2)}) copy-start(bf16[128,256]{1,0:T(8,128)(2,1)} %w_self_ref.1) | copy-start | bytes 196612
  0.7 83.4 %copy-start = (bf16[16,256,256]{2,1,0:T(8,128)(2,1)S(1)}, bf16[16,256,256]{2,1,0:T(8,128)(2,1)}, u32[]{:S(2)}) copy-start(bf16[16,256,256]{2,1,0:T(8,128)(2,1)} %adj_ref.3) | copy-start | bytes 6291460
  0.7 83.4 %copy-start.5 = (f32[256]{0:T(256)S(1)}, f32[256]{0:T(256)}, u32[]{:S(2)}) copy-start(f32[256]{0:T(256)} %param.16) | copy-start | bytes 3076
  0.7 83.4 %copy-start.6 = (s32[16]{0:T(128)S(1)}, s32[16]{0:T(128)}, u32[]{:S(2)}) copy-start(s32[16]{0:T(128)} %pos_ref.1) | copy-start | bytes 196
  46.1 26.4 %collective-permute-start.2 = (bf16[8,128,128]{2,1,0:T(8,128)(2,1)S(1)}, bf16[8,128,128]{2,1,0:T(8,128)(2,1)S(1)}, u32[]{:S(2)}, u32[]{:S(2)}) collective-permute-start(bf16[8,128,128]{2,1,0:T(8,128)(2,1)S(1)} %bitcast.19), channel_id=1, source_target_pairs={{0,32},{32,0},{1,33},{33,1},{2,34},{34,2},{3,35},{35,3},{4,36},{36... | collective-permute-start | bytes 786440 | tf_op jit(solution)/shard_map/ppermute | solution.py:201
  50.7 23.8 %collective-permute-start.3 = (bf16[8,128,128]{2,1,0:T(8,128)(2,1)S(1)}, bf16[8,128,128]{2,1,0:T(8,128)(2,1)}, u32[]{:S(2)}, u32[]{:S(2)}) collective-permute-start(bf16[8,128,128]{2,1,0:T(8,128)(2,1)S(1)} %bitcast.15), channel_id=1, source_target_pairs={{0,32},{32,0},{1,33},{33,1},{2,34},{34,2},{3,35},{35,3},{4,36},{36... | collective-permute-start | bytes 786440 | tf_op jit(solution)/shard_map/ppermute | solution.py:201
  52.9 26.9 %all-to-all-start = ((bf16[16,128,128]{2,1,0:T(8,128)(2,1)}), bf16[16,128,128]{2,1,0:T(8,128)(2,1)S(1)}, u32[]{:S(2)}, u32[]{:S(2)}) async-start(bf16[16,128,128]{2,1,0:T(8,128)(2,1)} %bitcast.24), calls=%async_computation | async-start | bytes 1048576 | tf_op jit(solution)/shard_map/all_to_all | solution.py:193
  66.0 15.6 %collective-permute-start = (bf16[8,128,128]{2,1,0:T(8,128)(2,1)S(1)}, bf16[8,128,128]{2,1,0:T(8,128)(2,1)}, u32[]{:S(2)}, u32[]{:S(2)}) collective-permute-start(bf16[8,128,128]{2,1,0:T(8,128)(2,1)S(1)} %bitcast.20), channel_id=1, source_target_pairs={{0,1},{1,2},{2,3},{3,4},{4,5},{5,6},{6,7},{7,8},{8,9},{9,10},{10,1... | collective-permute-start | bytes 786440 | tf_op jit(solution)/shard_map/ppermute | solution.py:205
  68.6 13.0 %collective-permute-start.1 = (bf16[8,128,128]{2,1,0:T(8,128)(2,1)S(1)}, bf16[8,128,128]{2,1,0:T(8,128)(2,1)}, u32[]{:S(2)}, u32[]{:S(2)}) collective-permute-start(bf16[8,128,128]{2,1,0:T(8,128)(2,1)S(1)} %bitcast.16), channel_id=1, source_target_pairs={{0,31},{1,0},{2,1},{3,2},{4,3},{5,4},{6,5},{7,6},{8,7},{9,8},{10,9... | collective-permute-start | bytes 786440 | tf_op jit(solution)/shard_map/ppermute | solution.py:206
  72.5 10.4 %collective-permute-start.4 = (bf16[8,128,128]{2,1,0:T(8,128)(2,1)S(1)}, bf16[8,128,128]{2,1,0:T(8,128)(2,1)}, u32[]{:S(2)}, u32[]{:S(2)}) collective-permute-start(bf16[8,128,128]{2,1,0:T(8,128)(2,1)S(1)} %collective-permute-done.2.bank_refs_4_), channel_id=1, source_target_pairs={{0,1},{1,2},{2,3},{3,4},{4,5},{5,6},{6,7},{7,8},{8,9},{9,10},{10,1... | collective-permute-start | bytes 786440 | tf_op jit(solution)/shard_map/ppermute | solution.py:209
  74.5 9.6 %collective-permute-start.5 = (bf16[8,128,128]{2,1,0:T(8,128)(2,1)}, bf16[8,128,128]{2,1,0:T(8,128)(2,1)}, u32[]{:S(2)}, u32[]{:S(2)}) collective-permute-start(bf16[8,128,128]{2,1,0:T(8,128)(2,1)} %collective-permute-done.3.bank_refs_5_), channel_id=1, source_target_pairs={{0,31},{1,0},{2,1},{3,2},{4,3},{5,4},{6,5},{7,6},{8,7},{9,8},{10,9... | collective-permute-start | bytes 786440 | tf_op jit(solution)/shard_map/ppermute | solution.py:210
  79.7 0.8 copy-start.3
  80.6 0.8 copy-start.4
  129.4 6.7 %collective-permute-start.6 = (f32[8,384]{1,0:T(8,128)S(1)}, f32[8,384]{1,0:T(8,128)S(1)}, u32[]{:S(2)}, u32[]{:S(2)}) collective-permute-start(f32[8,384]{1,0:T(8,128)S(1)} %convert_reduce_fusion), channel_id=1, source_target_pairs={{0,1},{1,0},{2,3},{3,2},{4,5},{5,4},{6,7},{7,6},{8,9},{9,8},{10,11... | collective-permute-start | bytes 36872 | tf_op jit(solution)/shard_map/ppermute | solution.py:293
  136.8 22.9 %all-to-all-start.2 = ((bf16[32,8,256]{2,1,0:T(8,128)(2,1)}), bf16[32,8,256]{2,1,0:T(8,128)(2,1)S(1)}, u32[]{:S(2)}, u32[]{:S(2)}) async-start(bf16[32,8,256]{2,1,0:T(8,128)(2,1)} %broadcast_in_dim.14), calls=%async_computation.2 | async-start | bytes 262144 | tf_op jit(solution)/shard_map/all_to_all | solution.py:19

commit v5 on v4

--- a/solution.py
+++ b/solution.py
@@ -57,7 +57,6 @@
     cot_ref,
     hidden_ref,
     grads_ref,
-    pos_out_ref,
     tiles_ref,
     sources_ref,
     tile_sem,
@@ -66,7 +65,7 @@
     tile = adj_ref.shape[1]
     node_dev, width = stale_ref.shape
     per_tile = tile // node_dev
-    bank_slots = bank_refs[0].shape[0]
+    bank_slots = 2 * bank_refs[0].shape[0]
     col_tiles = place_ref.shape[0] // per_tile
     own = own_ref[0]
     own_tile, own_part = lax.div(own, per_tile), lax.rem(own, per_tile)
@@ -86,10 +85,9 @@
         )
 
     def fetch(slot, carry):
-        pos_out_ref[slot] = pos_ref[slot]
         row_tile, first = split_position(pos_ref[slot], col_tiles, per_tile)
 
-        @pl.when((row_tile == own_tile) & (slot < count))
+        @pl.when(row_tile == own_tile)
         def _():
             tile_copy(slot).start()
             for j in range(per_tile):
@@ -103,7 +101,7 @@
 
         return carry
 
-    lax.fori_loop(0, pos_ref.shape[0], fetch, 0)
+    lax.fori_loop(0, count, fetch, 0)
 
     def add_tile(slot, fresh):
         row_tile, _ = split_position(pos_ref[slot], col_tiles, per_tile)
@@ -152,12 +150,12 @@
 
 
 def partial_kernel(
-    count_ref, pos_ref, place_ref, adj_ref, bank_refs, part_ref, acc_ref, source_ref
+    count_ref, pos_ref, place_ref, adj_ref, bank_refs, _, part_ref, acc_ref, source_ref
 ):
     tile = adj_ref.shape[1]
     _, node_dev, _ = part_ref.shape
     per_tile = tile // node_dev
-    bank_slots = bank_refs[0].shape[0]
+    bank_slots = 2 * bank_refs[0].shape[0]
     col_tiles = place_ref.shape[0] // per_tile
     acc_ref[...] = jnp.zeros_like(acc_ref)
 
@@ -199,21 +197,22 @@
     low, high = same[:half], same[half:]
     swap = [(0, 1), (1, 0)]
     side_low, side_high = lax.ppermute(low, "x_hi", swap), lax.ppermute(high, "x_hi", swap)
+    beside = lax.ppermute(same, LINE, up)
     banks = (
-        low,
-        high,
-        lax.ppermute(low, LINE, up),
-        lax.ppermute(high, LINE, down),
+        same,
+        beside,
         side_low,
         side_high,
-        lax.ppermute(side_low, LINE, up),
-        lax.ppermute(side_high, LINE, down),
+        lax.ppermute(side_low, LINE, down),
+        lax.ppermute(side_high, LINE, up),
     )
     index = jnp.arange(blocks, dtype=jnp.int32)
     other_side = index // length != lax.axis_index("x_hi")
     other_parity = index % 2 != lax.axis_index("z_near")
     slot = index % length // 2
-    place = slot + length // 2 * (other_parity.astype(jnp.int32) + 2 * other_side)
+    low_bank = jnp.where(other_side, 2 + 2 * other_parity, other_parity)
+    first = other_side & (slot >= half)
+    place = (low_bank + first) * length + jnp.where(first, slot - half, slot)
     own = lax.axis_index(GRP).reshape(1).astype(jnp.int32)
 
     smem = pl.BlockSpec(memory_space=pltpu.SMEM)
@@ -238,15 +237,14 @@
             flops=2 * node_dev * width * hid, bytes_accessed=2**20, transcendentals=0
         ),
     )(own, stale, node_feats, w_self, w_neigh, cotangent)
-    hidden, grads, positions = pl.pallas_call(
+    hidden, grads = pl.pallas_call(
         layer_kernel,
         out_shape=(
             jax.ShapeDtypeStruct((node_dev, hid), bf16),
             jax.ShapeDtypeStruct((plane, piece_rows, hid + hid // 2), bf16),
-            jax.ShapeDtypeStruct(tile_pos.shape, jnp.int32),
         ),
         in_specs=[smem] * 4 + [whole, [whole] * len(banks)] + [vmem] * 6,
-        out_specs=(vmem, vmem, smem),
+        out_specs=(vmem, vmem),
         scratch_shapes=[
             pltpu.VMEM((slots, node_dev, tile), bf16),
             pltpu.VMEM((slots, tile, width), bf16),
@@ -271,10 +269,15 @@
         bias_vec[None],
         cotangent,
     )
+    scaling = float(node_dev * groups * blocks) ** (-0.5)
+    piece = lax.all_to_all(grads, PLANE, 0, 0, tiled=True).astype(f32)
+    piece = lax.all_gather(jnp.sum(piece, axis=0).astype(bf16), EVERY_OTHER).astype(f32)
+    piece = jnp.sum(piece, axis=0)
+    piece = (piece + lax.ppermute(piece, "z_near", swap)) * scaling
     new_part = pl.pallas_call(
         partial_kernel,
         out_shape=jax.ShapeDtypeStruct((groups, node_dev, width), bf16),
-        in_specs=[smem] * 3 + [vmem, [vmem] * len(banks)],
+        in_specs=[smem] * 3 + [vmem, [vmem] * len(banks), whole],
         out_specs=vmem,
         scratch_shapes=[
             pltpu.VMEM((groups * node_dev, width), f32),
@@ -284,13 +287,7 @@
         cost_estimate=pl.CostEstimate(
             flops=2 * slots * tile * tile * width, bytes_accessed=8 * 2**20, transcendentals=0
         ),
-    )(tile_count, positions, place, adj_tiles, list(banks))
-
-    scaling = float(node_dev * groups * blocks) ** (-0.5)
-    piece = lax.all_to_all(grads, PLANE, 0, 0, tiled=True).astype(f32)
-    piece = lax.all_gather(jnp.sum(piece, axis=0).astype(bf16), EVERY_OTHER).astype(f32)
-    piece = jnp.sum(piece, axis=0)
-    piece = (piece + lax.ppermute(piece, "z_near", swap)) * scaling
+    )(tile_count, tile_pos, place, adj_tiles, list(banks), piece)
     grad_bias = piece[:2, hid:].reshape(hid)
     both = spread(piece[:, :hid].astype(bf16), PLANE).astype(f32).reshape(2 * width, hid)
     return new_part[None], hidden, both[:width], both[width:], grad_bias

time: 161 us -> 157 us (0.975)
  starting transfers between devices: 52.5 us -> 43.2 us
  blocking collectives: 88.5 us -> 85.3 us
  waiting for transfers between devices: 9.43 us -> 12.2 us
  Pallas kernels: 4.77 us -> 7.39 us
  other arithmetic: 0.09 us -> 1.93 us
    ppermute x4 -> x3, starting transfers between devices: 13 us -> 8.47 us  [the longest x1 3.91 us: body(): lax.ppermute(side_low, LINE, down)]
    all_to_all x1, waiting for transfers between devices: 0.01 us -> 3.36 us  [body(): stale = lax.all_to_all(stale_part[0], GRP, 0, 0, tiled=True)]
    all_to_all x1, waiting for transfers between devices: 7 us -> 4 us  [spread(): lax.all_to_all(jnp.broadcast_to(value[None], (copies,) + value.shape), ax...]
    ppermute x1, waiting for transfers between devices: 0.01 us -> 2.84 us  [body(): piece = (piece + lax.ppermute(piece, 'z_near', swap)) * scaling]
    all_to_all x1, starting transfers between devices: 15.3 us -> 12.7 us  [spread(): lax.all_to_all(jnp.broadcast_to(value[None], (copies,) + value.shape), ax...]
    all_to_all x1, blocking collectives: 18 us -> 15.6 us  [body(): piece = lax.all_to_all(grads, PLANE, 0, 0, tiled=True).astype(f32)]
    ppermute x1, starting transfers between devices: 4.22 us -> 1.92 us  [body(): piece = (piece + lax.ppermute(piece, 'z_near', swap)) * scaling]
  transfers between devices with their start and end apart: 9 -> 8, of which waited for: 3 -> 4; matrix products, arithmetic and copies ran while one was open for 0% -> 0% of each run, Pallas kernels for 2% -> 3%
where the time goes in v5:
time: 157 us; the launch traced here: 156 us
  blocking collectives  85.3 us (54%)
  starting transfers between devices  43.2 us (28%)
  waiting for transfers between devices  12.2 us (8%)
  Pallas kernels  7.39 us (5%)
  local copies, waits for them, and re-layouts  4.49 us (3%)
  other arithmetic  1.93 us (1%)
    all_gather x1, blocking collectives, body(): same = lax.all_gather(node_feats, EVERY_OTHER)  45.3 us
    all_gather x1, blocking collectives, body(): lax.all_gather(jnp.sum(piece, axis=0).astype(bf16), EVERY_OTHER).astype(f32)  24.4 us
    all_to_all x1, blocking collectives, body(): piece = lax.all_to_all(grads, PLANE, 0, 0, tiled=True).astype(f32)  15.6 us
    all_to_all x1, starting transfers between devices, body(): stale = lax.all_to_all(stale_part[0], GRP, 0, 0, tiled=True)  13.3 us
    all_to_all x1, starting transfers between devices, spread(): lax.all_to_all(jnp.broadcast_to(value[None], (copies,) + value.shape), ax...  12.7 us
    ppermute x1, starting transfers between devices, body(): lax.ppermute(low, 'x_hi', swap)  4.6 us
    all_to_all x1, waiting for transfers between devices, spread(): lax.all_to_all(jnp.broadcast_to(value[None], (copies,) + value.shape), ax...  4 us
    ppermute x1, starting transfers between devices, body(): lax.ppermute(side_low, LINE, down)  3.91 us
  transfers between devices with their start and end apart: 8, of which 4 were waited for; matrix products, arithmetic and copies ran while one was open for 0% of the time, Pallas kernels for 3%

profile of v5, /device:TPU:1, one launch (start us, length us, event | category | flops | bytes accessed | tf_op | source)
XLA Modules:
  0.0 156.0 jit_solution(16388950072933956681)
XLA Ops:
  0.7 45.3 %all-gather = bf16[2048,128]{1,0:T(8,128)(2,1)S(1)} all-gather(bf16[128,128]{1,0:T(8,128)(2,1)} %feats_ref.3), channel_id=2, replica_groups=mesh['y'=4,'x_lo'=2,'core'=2,'x_hi'=2,'z_far'=8,'z_mid'=2,'z_near'=2] {'..., dimensions={0}, use_global_device_ids=true | all-gather | bytes 557056 | tf_op jit(solution)/shard_map/all_gather | solution.py:192
  46.0 0.8 fusion.3
  46.9 4.6 %collective-permute-start.1 = (bf16[8,128,128]{2,1,0:T(8,128)(2,1)}, bf16[8,128,128]{2,1,0:T(8,128)(2,1)S(1)}, u32[]{:S(2)}, u32[]{:S(2)}) collective-permute-start(bf16[8,128,128]{2,1,0:T(8,128)(2,1)} %bitcast.1), channel_id=1, source_target_pairs={{0,32},{32,0},{1,33},{33,1},{2,34},{34,2},{3,35},{35,3},{4,36},{36... | collective-permute-start | bytes 786440 | tf_op jit(solution)/shard_map/ppermute | solution.py:199
  51.5 2.2 %collective-permute-start.2 = (bf16[8,128,128]{2,1,0:T(8,128)(2,1)}, bf16[8,128,128]{2,1,0:T(8,128)(2,1)}, u32[]{:S(2)}, u32[]{:S(2)}) collective-permute-start(bf16[8,128,128]{2,1,0:T(8,128)(2,1)} %bitcast.2), channel_id=1, source_target_pairs={{0,32},{32,0},{1,33},{33,1},{2,34},{34,2},{3,35},{35,3},{4,36},{36... | collective-permute-start | bytes 786440 | tf_op jit(solution)/shard_map/ppermute | solution.py:199
  53.7 2.6 %collective-permute-start = (bf16[16,128,128]{2,1,0:T(8,128)(2,1)S(1)}, bf16[16,128,128]{2,1,0:T(8,128)(2,1)S(1)}, u32[]{:S(2)}, u32[]{:S(2)}) collective-permute-start(bf16[16,128,128]{2,1,0:T(8,128)(2,1)S(1)} %bitcast.16), channel_id=1, source_target_pairs={{0,1},{1,2},{2,3},{3,4},{4,5},{5,6},{6,7},{7,8},{8,9},{9,10},{10,1... | collective-permute-start | bytes 1572872 | tf_op jit(solution)/shard_map/ppermute | solution.py:200
  56.3 13.3 %all-to-all-start = ((bf16[16,128,128]{2,1,0:T(8,128)(2,1)}), bf16[16,128,128]{2,1,0:T(8,128)(2,1)}, u32[]{:S(2)}, u32[]{:S(2)}) async-start(bf16[16,128,128]{2,1,0:T(8,128)(2,1)} %bitcast.21), calls=%async_computation | async-start | bytes 1048576 | tf_op jit(solution)/shard_map/all_to_all | solution.py:191
  69.6 3.9 %collective-permute-start.3 = (bf16[8,128,128]{2,1,0:T(8,128)(2,1)S(1)}, bf16[8,128,128]{2,1,0:T(8,128)(2,1)}, u32[]{:S(2)}, u32[]{:S(2)}) collective-permute-start(bf16[8,128,128]{2,1,0:T(8,128)(2,1)S(1)} %collective-permute-done.1.bank_refs_2_), channel_id=1, source_target_pairs={{0,31},{1,0},{2,1},{3,2},{4,3},{5,4},{6,5},{7,6},{8,7},{9,8},{10,9... | collective-permute-start | bytes 786440 | tf_op jit(solution)/shard_map/ppermute | solution.py:206
  73.6 1.9 %collective-permute-start.4 = (bf16[8,128,128]{2,1,0:T(8,128)(2,1)}, bf16[8,128,128]{2,1,0:T(8,128)(2,1)}, u32[]{:S(2)}, u32[]{:S(2)}) collective-permute-start(bf16[8,128,128]{2,1,0:T(8,128)(2,1)} %collective-permute-done.2.bank_refs_3_), channel_id=1, source_target_pairs={{0,1},{1,2},{2,3},{3,4},{4,5},{5,6},{6,7},{7,8},{8,9},{9,10},{10,1... | collective-permute-start | bytes 786440 | tf_op jit(solution)/shard_map/ppermute | solution.py:207
  76.2 3.4 %all-to-all-done.stale_ref = bf16[16,128,128]{2,1,0:T(8,128)(2,1)} async-done(((bf16[16,128,128]{2,1,0:T(8,128)(2,1)}), bf16[16,128,128]{2,1,0:T(8,128)(2,1)}, u32[]{:S(2)}, u32[]{:S(2)}) %all-to-all-start) | async-done | bytes 524320 | tf_op jit(solution)/shard_map/all_to_all | solution.py:191
  79.5 0.8 copy-done.3
  80.4 0.8 copy-done.4
  81.2 1.2 shard_map.128
  82.4 2.0 %collective-permute-done.4.bank_refs_5_ = bf16[8,128,128]{2,1,0:T(8,128)(2,1)} collective-permute-done((bf16[8,128,128]{2,1,0:T(8,128)(2,1)}, bf16[8,128,128]{2,1,0:T(8,128)(2,1)}, u32[]{:S(2)}, u32[]{:S(2)}) %collective-permute-start.4) | collective-permute-done | bytes 262176 | tf_op jit(solution)/shard_map/ppermute | solution.py:207
  84.5 3.1 %shard_map.129 = (bf16[128,256]{1,0:T(8,128)(2,1)}, bf16[32,8,384]{2,1,0:T(8,128)(2,1)S(1)}) custom-call(s32[1]{0:T(128)S(6)} %copy.14.count_ref, s32[16]{0:T(128)S(1)} %copy-done.5, s32[64]{0:T(128)S(1)} %fusion.place_ref, s32[1]{0:T(128)} %bitcast.3.own_ref, bf16[16,256,256]{2,1,0:T(8,128)(2,1)S(1)} %copy-done, bf16[16,128,128]{2,1,0:T(8,128)(2,1)S(1)} %bitcast.17, ...), custom_call_target="tpu_custom_call" | custom-call | flops 33554432 | bytes 1048576 | tf_op jit(solution)/shard_map/pallas_call | solution.py:240
  87.6 15.6 %all_to_all.15 = bf16[32,8,384]{2,1,0:T(8,128)(2,1)} all-to-all(bf16[32,8,384]{2,1,0:T(8,128)(2,1)S(1)} %get-tuple-element.15), channel_id=1, replica_groups=mesh['y'=4,'x_lo'=2,'core'=2,'x_hi'=2,'z_far'=8,'z_mid'=2,'z_near'=2] {'..., dimensions={0} | all-to-all | bytes 393216 | tf_op jit(solution)/shard_map/all_to_all | solution.py:273
  103.2 1.0 reduce_sum.21
  104.1 24.4 %all-gather.1 = bf16[128,384]{1,0:T(8,128)(2,1)S(1)} all-gather(bf16[8,384]{1,0:T(8,128)(2,1)S(1)} %reduce_sum.21), channel_id=3, replica_groups=mesh['y'=4,'x_lo'=2,'core'=2,'x_hi'=2,'z_far'=8,'z_mid'=2,'z_near'=2] {'..., dimensions={0}, use_global_device_ids=true | all-gather | bytes 104448 | tf_op jit(solution)/shard_map/all_gather | solution.py:274
  128.5 1.9 %collective-permute-start.5 = (f32[8,384]{1,0:T(8,128)S(1)}, f32[8,384]{1,0:T(8,128)S(1)}, u32[]{:S(2)}, u32[]{:S(2)}) collective-permute-start(f32[8,384]{1,0:T(8,128)S(1)} %convert_reduce_fusion), channel_id=1, source_target_pairs={{0,1},{1,0},{2,3},{3,2},{4,5},{5,4},{6,7},{7,6},{8,9},{9,8},{10,11... | collective-permute-start | bytes 36872 | tf_op jit(solution)/shard_map/ppermute | solution.py:276
  130.4 2.8 %collective-permute-done.5 = f32[8,384]{1,0:T(8,128)S(1)} collective-permute-done((f32[8,384]{1,0:T(8,128)S(1)}, f32[8,384]{1,0:T(8,128)S(1)}, u32[]{:S(2)}, u32[]{:S(2)}) %collective-permute-start.5) | collective-permute-done | bytes 12320 | tf_op jit(solution)/shard_map/ppermute | solution.py:276
  134.0 12.7 %all-to-all-start.2 = ((bf16[32,8,256]{2,1,0:T(8,128)(2,1)}), bf16[32,8,256]{2,1,0:T(8,128)(2,1)}, u32[]{:S(2)}, u32[]{:S(2)}) async-start(bf16[32,8,256]{2,1,0:T(8,128)(2,1)} %broadcast_in_dim.14), calls=%async_computation.2 | async-start | bytes 262144 | tf_op jit(solution)/shard_map/all_to_all | solution.py:19
  146.7 3.0 %shard_map.130 = bf16[16,128,128]{2,1,0:T(8,128)(2,1)} custom-call(s32[1]{0:T(128)S(6)} %copy.14.count_ref, s32[16]{0:T(128)S(1)} %copy-done.5, s32[64]{0:T(128)S(1)} %fusion.place_ref, bf16[16,256,256]{2,1,0:T(8,128)(2,1)S(1)} %copy-done, bf16[16,128,128]{2,1,0:T(8,128)(2,1)S(1)} %bitcast.18, bf16[16,128,128]{2,1,0:T(8,128)(2,1)S(1)} %collective-permute-done.bank_refs_1_, ...), custom_call_target="tpu_custom_call" | custom-call | flops 268435456 | bytes 8388608 | tf_op jit(solution)/shard_map/pallas_call | solution.py:277
  150.3 4.0 %all-to-all-done.2 = bf16[32,8,256]{2,1,0:T(8,128)(2,1)} async-done(((bf16[32,8,256]{2,1,0:T(8,128)(2,1)}), bf16[32,8,256]{2,1,0:T(8,128)(2,1)}, u32[]{:S(2)}, u32[]{:S(2)}) %all-to-all-start.2) | async-done | bytes 131104 | tf_op jit(solution)/shard_map/all_to_all | solution.py:19
  154.3 0.9 convert_element_type.20
  155.2 0.7 slice_bitcast_fusion
  (22 shorter events, 1.3 us)
Async XLA Ops:
  0.6 78.9 %copy-start.1 = (bf16[128,128]{1,0:T(8,128)(2,1)S(1)}, bf16[128,128]{1,0:T(8,128)(2,1)}, u32[]{:S(2)}) copy-start(bf16[128,128]{1,0:T(8,128)(2,1)} %feats_ref.3) | copy-start | bytes 98308
  0.6 78.9 %copy-start.2 = (bf16[128,256]{1,0:T(8,128)(2,1)S(1)}, bf16[128,256]{1,0:T(8,128)(2,1)}, u32[]{:S(2)}) copy-start(bf16[128,256]{1,0:T(8,128)(2,1)} %w_self_ref.1) | copy-start | bytes 196612
  0.7 83.8 %copy-start.5 = (s32[16]{0:T(128)S(1)}, s32[16]{0:T(128)}, u32[]{:S(2)}) copy-start(s32[16]{0:T(128)} %pos_ref.3) | copy-start | bytes 196
  0.7 83.8 %copy-start = (bf16[16,256,256]{2,1,0:T(8,128)(2,1)S(1)}, bf16[16,256,256]{2,1,0:T(8,128)(2,1)}, u32[]{:S(2)}) copy-start(bf16[16,256,256]{2,1,0:T(8,128)(2,1)} %adj_ref.3) | copy-start | bytes 6291460
  0.7 83.8 %copy-start.6 = (f32[256]{0:T(256)S(1)}, f32[256]{0:T(256)}, u32[]{:S(2)}) copy-start(f32[256]{0:T(256)} %param.16) | copy-start | bytes 3076
  46.9 22.8 %collective-permute-start.1 = (bf16[8,128,128]{2,1,0:T(8,128)(2,1)}, bf16[8,128,128]{2,1,0:T(8,128)(2,1)S(1)}, u32[]{:S(2)}, u32[]{:S(2)}) collective-permute-start(bf16[8,128,128]{2,1,0:T(8,128)(2,1)} %bitcast.1), channel_id=1, source_target_pairs={{0,32},{32,0},{1,33},{33,1},{2,34},{34,2},{3,35},{35,3},{4,36},{36... | collective-permute-start | bytes 786440 | tf_op jit(solution)/shard_map/ppermute | solution.py:199
  51.5 22.1 %collective-permute-start.2 = (bf16[8,128,128]{2,1,0:T(8,128)(2,1)}, bf16[8,128,128]{2,1,0:T(8,128)(2,1)}, u32[]{:S(2)}, u32[]{:S(2)}) collective-permute-start(bf16[8,128,128]{2,1,0:T(8,128)(2,1)} %bitcast.2), channel_id=1, source_target_pairs={{0,32},{32,0},{1,33},{33,1},{2,34},{34,2},{3,35},{35,3},{4,36},{36... | collective-permute-start | bytes 786440 | tf_op jit(solution)/shard_map/ppermute | solution.py:199
  53.7 30.8 %collective-permute-start = (bf16[16,128,128]{2,1,0:T(8,128)(2,1)S(1)}, bf16[16,128,128]{2,1,0:T(8,128)(2,1)S(1)}, u32[]{:S(2)}, u32[]{:S(2)}) collective-permute-start(bf16[16,128,128]{2,1,0:T(8,128)(2,1)S(1)} %bitcast.16), channel_id=1, source_target_pairs={{0,1},{1,2},{2,3},{3,4},{4,5},{5,6},{6,7},{7,8},{8,9},{9,10},{10,1... | collective-permute-start | bytes 1572872 | tf_op jit(solution)/shard_map/ppermute | solution.py:200
  56.3 23.2 %all-to-all-start = ((bf16[16,128,128]{2,1,0:T(8,128)(2,1)}), bf16[16,128,128]{2,1,0:T(8,128)(2,1)}, u32[]{:S(2)}, u32[]{:S(2)}) async-start(bf16[16,128,128]{2,1,0:T(8,128)(2,1)} %bitcast.21), calls=%async_computation | async-start | bytes 1048576 | tf_op jit(solution)/shard_map/all_to_all | solution.py:191
  69.6 12.8 %collective-permute-start.3 = (bf16[8,128,128]{2,1,0:T(8,128)(2,1)S(1)}, bf16[8,128,128]{2,1,0:T(8,128)(2,1)}, u32[]{:S(2)}, u32[]{:S(2)}) collective-permute-start(bf16[8,128,128]{2,1,0:T(8,128)(2,1)S(1)} %collective-permute-done.1.bank_refs_2_), channel_id=1, source_target_pairs={{0,31},{1,0},{2,1},{3,2},{4,3},{5,4},{6,5},{7,6},{8,7},{9,8},{10,9... | collective-permute-start | bytes 786440 | tf_op jit(solution)/shard_map/ppermute | solution.py:206
  73.6 10.9 %collective-permute-start.4 = (bf16[8,128,128]{2,1,0:T(8,128)(2,1)}, bf16[8,128,128]{2,1,0:T(8,128)(2,1)}, u32[]{:S(2)}, u32[]{:S(2)}) collective-permute-start(bf16[8,128,128]{2,1,0:T(8,128)(2,1)} %collective-permute-done.2.bank_refs_3_), channel_id=1, source_target_pairs={{0,1},{1,2},{2,3},{3,4},{4,5},{5,6},{6,7},{7,8},{8,9},{9,10},{10,1... | collective-permute-start | bytes 786440 | tf_op jit(solution)/shard_map/ppermute | solution.py:207
  79.5 0.8 copy-start.3
  80.4 0.8 copy-start.4
  128.5 4.8 %collective-permute-start.5 = (f32[8,384]{1,0:T(8,128)S(1)}, f32[8,384]{1,0:T(8,128)S(1)}, u32[]{:S(2)}, u32[]{:S(2)}) collective-permute-start(f32[8,384]{1,0:T(8,128)S(1)} %convert_reduce_fusion), channel_id=1, source_target_pairs={{0,1},{1,0},{2,3},{3,2},{4,5},{5,4},{6,7},{7,6},{8,9},{9,8},{10,11... | collective-permute-start | bytes 36872 | tf_op jit(solution)/shard_map/ppermute | solution.py:276
  134.0 20.3 %all-to-all-start.2 = ((bf16[32,8,256]{2,1,0:T(8,128)(2,1)}), bf16[32,8,256]{2,1,0:T(8,128)(2,1)}, u32[]{:S(2)}, u32[]{:S(2)}) async-start(bf16[32,8,256]{2,1,0:T(8,128)(2,1)} %broadcast_in_dim.14), calls=%async_computation.2 | async-start | bytes 262144 | tf_op jit(solution)/shard_map/all_to_all | solution.py:19

commit v6 on v5

--- a/solution.py
+++ b/solution.py
@@ -150,13 +150,33 @@
 
 
 def partial_kernel(
-    count_ref, pos_ref, place_ref, adj_ref, bank_refs, _, part_ref, acc_ref, source_ref
+    count_ref,
+    pos_ref,
+    place_ref,
+    adj_ref,
+    bank_refs,
+    _,
+    part_ref,
+    acc_ref,
+    source_ref,
+    tiles_ref,
+    tile_sem,
 ):
     tile = adj_ref.shape[1]
     _, node_dev, _ = part_ref.shape
     per_tile = tile // node_dev
     bank_slots = 2 * bank_refs[0].shape[0]
     col_tiles = place_ref.shape[0] // per_tile
+    count = count_ref[0]
+
+    def tile_copy(slot):
+        return pltpu.make_async_copy(adj_ref.at[slot], tiles_ref.at[slot], tile_sem.at[slot])
+
+    def fetch(slot, carry):
+        tile_copy(slot).start()
+        return carry
+
+    lax.fori_loop(0, count, fetch, 0)
     acc_ref[...] = jnp.zeros_like(acc_ref)
 
     def add_tile(slot, carry):
@@ -170,12 +190,13 @@
                 def _():
                     source_ref[j * node_dev : (j + 1) * node_dev, :] = ref[block]
 
-        product = jnp.dot(adj_ref[slot], source_ref[...], preferred_element_type=jnp.float32)
+        tile_copy(slot).wait()
+        product = jnp.dot(tiles_ref[slot], source_ref[...], preferred_element_type=jnp.float32)
         rows = pl.ds(pl.multiple_of(row_tile * tile, tile), tile)
         acc_ref[rows, :] += product
         return carry
 
-    lax.fori_loop(0, count_ref[0], add_tile, 0)
+    lax.fori_loop(0, count, add_tile, 0)
     part_ref[...] = acc_ref[...].reshape(part_ref.shape).astype(part_ref.dtype)
 
 
@@ -193,8 +214,8 @@
     length = lax.axis_size(LINE)
     up = [(i, (i + 1) % length) for i in range(length)]
     down = [(i, (i - 1) % length) for i in range(length)]
-    half = same.shape[0] // 2
-    low, high = same[:half], same[half:]
+    cut = same.shape[0] // 2
+    low, high = same[:cut], same[cut:]
     swap = [(0, 1), (1, 0)]
     side_low, side_high = lax.ppermute(low, "x_hi", swap), lax.ppermute(high, "x_hi", swap)
     beside = lax.ppermute(same, LINE, up)
@@ -211,8 +232,8 @@
     other_parity = index % 2 != lax.axis_index("z_near")
     slot = index % length // 2
     low_bank = jnp.where(other_side, 2 + 2 * other_parity, other_parity)
-    first = other_side & (slot >= half)
-    place = (low_bank + first) * length + jnp.where(first, slot - half, slot)
+    first = other_side & (slot >= cut)
+    place = (low_bank + first) * length + jnp.where(first, slot - cut, slot)
     own = lax.axis_index(GRP).reshape(1).astype(jnp.int32)
 
     smem = pl.BlockSpec(memory_space=pltpu.SMEM)
@@ -220,8 +241,10 @@
     piece_rows = 2 * width // plane
     tile, slots = adj_tiles.shape[1], adj_tiles.shape[0]
     whole = pl.BlockSpec(memory_space=pl.ANY)
+    hbm = pl.BlockSpec(memory_space=pltpu.HBM)
     bf16, f32 = jnp.bfloat16, jnp.float32
     limit = pltpu.CompilerParams(vmem_limit_bytes=32 * 1024 * 1024)
+    most = pltpu.CompilerParams(vmem_limit_bytes=62 * 1024 * 1024)
     stale_sum, base, w_neigh, cotangent = pl.pallas_call(
         early_kernel,
         out_shape=(
@@ -243,7 +266,7 @@
             jax.ShapeDtypeStruct((node_dev, hid), bf16),
             jax.ShapeDtypeStruct((plane, piece_rows, hid + hid // 2), bf16),
         ),
-        in_specs=[smem] * 4 + [whole, [whole] * len(banks)] + [vmem] * 6,
+        in_specs=[smem] * 4 + [hbm, [whole] * len(banks)] + [vmem] * 6,
         out_specs=(vmem, vmem),
         scratch_shapes=[
             pltpu.VMEM((slots, node_dev, tile), bf16),
@@ -277,13 +300,15 @@
     new_part = pl.pallas_call(
         partial_kernel,
         out_shape=jax.ShapeDtypeStruct((groups, node_dev, width), bf16),
-        in_specs=[smem] * 3 + [vmem, [vmem] * len(banks), whole],
+        in_specs=[smem] * 3 + [hbm, [vmem] * len(banks), whole],
         out_specs=vmem,
         scratch_shapes=[
             pltpu.VMEM((groups * node_dev, width), f32),
             pltpu.VMEM((tile, width), bf16),
+            pltpu.VMEM((slots, tile, tile), bf16),
+            pltpu.SemaphoreType.DMA((slots,)),
         ],
-        compiler_params=limit,
+        compiler_params=most,
         cost_estimate=pl.CostEstimate(
             flops=2 * slots * tile * tile * width, bytes_accessed=8 * 2**20, transcendentals=0
         ),

time: 157 us -> 154 us (0.981)
  waiting for transfers between devices: 12.2 us -> 9.6 us
  other arithmetic: 1.93 us -> 0.1 us
    all_to_all x1, blocking collectives: 15.6 us -> 17.3 us  [body(): piece = lax.all_to_all(grads, PLANE, 0, 0, tiled=True).astype(f32)]
  transfers between devices with their start and end apart: 8 -> 8, of which waited for: 4 -> 4; matrix products, arithmetic and copies ran while one was open for 0% -> 1% of each run, Pallas kernels for 3% -> 3%
where the time goes in v6:
time: 154 us; the launch traced here: 153 us
  blocking collectives  86.2 us (56%)
  starting transfers between devices  43.8 us (28%)
  waiting for transfers between devices  9.6 us (6%)
  Pallas kernels  6.66 us (4%)
  local copies, waits for them, and re-layouts  5.26 us (3%)
    all_gather x1, blocking collectives, body(): same = lax.all_gather(node_feats, EVERY_OTHER)  45.3 us
    all_gather x1, blocking collectives, body(): lax.all_gather(jnp.sum(piece, axis=0).astype(bf16), EVERY_OTHER).astype(f32)  23.5 us
    all_to_all x1, blocking collectives, body(): piece = lax.all_to_all(grads, PLANE, 0, 0, tiled=True).astype(f32)  17.3 us
    all_to_all x1, starting transfers between devices, body(): stale = lax.all_to_all(stale_part[0], GRP, 0, 0, tiled=True)  13.3 us
    all_to_all x1, starting transfers between devices, spread(): lax.all_to_all(jnp.broadcast_to(value[None], (copies,) + value.shape), ax...  12 us
    ppermute x1, starting transfers between devices, body(): lax.ppermute(low, 'x_hi', swap)  4.6 us
    ppermute x1, starting transfers between devices, body(): lax.ppermute(side_low, LINE, down)  3.91 us
    pallas_call x1, Pallas kernels, body(): pl.pallas_call(partial_kernel, out_shape=jax.ShapeDtypeStruct((groups, no...  3.58 us
  transfers between devices with their start and end apart: 8, of which 4 were waited for; matrix products, arithmetic and copies ran while one was open for 1% of the time, Pallas kernels for 3%

profile of v6, /device:TPU:1, one launch (start us, length us, event | category | flops | bytes accessed | tf_op | source)
XLA Modules:
  0.0 153.1 jit_solution(14261040558379226878)
XLA Ops:
  0.7 45.3 %all-gather = bf16[2048,128]{1,0:T(8,128)(2,1)S(1)} all-gather(bf16[128,128]{1,0:T(8,128)(2,1)} %feats_ref.3), channel_id=2, replica_groups=mesh['y'=4,'x_lo'=2,'core'=2,'x_hi'=2,'z_far'=8,'z_mid'=2,'z_near'=2] {'..., dimensions={0}, use_global_device_ids=true | all-gather | bytes 557056 | tf_op jit(solution)/shard_map/all_gather | solution.py:213
  46.0 0.9 fusion.3
  46.9 4.6 %collective-permute-start.1 = (bf16[8,128,128]{2,1,0:T(8,128)(2,1)}, bf16[8,128,128]{2,1,0:T(8,128)(2,1)S(1)}, u32[]{:S(2)}, u32[]{:S(2)}) collective-permute-start(bf16[8,128,128]{2,1,0:T(8,128)(2,1)} %bitcast.1), channel_id=1, source_target_pairs={{0,32},{32,0},{1,33},{33,1},{2,34},{34,2},{3,35},{35,3},{4,36},{36... | collective-permute-start | bytes 786440 | tf_op jit(solution)/shard_map/ppermute | solution.py:220
  51.5 2.2 %collective-permute-start.2 = (bf16[8,128,128]{2,1,0:T(8,128)(2,1)}, bf16[8,128,128]{2,1,0:T(8,128)(2,1)}, u32[]{:S(2)}, u32[]{:S(2)}) collective-permute-start(bf16[8,128,128]{2,1,0:T(8,128)(2,1)} %bitcast.2), channel_id=1, source_target_pairs={{0,32},{32,0},{1,33},{33,1},{2,34},{34,2},{3,35},{35,3},{4,36},{36... | collective-permute-start | bytes 786440 | tf_op jit(solution)/shard_map/ppermute | solution.py:220
  53.7 2.6 %collective-permute-start = (bf16[16,128,128]{2,1,0:T(8,128)(2,1)S(1)}, bf16[16,128,128]{2,1,0:T(8,128)(2,1)S(1)}, u32[]{:S(2)}, u32[]{:S(2)}) collective-permute-start(bf16[16,128,128]{2,1,0:T(8,128)(2,1)S(1)} %bitcast.16), channel_id=1, source_target_pairs={{0,1},{1,2},{2,3},{3,4},{4,5},{5,6},{6,7},{7,8},{8,9},{9,10},{10,1... | collective-permute-start | bytes 1572872 | tf_op jit(solution)/shard_map/ppermute | solution.py:221
  56.4 13.3 %all-to-all-start = ((bf16[16,128,128]{2,1,0:T(8,128)(2,1)}), bf16[16,128,128]{2,1,0:T(8,128)(2,1)}, u32[]{:S(2)}, u32[]{:S(2)}) async-start(bf16[16,128,128]{2,1,0:T(8,128)(2,1)} %bitcast.21), calls=%async_computation | async-start | bytes 1048576 | tf_op jit(solution)/shard_map/all_to_all | solution.py:212
  69.7 3.9 %collective-permute-start.3 = (bf16[8,128,128]{2,1,0:T(8,128)(2,1)S(1)}, bf16[8,128,128]{2,1,0:T(8,128)(2,1)}, u32[]{:S(2)}, u32[]{:S(2)}) collective-permute-start(bf16[8,128,128]{2,1,0:T(8,128)(2,1)S(1)} %collective-permute-done.1.bank_refs_2_), channel_id=1, source_target_pairs={{0,31},{1,0},{2,1},{3,2},{4,3},{5,4},{6,5},{7,6},{8,7},{9,8},{10,9... | collective-permute-start | bytes 786440 | tf_op jit(solution)/shard_map/ppermute | solution.py:227
  73.6 1.9 %collective-permute-start.4 = (bf16[8,128,128]{2,1,0:T(8,128)(2,1)}, bf16[8,128,128]{2,1,0:T(8,128)(2,1)}, u32[]{:S(2)}, u32[]{:S(2)}) collective-permute-start(bf16[8,128,128]{2,1,0:T(8,128)(2,1)} %collective-permute-done.2.bank_refs_3_), channel_id=1, source_target_pairs={{0,1},{1,2},{2,3},{3,4},{4,5},{5,6},{6,7},{7,8},{8,9},{9,10},{10,1... | collective-permute-start | bytes 786440 | tf_op jit(solution)/shard_map/ppermute | solution.py:228
  76.3 3.3 %all-to-all-done.stale_ref = bf16[16,128,128]{2,1,0:T(8,128)(2,1)} async-done(((bf16[16,128,128]{2,1,0:T(8,128)(2,1)}), bf16[16,128,128]{2,1,0:T(8,128)(2,1)}, u32[]{:S(2)}, u32[]{:S(2)}) %all-to-all-start) | async-done | bytes 524320 | tf_op jit(solution)/shard_map/all_to_all | solution.py:212
  79.6 0.8 copy-done.6
  80.5 0.8 copy-done.7
  81.3 1.2 shard_map.128
  82.5 2.0 %collective-permute-done.4.bank_refs_5_ = bf16[8,128,128]{2,1,0:T(8,128)(2,1)} collective-permute-done((bf16[8,128,128]{2,1,0:T(8,128)(2,1)}, bf16[8,128,128]{2,1,0:T(8,128)(2,1)}, u32[]{:S(2)}, u32[]{:S(2)}) %collective-permute-start.4) | collective-permute-done | bytes 262176 | tf_op jit(solution)/shard_map/ppermute | solution.py:228
  84.5 1.9 %shard_map.129 = (bf16[128,256]{1,0:T(8,128)(2,1)}, bf16[32,8,384]{2,1,0:T(8,128)(2,1)S(1)}) custom-call(s32[1]{0:T(128)S(6)} %copy.14.count_ref, s32[16]{0:T(128)S(1)} %copy-done.8, s32[64]{0:T(128)S(1)} %fusion.place_ref, s32[1]{0:T(128)} %bitcast.3.own_ref, bf16[16,256,256]{2,1,0:T(8,128)(2,1)S(1)} %copy-done, bf16[16,128,128]{2,1,0:T(8,128)(2,1)S(1)} %bitcast.17, ...), custom_call_target="tpu_custom_call" | custom-call | flops 33554432 | bytes 1048576 | tf_op jit(solution)/shard_map/pallas_call | solution.py:263
  86.5 17.3 %all_to_all.15 = bf16[32,8,384]{2,1,0:T(8,128)(2,1)S(1)} all-to-all(bf16[32,8,384]{2,1,0:T(8,128)(2,1)S(1)} %get-tuple-element.15), channel_id=1, replica_groups=mesh['y'=4,'x_lo'=2,'core'=2,'x_hi'=2,'z_far'=8,'z_mid'=2,'z_near'=2] {'..., dimensions={0} | all-to-all | bytes 393216 | tf_op jit(solution)/shard_map/all_to_all | solution.py:296
  103.8 23.5 %all-gather.1 = bf16[128,384]{1,0:T(8,128)(2,1)S(1)} all-gather(bf16[8,384]{1,0:T(8,128)(2,1)S(1)} %reduce_sum.21), channel_id=3, replica_groups=mesh['y'=4,'x_lo'=2,'core'=2,'x_hi'=2,'z_far'=8,'z_mid'=2,'z_near'=2] {'..., dimensions={0}, use_global_device_ids=true | all-gather | bytes 104448 | tf_op jit(solution)/shard_map/all_gather | solution.py:297
  127.4 3.2 %collective-permute-start.5 = (f32[8,384]{1,0:T(8,128)S(1)}, f32[8,384]{1,0:T(8,128)S(1)}, u32[]{:S(2)}, u32[]{:S(2)}) collective-permute-start(f32[8,384]{1,0:T(8,128)S(1)} %convert_reduce_fusion), channel_id=1, source_target_pairs={{0,1},{1,0},{2,3},{3,2},{4,5},{5,4},{6,7},{7,6},{8,9},{9,8},{10,11... | collective-permute-start | bytes 36872 | tf_op jit(solution)/shard_map/ppermute | solution.py:299
  130.5 1.5 %collective-permute-done.5 = f32[8,384]{1,0:T(8,128)S(1)} collective-permute-done((f32[8,384]{1,0:T(8,128)S(1)}, f32[8,384]{1,0:T(8,128)S(1)}, u32[]{:S(2)}, u32[]{:S(2)}) %collective-permute-start.5) | collective-permute-done | bytes 12320 | tf_op jit(solution)/shard_map/ppermute | solution.py:299
  132.1 0.7 broadcast_in_dim.14
  132.8 12.0 %all-to-all-start.2 = ((bf16[32,8,256]{2,1,0:T(8,128)(2,1)}), bf16[32,8,256]{2,1,0:T(8,128)(2,1)S(1)}, u32[]{:S(2)}, u32[]{:S(2)}) async-start(bf16[32,8,256]{2,1,0:T(8,128)(2,1)} %broadcast_in_dim.14), calls=%async_computation.2 | async-start | bytes 262144 | tf_op jit(solution)/shard_map/all_to_all | solution.py:19
  144.8 3.6 %shard_map.130 = bf16[16,128,128]{2,1,0:T(8,128)(2,1)} custom-call(s32[1]{0:T(128)S(6)} %copy.14.count_ref, s32[16]{0:T(128)} %pos_ref.3, s32[64]{0:T(128)} %copy-done.9, bf16[16,256,256]{2,1,0:T(8,128)(2,1)} %adj_ref.3, bf16[16,128,128]{2,1,0:T(8,128)(2,1)} %bitcast.18, bf16[16,128,128]{2,1,0:T(8,128)(2,1)} %copy-done.2, bf16[8,128,128]{2,1,0:T(8,128)(2,1)} %copy-done.3, ...), custom_call_target="tpu_custom_call" | custom-call | flops 268435456 | bytes 8388608 | tf_op jit(solution)/shard_map/pallas_call | solution.py:300
  148.4 1.3 slice_bitcast_fusion.2
  149.6 2.7 %all-to-all-done.2 = bf16[32,8,256]{2,1,0:T(8,128)(2,1)S(1)} async-done(((bf16[32,8,256]{2,1,0:T(8,128)(2,1)}), bf16[32,8,256]{2,1,0:T(8,128)(2,1)S(1)}, u32[]{:S(2)}, u32[]{:S(2)}) %all-to-all-start.2) | async-done | bytes 131104 | tf_op jit(solution)/shard_map/all_to_all | solution.py:19
  152.4 0.7 slice_bitcast_fusion
  (32 shorter events, 0.2 us)
Async XLA Ops:
  0.6 79.0 %copy-start.4 = (bf16[128,128]{1,0:T(8,128)(2,1)S(1)}, bf16[128,128]{1,0:T(8,128)(2,1)}, u32[]{:S(2)}) copy-start(bf16[128,128]{1,0:T(8,128)(2,1)} %feats_ref.3) | copy-start | bytes 98308
  0.6 79.0 %copy-start.5 = (bf16[128,256]{1,0:T(8,128)(2,1)S(1)}, bf16[128,256]{1,0:T(8,128)(2,1)}, u32[]{:S(2)}) copy-start(bf16[128,256]{1,0:T(8,128)(2,1)} %w_self_ref.1) | copy-start | bytes 196612
  0.7 83.9 %copy-start.8 = (s32[16]{0:T(128)S(1)}, s32[16]{0:T(128)}, u32[]{:S(2)}) copy-start(s32[16]{0:T(128)} %pos_ref.3) | copy-start | bytes 196
  0.7 83.9 %copy-start = (bf16[16,256,256]{2,1,0:T(8,128)(2,1)S(1)}, bf16[16,256,256]{2,1,0:T(8,128)(2,1)}, u32[]{:S(2)}) copy-start(bf16[16,256,256]{2,1,0:T(8,128)(2,1)} %adj_ref.3) | copy-start | bytes 6291460
  0.7 83.9 %copy-start.10 = (f32[256]{0:T(256)S(1)}, f32[256]{0:T(256)}, u32[]{:S(2)}) copy-start(f32[256]{0:T(256)} %param.16) | copy-start | bytes 3076
  46.0 40.4 %copy-start.1 = (bf16[2048,128]{1,0:T(8,128)(2,1)}, bf16[2048,128]{1,0:T(8,128)(2,1)S(1)}, u32[]{:S(2)}) copy-start(bf16[2048,128]{1,0:T(8,128)(2,1)S(1)} %all-gather) | copy-start | bytes 1572868
  46.9 22.8 %collective-permute-start.1 = (bf16[8,128,128]{2,1,0:T(8,128)(2,1)}, bf16[8,128,128]{2,1,0:T(8,128)(2,1)S(1)}, u32[]{:S(2)}, u32[]{:S(2)}) collective-permute-start(bf16[8,128,128]{2,1,0:T(8,128)(2,1)} %bitcast.1), channel_id=1, source_target_pairs={{0,32},{32,0},{1,33},{33,1},{2,34},{34,2},{3,35},{35,3},{4,36},{36... | collective-permute-start | bytes 786440 | tf_op jit(solution)/shard_map/ppermute | solution.py:220
  51.5 22.1 %collective-permute-start.2 = (bf16[8,128,128]{2,1,0:T(8,128)(2,1)}, bf16[8,128,128]{2,1,0:T(8,128)(2,1)}, u32[]{:S(2)}, u32[]{:S(2)}) collective-permute-start(bf16[8,128,128]{2,1,0:T(8,128)(2,1)} %bitcast.2), channel_id=1, source_target_pairs={{0,32},{32,0},{1,33},{33,1},{2,34},{34,2},{3,35},{35,3},{4,36},{36... | collective-permute-start | bytes 786440 | tf_op jit(solution)/shard_map/ppermute | solution.py:220
  53.7 30.8 %collective-permute-start = (bf16[16,128,128]{2,1,0:T(8,128)(2,1)S(1)}, bf16[16,128,128]{2,1,0:T(8,128)(2,1)S(1)}, u32[]{:S(2)}, u32[]{:S(2)}) collective-permute-start(bf16[16,128,128]{2,1,0:T(8,128)(2,1)S(1)} %bitcast.16), channel_id=1, source_target_pairs={{0,1},{1,2},{2,3},{3,4},{4,5},{5,6},{6,7},{7,8},{8,9},{9,10},{10,1... | collective-permute-start | bytes 1572872 | tf_op jit(solution)/shard_map/ppermute | solution.py:221
  56.4 23.2 %all-to-all-start = ((bf16[16,128,128]{2,1,0:T(8,128)(2,1)}), bf16[16,128,128]{2,1,0:T(8,128)(2,1)}, u32[]{:S(2)}, u32[]{:S(2)}) async-start(bf16[16,128,128]{2,1,0:T(8,128)(2,1)} %bitcast.21), calls=%async_computation | async-start | bytes 1048576 | tf_op jit(solution)/shard_map/all_to_all | solution.py:212
  69.7 16.7 %copy-start.3 = (bf16[8,128,128]{2,1,0:T(8,128)(2,1)}, bf16[8,128,128]{2,1,0:T(8,128)(2,1)S(1)}, u32[]{:S(2)}) copy-start(bf16[8,128,128]{2,1,0:T(8,128)(2,1)S(1)} %collective-permute-done.1.bank_refs_2_) | copy-start | bytes 786436
  69.7 12.8 %collective-permute-start.3 = (bf16[8,128,128]{2,1,0:T(8,128)(2,1)S(1)}, bf16[8,128,128]{2,1,0:T(8,128)(2,1)}, u32[]{:S(2)}, u32[]{:S(2)}) collective-permute-start(bf16[8,128,128]{2,1,0:T(8,128)(2,1)S(1)} %collective-permute-done.1.bank_refs_2_), channel_id=1, source_target_pairs={{0,31},{1,0},{2,1},{3,2},{4,3},{5,4},{6,5},{7,6},{8,7},{9,8},{10,9... | collective-permute-start | bytes 786440 | tf_op jit(solution)/shard_map/ppermute | solution.py:227
  73.6 10.9 %collective-permute-start.4 = (bf16[8,128,128]{2,1,0:T(8,128)(2,1)}, bf16[8,128,128]{2,1,0:T(8,128)(2,1)}, u32[]{:S(2)}, u32[]{:S(2)}) collective-permute-start(bf16[8,128,128]{2,1,0:T(8,128)(2,1)} %collective-permute-done.2.bank_refs_3_), channel_id=1, source_target_pairs={{0,1},{1,2},{2,3},{3,4},{4,5},{5,6},{6,7},{7,8},{8,9},{9,10},{10,1... | collective-permute-start | bytes 786440 | tf_op jit(solution)/shard_map/ppermute | solution.py:228
  76.3 10.2 %copy-start.9 = (s32[64]{0:T(128)}, s32[64]{0:T(128)S(1)}, u32[]{:S(2)}) copy-start(s32[64]{0:T(128)S(1)} %fusion.place_ref) | copy-start | bytes 772
  79.6 0.8 copy-start.6
  80.4 0.8 copy-start.7
  84.5 1.9 %copy-start.2 = (bf16[16,128,128]{2,1,0:T(8,128)(2,1)}, bf16[16,128,128]{2,1,0:T(8,128)(2,1)S(1)}, u32[]{:S(2)}) copy-start(bf16[16,128,128]{2,1,0:T(8,128)(2,1)S(1)} %collective-permute-done.bank_refs_1_) | copy-start | bytes 1572868
  127.4 4.7 %collective-permute-start.5 = (f32[8,384]{1,0:T(8,128)S(1)}, f32[8,384]{1,0:T(8,128)S(1)}, u32[]{:S(2)}, u32[]{:S(2)}) collective-permute-start(f32[8,384]{1,0:T(8,128)S(1)} %convert_reduce_fusion), channel_id=1, source_target_pairs={{0,1},{1,0},{2,3},{3,2},{4,5},{5,4},{6,7},{7,6},{8,9},{9,8},{10,11... | collective-permute-start | bytes 36872 | tf_op jit(solution)/shard_map/ppermute | solution.py:299
  132.1 12.7 %copy-start.11 = (f32[8,384]{1,0:T(8,128)}, f32[8,384]{1,0:T(8,128)S(1)}, u32[]{:S(2)}) copy-start(f32[8,384]{1,0:T(8,128)S(1)} %add_multiply_fusion._) | copy-start | bytes 36868
  132.8 19.6 %all-to-all-start.2 = ((bf16[32,8,256]{2,1,0:T(8,128)(2,1)}), bf16[32,8,256]{2,1,0:T(8,128)(2,1)S(1)}, u32[]{:S(2)}, u32[]{:S(2)}) async-start(bf16[32,8,256]{2,1,0:T(8,128)(2,1)} %broadcast_in_dim.14), calls=%async_computation.2 | async-start | bytes 262144 | tf_op jit(solution)/shard_map/all_to_all | solution.py:19

commit v7 on v6

--- a/solution.py
+++ b/solution.py
@@ -12,13 +12,6 @@
 BLK = ("x_hi",) + LINE
 ALL = GRP + BLK
 SIZES = (4, 2, 2, 2, 8, 2, 2)
-
-
-def spread(value, axes):
-    copies = lax.axis_size(axes)
-    return lax.all_to_all(
-        jnp.broadcast_to(value[None], (copies,) + value.shape), axes, 0, 0, tiled=True
-    )
 
 
 def split_position(position, col_tiles, per_tile):
@@ -244,6 +237,7 @@
     hbm = pl.BlockSpec(memory_space=pltpu.HBM)
     bf16, f32 = jnp.bfloat16, jnp.float32
     limit = pltpu.CompilerParams(vmem_limit_bytes=32 * 1024 * 1024)
+    broad = pltpu.CompilerParams(vmem_limit_bytes=51 * 1024 * 1024)
     most = pltpu.CompilerParams(vmem_limit_bytes=62 * 1024 * 1024)
     stale_sum, base, w_neigh, cotangent = pl.pallas_call(
         early_kernel,
@@ -274,7 +268,7 @@
             pltpu.SemaphoreType.DMA((slots,)),
             pltpu.SemaphoreType.DMA((slots, tile // node_dev)),
         ],
-        compiler_params=limit,
+        compiler_params=broad,
         cost_estimate=pl.CostEstimate(
             flops=8 * node_dev * width * hid, bytes_accessed=2**20, transcendentals=0
         ),
@@ -297,6 +291,9 @@
     piece = lax.all_gather(jnp.sum(piece, axis=0).astype(bf16), EVERY_OTHER).astype(f32)
     piece = jnp.sum(piece, axis=0)
     piece = (piece + lax.ppermute(piece, "z_near", swap)) * scaling
+    grad_bias = piece[:2, hid:].reshape(hid)
+    copies = jnp.broadcast_to(piece[None, :, :hid].astype(bf16), (plane, piece_rows, hid))
+    both = lax.all_to_all(copies, PLANE, 0, 0, tiled=True).astype(f32).reshape(2 * width, hid)
     new_part = pl.pallas_call(
         partial_kernel,
         out_shape=jax.ShapeDtypeStruct((groups, node_dev, width), bf16),
@@ -312,9 +309,7 @@
         cost_estimate=pl.CostEstimate(
             flops=2 * slots * tile * tile * width, bytes_accessed=8 * 2**20, transcendentals=0
         ),
-    )(tile_count, tile_pos, place, adj_tiles, list(banks), piece)
-    grad_bias = piece[:2, hid:].reshape(hid)
-    both = spread(piece[:, :hid].astype(bf16), PLANE).astype(f32).reshape(2 * width, hid)
+    )(tile_count, tile_pos, place, adj_tiles, list(banks), copies)
     return new_part[None], hidden, both[:width], both[width:], grad_bias
 
 

time: 154 us -> 153 us (level)
  waiting for transfers between devices: 9.6 us -> 13.8 us
  local copies, waits for them, and re-layouts: 5.26 us -> 2.05 us
    ppermute x1, waiting for transfers between devices: 2 us -> 4.6 us  [body(): lax.ppermute(side_high, LINE, up)]
    unnamed x24 -> x26, local copies, waits for them, and re-layouts: 1.73 us -> 0.06 us
  transfers between devices with their start and end apart: 8 -> 8, of which waited for: 4 -> 4; matrix products, arithmetic and copies ran while one was open for 1% -> 0% of each run, Pallas kernels for 3% -> 3%
where the time goes in v7:
time: 153 us; the launch traced here: 152 us
  blocking collectives  86.7 us (57%)
  starting transfers between devices  42.3 us (28%)
  waiting for transfers between devices  13.8 us (9%)
  Pallas kernels  5.92 us (4%)
  local copies, waits for them, and re-layouts  2.05 us (1%)
  between operations  1.56 us (1%)
    all_gather x1, blocking collectives, body(): same = lax.all_gather(node_feats, EVERY_OTHER)  45.3 us
    all_gather x1, blocking collectives, body(): lax.all_gather(jnp.sum(piece, axis=0).astype(bf16), EVERY_OTHER).astype(f32)  24.6 us
    all_to_all x1, blocking collectives, body(): piece = lax.all_to_all(grads, PLANE, 0, 0, tiled=True).astype(f32)  16.7 us
    all_to_all x1, starting transfers between devices, body(): stale = lax.all_to_all(stale_part[0], GRP, 0, 0, tiled=True)  13.3 us
    all_to_all x1, starting transfers between devices, body(): lax.all_to_all(copies, PLANE, 0, 0, tiled=True).astype(f32)  11.7 us
    ppermute x1, starting transfers between devices, body(): lax.ppermute(low, 'x_hi', swap)  4.61 us
    ppermute x1, waiting for transfers between devices, body(): lax.ppermute(side_high, LINE, up)  4.6 us
    ppermute x1, starting transfers between devices, body(): lax.ppermute(side_low, LINE, down)  3.94 us
  transfers between devices with their start and end apart: 8, of which 4 were waited for; matrix products, arithmetic and copies ran while one was open for 0% of the time, Pallas kernels for 3%

profile of v7, /device:TPU:1, one launch (start us, length us, event | category | flops | bytes accessed | tf_op | source)
XLA Modules:
  0.0 152.4 jit_solution(4847302616021045857)
XLA Ops:
  0.7 0.0 copy-start.10
  0.7 45.3 %all-gather = bf16[2048,128]{1,0:T(8,128)(2,1)S(1)} all-gather(bf16[128,128]{1,0:T(8,128)(2,1)} %feats_ref.3), channel_id=2, replica_groups=mesh['y'=4,'x_lo'=2,'core'=2,'x_hi'=2,'z_far'=8,'z_mid'=2,'z_near'=2] {'..., dimensions={0}, use_global_device_ids=true | all-gather | bytes 557056 | tf_op jit(solution)/shard_map/all_gather | solution.py:206
  46.1 4.6 %collective-permute-start.1 = (bf16[8,128,128]{2,1,0:T(8,128)(2,1)S(1)}, bf16[8,128,128]{2,1,0:T(8,128)(2,1)S(1)}, u32[]{:S(2)}, u32[]{:S(2)}) collective-permute-start(bf16[8,128,128]{2,1,0:T(8,128)(2,1)S(1)} %bitcast.23), channel_id=1, source_target_pairs={{0,32},{32,0},{1,33},{33,1},{2,34},{34,2},{3,35},{35,3},{4,36},{36... | collective-permute-start | bytes 786440 | tf_op jit(solution)/shard_map/ppermute | solution.py:213
  50.7 2.2 %collective-permute-start.2 = (bf16[8,128,128]{2,1,0:T(8,128)(2,1)S(1)}, bf16[8,128,128]{2,1,0:T(8,128)(2,1)S(1)}, u32[]{:S(2)}, u32[]{:S(2)}) collective-permute-start(bf16[8,128,128]{2,1,0:T(8,128)(2,1)S(1)} %bitcast.22), channel_id=1, source_target_pairs={{0,32},{32,0},{1,33},{33,1},{2,34},{34,2},{3,35},{35,3},{4,36},{36... | collective-permute-start | bytes 786440 | tf_op jit(solution)/shard_map/ppermute | solution.py:213
  52.9 2.6 %collective-permute-start = (bf16[16,128,128]{2,1,0:T(8,128)(2,1)S(1)}, bf16[16,128,128]{2,1,0:T(8,128)(2,1)S(1)}, u32[]{:S(2)}, u32[]{:S(2)}) collective-permute-start(bf16[16,128,128]{2,1,0:T(8,128)(2,1)S(1)} %bitcast.16), channel_id=1, source_target_pairs={{0,1},{1,2},{2,3},{3,4},{4,5},{5,6},{6,7},{7,8},{8,9},{9,10},{10,1... | collective-permute-start | bytes 1572872 | tf_op jit(solution)/shard_map/ppermute | solution.py:214
  55.5 13.3 %all-to-all-start = ((bf16[16,128,128]{2,1,0:T(8,128)(2,1)}), bf16[16,128,128]{2,1,0:T(8,128)(2,1)S(1)}, u32[]{:S(2)}, u32[]{:S(2)}) async-start(bf16[16,128,128]{2,1,0:T(8,128)(2,1)} %bitcast.20), calls=%async_computation | async-start | bytes 1048576 | tf_op jit(solution)/shard_map/all_to_all | solution.py:205
  68.9 0.0 collective-permute-done.1.bank_refs_2_
  68.9 3.9 %collective-permute-start.3 = (bf16[8,128,128]{2,1,0:T(8,128)(2,1)S(1)}, bf16[8,128,128]{2,1,0:T(8,128)(2,1)S(1)}, u32[]{:S(2)}, u32[]{:S(2)}) collective-permute-start(bf16[8,128,128]{2,1,0:T(8,128)(2,1)S(1)} %collective-permute-done.1.bank_refs_2_), channel_id=1, source_target_pairs={{0,31},{1,0},{2,1},{3,2},{4,3},{5,4},{6,5},{7,6},{8,7},{9,8},{10,9... | collective-permute-start | bytes 786440 | tf_op jit(solution)/shard_map/ppermute | solution.py:220
  72.8 1.9 %collective-permute-start.4 = (bf16[8,128,128]{2,1,0:T(8,128)(2,1)S(1)}, bf16[8,128,128]{2,1,0:T(8,128)(2,1)S(1)}, u32[]{:S(2)}, u32[]{:S(2)}) collective-permute-start(bf16[8,128,128]{2,1,0:T(8,128)(2,1)S(1)} %collective-permute-done.2.bank_refs_3_), channel_id=1, source_target_pairs={{0,1},{1,2},{2,3},{3,4},{4,5},{5,6},{6,7},{7,8},{8,9},{9,10},{10,1... | collective-permute-start | bytes 786440 | tf_op jit(solution)/shard_map/ppermute | solution.py:221
  75.4 0.0 copy-start.11
  75.5 3.2 %all-to-all-done.stale_ref = bf16[16,128,128]{2,1,0:T(8,128)(2,1)S(1)} async-done(((bf16[16,128,128]{2,1,0:T(8,128)(2,1)}), bf16[16,128,128]{2,1,0:T(8,128)(2,1)S(1)}, u32[]{:S(2)}, u32[]{:S(2)}) %all-to-all-start) | async-done | bytes 524320 | tf_op jit(solution)/shard_map/all_to_all | solution.py:205
  78.7 0.2 shard_map.128
  78.9 4.6 %collective-permute-done.4.bank_refs_5_ = bf16[8,128,128]{2,1,0:T(8,128)(2,1)S(1)} collective-permute-done((bf16[8,128,128]{2,1,0:T(8,128)(2,1)S(1)}, bf16[8,128,128]{2,1,0:T(8,128)(2,1)S(1)}, u32[]{:S(2)}, u32[]{:S(2)}) %collective-permute-start.4) | collective-permute-done | bytes 262176 | tf_op jit(solution)/shard_map/ppermute | solution.py:221
  83.5 1.9 %shard_map.129 = (bf16[128,256]{1,0:T(8,128)(2,1)}, bf16[32,8,384]{2,1,0:T(8,128)(2,1)S(1)}) custom-call(s32[1]{0:T(128)S(6)} %copy.14.count_ref, s32[16]{0:T(128)S(1)} %copy-done.10, s32[64]{0:T(128)S(1)} %fusion.place_ref, s32[1]{0:T(128)} %bitcast.3.own_ref, bf16[16,256,256]{2,1,0:T(8,128)(2,1)} %adj_ref.3, bf16[16,128,128]{2,1,0:T(8,128)(2,1)S(1)} %bitcast.17, ...), custom_call_target="tpu_custom_call" | custom-call | flops 33554432 | bytes 1048576 | tf_op jit(solution)/shard_map/pallas_call | solution.py:257
  85.5 16.7 %all_to_all.15 = bf16[32,8,384]{2,1,0:T(8,128)(2,1)S(1)} all-to-all(bf16[32,8,384]{2,1,0:T(8,128)(2,1)S(1)} %get-tuple-element.15), channel_id=1, replica_groups=mesh['y'=4,'x_lo'=2,'core'=2,'x_hi'=2,'z_far'=8,'z_mid'=2,'z_near'=2] {'..., dimensions={0} | all-to-all | bytes 393216 | tf_op jit(solution)/shard_map/all_to_all | solution.py:290
  102.3 24.6 %all-gather.1 = bf16[128,384]{1,0:T(8,128)(2,1)S(1)} all-gather(bf16[8,384]{1,0:T(8,128)(2,1)S(1)} %reduce_sum.21), channel_id=3, replica_groups=mesh['y'=4,'x_lo'=2,'core'=2,'x_hi'=2,'z_far'=8,'z_mid'=2,'z_near'=2] {'..., dimensions={0}, use_global_device_ids=true | all-gather | bytes 104448 | tf_op jit(solution)/shard_map/all_gather | solution.py:291
  126.9 1.9 %collective-permute-start.5 = (f32[8,384]{1,0:T(8,128)S(1)}, f32[8,384]{1,0:T(8,128)S(1)}, u32[]{:S(2)}, u32[]{:S(2)}) collective-permute-start(f32[8,384]{1,0:T(8,128)S(1)} %convert_reduce_fusion), channel_id=1, source_target_pairs={{0,1},{1,0},{2,3},{3,2},{4,5},{5,4},{6,7},{7,6},{8,9},{9,8},{10,11... | collective-permute-start | bytes 36872 | tf_op jit(solution)/shard_map/ppermute | solution.py:293
  128.8 2.8 %collective-permute-done.5 = f32[8,384]{1,0:T(8,128)S(1)} collective-permute-done((f32[8,384]{1,0:T(8,128)S(1)}, f32[8,384]{1,0:T(8,128)S(1)}, u32[]{:S(2)}, u32[]{:S(2)}) %collective-permute-start.5) | collective-permute-done | bytes 12320 | tf_op jit(solution)/shard_map/ppermute | solution.py:293
  131.7 0.7 broadcast_in_dim.13._
  132.3 11.7 %all-to-all-start.2 = ((bf16[32,8,256]{2,1,0:T(8,128)(2,1)}), bf16[32,8,256]{2,1,0:T(8,128)(2,1)S(1)}, u32[]{:S(2)}, u32[]{:S(2)}) async-start(bf16[32,8,256]{2,1,0:T(8,128)(2,1)} %broadcast_in_dim.13._), calls=%async_computation.2 | async-start | bytes 262144 | tf_op jit(solution)/shard_map/all_to_all | solution.py:296
  144.1 3.8 %shard_map.130 = bf16[16,128,128]{2,1,0:T(8,128)(2,1)} custom-call(s32[1]{0:T(128)S(6)} %copy.14.count_ref, s32[16]{0:T(128)} %pos_ref.3, s32[64]{0:T(128)} %copy-done.11, bf16[16,256,256]{2,1,0:T(8,128)(2,1)} %adj_ref.3, bf16[16,128,128]{2,1,0:T(8,128)(2,1)} %bitcast.18, bf16[16,128,128]{2,1,0:T(8,128)(2,1)} %copy-done.1, bf16[8,128,128]{2,1,0:T(8,128)(2,1)} %copy-done.2, ...), custom_call_target="tpu_custom_call" | custom-call | flops 268435456 | bytes 8388608 | tf_op jit(solution)/shard_map/pallas_call | solution.py:297
  147.9 0.6 slice_bitcast_fusion.2
  148.5 3.2 %all-to-all-done.2 = bf16[32,8,256]{2,1,0:T(8,128)(2,1)S(1)} async-done(((bf16[32,8,256]{2,1,0:T(8,128)(2,1)}), bf16[32,8,256]{2,1,0:T(8,128)(2,1)S(1)}, u32[]{:S(2)}, u32[]{:S(2)}) %all-to-all-start.2) | async-done | bytes 131104 | tf_op jit(solution)/shard_map/all_to_all | solution.py:296
  151.7 0.7 slice_bitcast_fusion
  (34 shorter events, 0.2 us)
Async XLA Ops:
  0.6 78.0 %copy-start.6 = (bf16[128,128]{1,0:T(8,128)(2,1)S(1)}, bf16[128,128]{1,0:T(8,128)(2,1)}, u32[]{:S(2)}) copy-start(bf16[128,128]{1,0:T(8,128)(2,1)} %feats_ref.3) | copy-start | bytes 98308
  0.6 78.0 %copy-start.9 = (bf16[128,256]{1,0:T(8,128)(2,1)S(1)}, bf16[128,256]{1,0:T(8,128)(2,1)}, u32[]{:S(2)}) copy-start(bf16[128,256]{1,0:T(8,128)(2,1)} %cot_ref.1) | copy-start | bytes 196612
  0.7 78.0 %copy-start.8 = (bf16[128,256]{1,0:T(8,128)(2,1)S(1)}, bf16[128,256]{1,0:T(8,128)(2,1)}, u32[]{:S(2)}) copy-start(bf16[128,256]{1,0:T(8,128)(2,1)} %w_neigh_ref.1) | copy-start | bytes 196612
  0.7 78.0 %copy-start.7 = (bf16[128,256]{1,0:T(8,128)(2,1)S(1)}, bf16[128,256]{1,0:T(8,128)(2,1)}, u32[]{:S(2)}) copy-start(bf16[128,256]{1,0:T(8,128)(2,1)} %w_self_ref.1) | copy-start | bytes 196612
  0.7 82.8 %copy-start.10 = (s32[16]{0:T(128)S(1)}, s32[16]{0:T(128)}, u32[]{:S(2)}) copy-start(s32[16]{0:T(128)} %pos_ref.3) | copy-start | bytes 196
  0.7 82.8 %copy-start.12 = (f32[256]{0:T(256)S(1)}, f32[256]{0:T(256)}, u32[]{:S(2)}) copy-start(f32[256]{0:T(256)} %param.16) | copy-start | bytes 3076
  46.0 39.4 %copy-start = (bf16[2048,128]{1,0:T(8,128)(2,1)}, bf16[2048,128]{1,0:T(8,128)(2,1)S(1)}, u32[]{:S(2)}) copy-start(bf16[2048,128]{1,0:T(8,128)(2,1)S(1)} %all-gather) | copy-start | bytes 1572868
  46.1 22.8 %collective-permute-start.1 = (bf16[8,128,128]{2,1,0:T(8,128)(2,1)S(1)}, bf16[8,128,128]{2,1,0:T(8,128)(2,1)S(1)}, u32[]{:S(2)}, u32[]{:S(2)}) collective-permute-start(bf16[8,128,128]{2,1,0:T(8,128)(2,1)S(1)} %bitcast.23), channel_id=1, source_target_pairs={{0,32},{32,0},{1,33},{33,1},{2,34},{34,2},{3,35},{35,3},{4,36},{36... | collective-permute-start | bytes 786440 | tf_op jit(solution)/shard_map/ppermute | solution.py:213
  50.7 22.1 %collective-permute-start.2 = (bf16[8,128,128]{2,1,0:T(8,128)(2,1)S(1)}, bf16[8,128,128]{2,1,0:T(8,128)(2,1)S(1)}, u32[]{:S(2)}, u32[]{:S(2)}) collective-permute-start(bf16[8,128,128]{2,1,0:T(8,128)(2,1)S(1)} %bitcast.22), channel_id=1, source_target_pairs={{0,32},{32,0},{1,33},{33,1},{2,34},{34,2},{3,35},{35,3},{4,36},{36... | collective-permute-start | bytes 786440 | tf_op jit(solution)/shard_map/ppermute | solution.py:213
  52.9 30.6 %collective-permute-start = (bf16[16,128,128]{2,1,0:T(8,128)(2,1)S(1)}, bf16[16,128,128]{2,1,0:T(8,128)(2,1)S(1)}, u32[]{:S(2)}, u32[]{:S(2)}) collective-permute-start(bf16[16,128,128]{2,1,0:T(8,128)(2,1)S(1)} %bitcast.16), channel_id=1, source_target_pairs={{0,1},{1,2},{2,3},{3,4},{4,5},{5,6},{6,7},{7,8},{8,9},{9,10},{10,1... | collective-permute-start | bytes 1572872 | tf_op jit(solution)/shard_map/ppermute | solution.py:214
  55.5 23.1 %all-to-all-start = ((bf16[16,128,128]{2,1,0:T(8,128)(2,1)}), bf16[16,128,128]{2,1,0:T(8,128)(2,1)S(1)}, u32[]{:S(2)}, u32[]{:S(2)}) async-start(bf16[16,128,128]{2,1,0:T(8,128)(2,1)} %bitcast.20), calls=%async_computation | async-start | bytes 1048576 | tf_op jit(solution)/shard_map/all_to_all | solution.py:205
  68.9 16.6 %copy-start.2 = (bf16[8,128,128]{2,1,0:T(8,128)(2,1)}, bf16[8,128,128]{2,1,0:T(8,128)(2,1)S(1)}, u32[]{:S(2)}) copy-start(bf16[8,128,128]{2,1,0:T(8,128)(2,1)S(1)} %collective-permute-done.1.bank_refs_2_) | copy-start | bytes 786436
  68.9 10.0 %collective-permute-start.3 = (bf16[8,128,128]{2,1,0:T(8,128)(2,1)S(1)}, bf16[8,128,128]{2,1,0:T(8,128)(2,1)S(1)}, u32[]{:S(2)}, u32[]{:S(2)}) collective-permute-start(bf16[8,128,128]{2,1,0:T(8,128)(2,1)S(1)} %collective-permute-done.1.bank_refs_2_), channel_id=1, source_target_pairs={{0,31},{1,0},{2,1},{3,2},{4,3},{5,4},{6,5},{7,6},{8,7},{9,8},{10,9... | collective-permute-start | bytes 786440 | tf_op jit(solution)/shard_map/ppermute | solution.py:220
  72.8 12.6 %copy-start.3 = (bf16[8,128,128]{2,1,0:T(8,128)(2,1)}, bf16[8,128,128]{2,1,0:T(8,128)(2,1)S(1)}, u32[]{:S(2)}) copy-start(bf16[8,128,128]{2,1,0:T(8,128)(2,1)S(1)} %collective-permute-done.2.bank_refs_3_) | copy-start | bytes 786436
  72.8 10.6 %collective-permute-start.4 = (bf16[8,128,128]{2,1,0:T(8,128)(2,1)S(1)}, bf16[8,128,128]{2,1,0:T(8,128)(2,1)S(1)}, u32[]{:S(2)}, u32[]{:S(2)}) collective-permute-start(bf16[8,128,128]{2,1,0:T(8,128)(2,1)S(1)} %collective-permute-done.2.bank_refs_3_), channel_id=1, source_target_pairs={{0,1},{1,2},{2,3},{3,4},{4,5},{5,6},{6,7},{7,8},{8,9},{9,10},{10,1... | collective-permute-start | bytes 786440 | tf_op jit(solution)/shard_map/ppermute | solution.py:221
  75.4 10.0 %copy-start.11 = (s32[64]{0:T(128)}, s32[64]{0:T(128)S(1)}, u32[]{:S(2)}) copy-start(s32[64]{0:T(128)S(1)} %fusion.place_ref) | copy-start | bytes 772
  78.9 6.6 %copy-start.4 = (bf16[8,128,128]{2,1,0:T(8,128)(2,1)}, bf16[8,128,128]{2,1,0:T(8,128)(2,1)S(1)}, u32[]{:S(2)}) copy-start(bf16[8,128,128]{2,1,0:T(8,128)(2,1)S(1)} %collective-permute-done.3.bank_refs_4_) | copy-start | bytes 786436
  83.5 2.0 %copy-start.5 = (bf16[8,128,128]{2,1,0:T(8,128)(2,1)}, bf16[8,128,128]{2,1,0:T(8,128)(2,1)S(1)}, u32[]{:S(2)}) copy-start(bf16[8,128,128]{2,1,0:T(8,128)(2,1)S(1)} %collective-permute-done.4.bank_refs_5_) | copy-start | bytes 786436
  83.5 2.0 %copy-start.1 = (bf16[16,128,128]{2,1,0:T(8,128)(2,1)}, bf16[16,128,128]{2,1,0:T(8,128)(2,1)S(1)}, u32[]{:S(2)}) copy-start(bf16[16,128,128]{2,1,0:T(8,128)(2,1)S(1)} %collective-permute-done.bank_refs_1_) | copy-start | bytes 1572868
  126.9 4.7 %collective-permute-start.5 = (f32[8,384]{1,0:T(8,128)S(1)}, f32[8,384]{1,0:T(8,128)S(1)}, u32[]{:S(2)}, u32[]{:S(2)}) collective-permute-start(f32[8,384]{1,0:T(8,128)S(1)} %convert_reduce_fusion), channel_id=1, source_target_pairs={{0,1},{1,0},{2,3},{3,2},{4,5},{5,4},{6,7},{7,6},{8,9},{9,8},{10,11... | collective-permute-start | bytes 36872 | tf_op jit(solution)/shard_map/ppermute | solution.py:293
  132.3 19.3 %all-to-all-start.2 = ((bf16[32,8,256]{2,1,0:T(8,128)(2,1)}), bf16[32,8,256]{2,1,0:T(8,128)(2,1)S(1)}, u32[]{:S(2)}, u32[]{:S(2)}) async-start(bf16[32,8,256]{2,1,0:T(8,128)(2,1)} %broadcast_in_dim.13._), calls=%async_computation.2 | async-start | bytes 262144 | tf_op jit(solution)/shard_map/all_to_all | solution.py:296

commit v8 on v7

--- a/solution.py
+++ b/solution.py
@@ -289,11 +289,13 @@
     scaling = float(node_dev * groups * blocks) ** (-0.5)
     piece = lax.all_to_all(grads, PLANE, 0, 0, tiled=True).astype(f32)
     piece = lax.all_gather(jnp.sum(piece, axis=0).astype(bf16), EVERY_OTHER).astype(f32)
-    piece = jnp.sum(piece, axis=0)
-    piece = (piece + lax.ppermute(piece, "z_near", swap)) * scaling
-    grad_bias = piece[:2, hid:].reshape(hid)
-    copies = jnp.broadcast_to(piece[None, :, :hid].astype(bf16), (plane, piece_rows, hid))
-    both = lax.all_to_all(copies, PLANE, 0, 0, tiled=True).astype(f32).reshape(2 * width, hid)
+    piece = (jnp.sum(piece, axis=0) * scaling).astype(bf16)
+    pair = plane * lax.axis_size("z_near")
+    copies = jnp.broadcast_to(piece[None], (pair,) + piece.shape)
+    both = lax.all_to_all(copies, PLANE + ("z_near",), 0, 0, tiled=True).astype(f32)
+    both = jnp.sum(both.reshape((plane, 2) + piece.shape), axis=1)
+    grad_bias = both[0, :2, hid:].reshape(hid)
+    both = both[:, :, :hid].reshape(2 * width, hid)
     new_part = pl.pallas_call(
         partial_kernel,
         out_shape=jax.ShapeDtypeStruct((groups, node_dev, width), bf16),

time: 153 us -> 152 us (level)
  starting transfers between devices: 42.3 us -> 40.5 us
    all_to_all x1, waiting for transfers between devices: 3.15 us -> 7.53 us  [body(): lax.all_to_all(copies, PLANE + ('z_near',), 0, 0, tiled=True).astype(f32)]
    ppermute x1 -> x0, waiting for transfers between devices: 2.81 us -> none  [body(): piece = (piece + lax.ppermute(piece, 'z_near', swap)) * scaling]
    ppermute x1 -> x0, starting transfers between devices: 1.92 us -> none  [body(): piece = (piece + lax.ppermute(piece, 'z_near', swap)) * scaling]
  transfers between devices with their start and end apart: 8 -> 7, of which waited for: 4 -> 3; matrix products, arithmetic and copies ran while one was open for 0% -> 0% of each run, Pallas kernels for 3% -> 2%
where the time goes in v8:
time: 152 us
  blocking collectives  85.3 us (56%)
  starting transfers between devices  40.5 us (27%)
  waiting for transfers between devices  15.3 us (10%)
  Pallas kernels  6.6 us (4%)
  local copies, waits for them, and re-layouts  2.17 us (1%)
  between operations  1.56 us (1%)
    all_gather x1, blocking collectives, body(): same = lax.all_gather(node_feats, EVERY_OTHER)  45.3 us
    all_gather x1, blocking collectives, body(): lax.all_gather(jnp.sum(piece, axis=0).astype(bf16), EVERY_OTHER).astype(f32)  24 us
    all_to_all x1, blocking collectives, body(): piece = lax.all_to_all(grads, PLANE, 0, 0, tiled=True).astype(f32)  16 us
    all_to_all x1, starting transfers between devices, body(): stale = lax.all_to_all(stale_part[0], GRP, 0, 0, tiled=True)  13.3 us
    all_to_all x1, starting transfers between devices, body(): lax.all_to_all(copies, PLANE + ('z_near',), 0, 0, tiled=True).astype(f32)  11.9 us
    all_to_all x1, waiting for transfers between devices, body(): lax.all_to_all(copies, PLANE + ('z_near',), 0, 0, tiled=True).astype(f32)  7.53 us
    ppermute x1, starting transfers between devices, body(): lax.ppermute(low, 'x_hi', swap)  4.61 us
    ppermute x1, waiting for transfers between devices, body(): lax.ppermute(side_high, LINE, up)  4.6 us
  transfers between devices with their start and end apart: 7, of which 3 were waited for; matrix products, arithmetic and copies ran while one was open for 0% of the time, Pallas kernels for 2%

profile of v8, /device:TPU:1, one launch (start us, length us, event | category | flops | bytes accessed | tf_op | source)
XLA Modules:
  0.0 151.6 jit_solution(11119976575455272067)
XLA Ops:
  0.7 0.0 copy-start.10
  0.7 45.3 %all-gather = bf16[2048,128]{1,0:T(8,128)(2,1)S(1)} all-gather(bf16[128,128]{1,0:T(8,128)(2,1)} %feats_ref.3), channel_id=2, replica_groups=mesh['y'=4,'x_lo'=2,'core'=2,'x_hi'=2,'z_far'=8,'z_mid'=2,'z_near'=2] {'..., dimensions={0}, use_global_device_ids=true | all-gather | bytes 557056 | tf_op jit(solution)/shard_map/all_gather | solution.py:206
  46.1 4.6 %collective-permute-start.1 = (bf16[8,128,128]{2,1,0:T(8,128)(2,1)S(1)}, bf16[8,128,128]{2,1,0:T(8,128)(2,1)S(1)}, u32[]{:S(2)}, u32[]{:S(2)}) collective-permute-start(bf16[8,128,128]{2,1,0:T(8,128)(2,1)S(1)} %bitcast.26), channel_id=1, source_target_pairs={{0,32},{32,0},{1,33},{33,1},{2,34},{34,2},{3,35},{35,3},{4,36},{36... | collective-permute-start | bytes 786440 | tf_op jit(solution)/shard_map/ppermute | solution.py:213
  50.7 2.2 %collective-permute-start.2 = (bf16[8,128,128]{2,1,0:T(8,128)(2,1)S(1)}, bf16[8,128,128]{2,1,0:T(8,128)(2,1)S(1)}, u32[]{:S(2)}, u32[]{:S(2)}) collective-permute-start(bf16[8,128,128]{2,1,0:T(8,128)(2,1)S(1)} %bitcast.25), channel_id=1, source_target_pairs={{0,32},{32,0},{1,33},{33,1},{2,34},{34,2},{3,35},{35,3},{4,36},{36... | collective-permute-start | bytes 786440 | tf_op jit(solution)/shard_map/ppermute | solution.py:213
  52.9 2.6 %collective-permute-start = (bf16[16,128,128]{2,1,0:T(8,128)(2,1)S(1)}, bf16[16,128,128]{2,1,0:T(8,128)(2,1)S(1)}, u32[]{:S(2)}, u32[]{:S(2)}) collective-permute-start(bf16[16,128,128]{2,1,0:T(8,128)(2,1)S(1)} %bitcast.19), channel_id=1, source_target_pairs={{0,1},{1,2},{2,3},{3,4},{4,5},{5,6},{6,7},{7,8},{8,9},{9,10},{10,1... | collective-permute-start | bytes 1572872 | tf_op jit(solution)/shard_map/ppermute | solution.py:214
  55.5 13.3 %all-to-all-start = ((bf16[16,128,128]{2,1,0:T(8,128)(2,1)}), bf16[16,128,128]{2,1,0:T(8,128)(2,1)S(1)}, u32[]{:S(2)}, u32[]{:S(2)}) async-start(bf16[16,128,128]{2,1,0:T(8,128)(2,1)} %bitcast.24), calls=%async_computation | async-start | bytes 1048576 | tf_op jit(solution)/shard_map/all_to_all | solution.py:205
  68.9 0.0 collective-permute-done.1.bank_refs_2_
  68.9 3.9 %collective-permute-start.3 = (bf16[8,128,128]{2,1,0:T(8,128)(2,1)S(1)}, bf16[8,128,128]{2,1,0:T(8,128)(2,1)S(1)}, u32[]{:S(2)}, u32[]{:S(2)}) collective-permute-start(bf16[8,128,128]{2,1,0:T(8,128)(2,1)S(1)} %collective-permute-done.1.bank_refs_2_), channel_id=1, source_target_pairs={{0,31},{1,0},{2,1},{3,2},{4,3},{5,4},{6,5},{7,6},{8,7},{9,8},{10,9... | collective-permute-start | bytes 786440 | tf_op jit(solution)/shard_map/ppermute | solution.py:220
  72.8 1.9 %collective-permute-start.4 = (bf16[8,128,128]{2,1,0:T(8,128)(2,1)S(1)}, bf16[8,128,128]{2,1,0:T(8,128)(2,1)S(1)}, u32[]{:S(2)}, u32[]{:S(2)}) collective-permute-start(bf16[8,128,128]{2,1,0:T(8,128)(2,1)S(1)} %collective-permute-done.2.bank_refs_3_), channel_id=1, source_target_pairs={{0,1},{1,2},{2,3},{3,4},{4,5},{5,6},{6,7},{7,8},{8,9},{9,10},{10,1... | collective-permute-start | bytes 786440 | tf_op jit(solution)/shard_map/ppermute | solution.py:221
  75.4 0.0 copy-start.11
  75.5 3.2 %all-to-all-done.stale_ref = bf16[16,128,128]{2,1,0:T(8,128)(2,1)S(1)} async-done(((bf16[16,128,128]{2,1,0:T(8,128)(2,1)}), bf16[16,128,128]{2,1,0:T(8,128)(2,1)S(1)}, u32[]{:S(2)}, u32[]{:S(2)}) %all-to-all-start) | async-done | bytes 524320 | tf_op jit(solution)/shard_map/all_to_all | solution.py:205
  78.7 0.2 shard_map.128
  78.9 0.0 collective-permute-done.3.bank_refs_4_
  78.9 4.6 %collective-permute-done.4.bank_refs_5_ = bf16[8,128,128]{2,1,0:T(8,128)(2,1)S(1)} collective-permute-done((bf16[8,128,128]{2,1,0:T(8,128)(2,1)S(1)}, bf16[8,128,128]{2,1,0:T(8,128)(2,1)S(1)}, u32[]{:S(2)}, u32[]{:S(2)}) %collective-permute-start.4) | collective-permute-done | bytes 262176 | tf_op jit(solution)/shard_map/ppermute | solution.py:221
  83.5 2.8 %shard_map.129 = (bf16[128,256]{1,0:T(8,128)(2,1)}, bf16[32,8,384]{2,1,0:T(8,128)(2,1)S(1)}) custom-call(s32[1]{0:T(128)S(6)} %copy.14.count_ref, s32[16]{0:T(128)S(1)} %copy-done.10, s32[64]{0:T(128)S(1)} %fusion.place_ref, s32[1]{0:T(128)} %bitcast.3.own_ref, bf16[16,256,256]{2,1,0:T(8,128)(2,1)} %adj_ref.3, bf16[16,128,128]{2,1,0:T(8,128)(2,1)S(1)} %bitcast.20, ...), custom_call_target="tpu_custom_call" | custom-call | flops 33554432 | bytes 1048576 | tf_op jit(solution)/shard_map/pallas_call | solution.py:257
  86.4 16.0 %all_to_all.15 = bf16[32,8,384]{2,1,0:T(8,128)(2,1)S(1)} all-to-all(bf16[32,8,384]{2,1,0:T(8,128)(2,1)S(1)} %get-tuple-element.15), channel_id=1, replica_groups=mesh['y'=4,'x_lo'=2,'core'=2,'x_hi'=2,'z_far'=8,'z_mid'=2,'z_near'=2] {'..., dimensions={0} | all-to-all | bytes 393216 | tf_op jit(solution)/shard_map/all_to_all | solution.py:290
  102.4 24.0 %all-gather.1 = bf16[128,384]{1,0:T(8,128)(2,1)S(1)} all-gather(bf16[8,384]{1,0:T(8,128)(2,1)S(1)} %reduce_sum.30), channel_id=3, replica_groups=mesh['y'=4,'x_lo'=2,'core'=2,'x_hi'=2,'z_far'=8,'z_mid'=2,'z_near'=2] {'..., dimensions={0}, use_global_device_ids=true | all-gather | bytes 104448 | tf_op jit(solution)/shard_map/all_gather | solution.py:291
  126.5 0.8 broadcast_in_dim.13._
  127.3 11.9 %all-to-all-start.2 = ((bf16[64,8,384]{2,1,0:T(8,128)(2,1)}), bf16[64,8,384]{2,1,0:T(8,128)(2,1)S(1)}, u32[]{:S(2)}, u32[]{:S(2)}) async-start(bf16[64,8,384]{2,1,0:T(8,128)(2,1)} %broadcast_in_dim.13._), calls=%async_computation.2 | async-start | bytes 786432 | tf_op jit(solution)/shard_map/all_to_all | solution.py:295
  139.2 3.6 %shard_map.130 = bf16[16,128,128]{2,1,0:T(8,128)(2,1)} custom-call(s32[1]{0:T(128)S(6)} %copy.14.count_ref, s32[16]{0:T(128)} %pos_ref.3, s32[64]{0:T(128)} %copy-done.11, bf16[16,256,256]{2,1,0:T(8,128)(2,1)} %adj_ref.3, bf16[16,128,128]{2,1,0:T(8,128)(2,1)} %bitcast.21, bf16[16,128,128]{2,1,0:T(8,128)(2,1)} %copy-done.1, bf16[8,128,128]{2,1,0:T(8,128)(2,1)} %copy-done.2, ...), custom_call_target="tpu_custom_call" | custom-call | flops 268435456 | bytes 8388608 | tf_op jit(solution)/shard_map/pallas_call | solution.py:299
  142.8 7.5 %all-to-all-done.2 = bf16[64,8,384]{2,1,0:T(8,128)(2,1)S(1)} async-done(((bf16[64,8,384]{2,1,0:T(8,128)(2,1)}), bf16[64,8,384]{2,1,0:T(8,128)(2,1)S(1)}, u32[]{:S(2)}, u32[]{:S(2)}) %all-to-all-start.2) | async-done | bytes 393248 | tf_op jit(solution)/shard_map/all_to_all | solution.py:295
  150.3 0.1 convert_reduce_fusion
  150.4 0.6 slice_bitcast_fusion.2
  150.9 0.7 slice_bitcast_fusion
  (31 shorter events, 0.2 us)
Async XLA Ops:
  0.6 78.0 %copy-start.6 = (bf16[128,128]{1,0:T(8,128)(2,1)S(1)}, bf16[128,128]{1,0:T(8,128)(2,1)}, u32[]{:S(2)}) copy-start(bf16[128,128]{1,0:T(8,128)(2,1)} %feats_ref.3) | copy-start | bytes 98308
  0.6 78.0 %copy-start.9 = (bf16[128,256]{1,0:T(8,128)(2,1)S(1)}, bf16[128,256]{1,0:T(8,128)(2,1)}, u32[]{:S(2)}) copy-start(bf16[128,256]{1,0:T(8,128)(2,1)} %cot_ref.1) | copy-start | bytes 196612
  0.7 78.0 %copy-start.8 = (bf16[128,256]{1,0:T(8,128)(2,1)S(1)}, bf16[128,256]{1,0:T(8,128)(2,1)}, u32[]{:S(2)}) copy-start(bf16[128,256]{1,0:T(8,128)(2,1)} %w_neigh_ref.1) | copy-start | bytes 196612
  0.7 78.0 %copy-start.7 = (bf16[128,256]{1,0:T(8,128)(2,1)S(1)}, bf16[128,256]{1,0:T(8,128)(2,1)}, u32[]{:S(2)}) copy-start(bf16[128,256]{1,0:T(8,128)(2,1)} %w_self_ref.1) | copy-start | bytes 196612
  0.7 82.8 %copy-start.10 = (s32[16]{0:T(128)S(1)}, s32[16]{0:T(128)}, u32[]{:S(2)}) copy-start(s32[16]{0:T(128)} %pos_ref.3) | copy-start | bytes 196
  0.7 82.8 %copy-start.12 = (f32[256]{0:T(256)S(1)}, f32[256]{0:T(256)}, u32[]{:S(2)}) copy-start(f32[256]{0:T(256)} %param.16) | copy-start | bytes 3076
  46.0 40.3 %copy-start = (bf16[2048,128]{1,0:T(8,128)(2,1)}, bf16[2048,128]{1,0:T(8,128)(2,1)S(1)}, u32[]{:S(2)}) copy-start(bf16[2048,128]{1,0:T(8,128)(2,1)S(1)} %all-gather) | copy-start | bytes 1572868
  46.1 22.8 %collective-permute-start.1 = (bf16[8,128,128]{2,1,0:T(8,128)(2,1)S(1)}, bf16[8,128,128]{2,1,0:T(8,128)(2,1)S(1)}, u32[]{:S(2)}, u32[]{:S(2)}) collective-permute-start(bf16[8,128,128]{2,1,0:T(8,128)(2,1)S(1)} %bitcast.26), channel_id=1, source_target_pairs={{0,32},{32,0},{1,33},{33,1},{2,34},{34,2},{3,35},{35,3},{4,36},{36... | collective-permute-start | bytes 786440 | tf_op jit(solution)/shard_map/ppermute | solution.py:213
  50.7 22.1 %collective-permute-start.2 = (bf16[8,128,128]{2,1,0:T(8,128)(2,1)S(1)}, bf16[8,128,128]{2,1,0:T(8,128)(2,1)S(1)}, u32[]{:S(2)}, u32[]{:S(2)}) collective-permute-start(bf16[8,128,128]{2,1,0:T(8,128)(2,1)S(1)} %bitcast.25), channel_id=1, source_target_pairs={{0,32},{32,0},{1,33},{33,1},{2,34},{34,2},{3,35},{35,3},{4,36},{36... | collective-permute-start | bytes 786440 | tf_op jit(solution)/shard_map/ppermute | solution.py:213
  52.9 30.6 %collective-permute-start = (bf16[16,128,128]{2,1,0:T(8,128)(2,1)S(1)}, bf16[16,128,128]{2,1,0:T(8,128)(2,1)S(1)}, u32[]{:S(2)}, u32[]{:S(2)}) collective-permute-start(bf16[16,128,128]{2,1,0:T(8,128)(2,1)S(1)} %bitcast.19), channel_id=1, source_target_pairs={{0,1},{1,2},{2,3},{3,4},{4,5},{5,6},{6,7},{7,8},{8,9},{9,10},{10,1... | collective-permute-start | bytes 1572872 | tf_op jit(solution)/shard_map/ppermute | solution.py:214
  55.5 23.1 %all-to-all-start = ((bf16[16,128,128]{2,1,0:T(8,128)(2,1)}), bf16[16,128,128]{2,1,0:T(8,128)(2,1)S(1)}, u32[]{:S(2)}, u32[]{:S(2)}) async-start(bf16[16,128,128]{2,1,0:T(8,128)(2,1)} %bitcast.24), calls=%async_computation | async-start | bytes 1048576 | tf_op jit(solution)/shard_map/all_to_all | solution.py:205
  68.9 17.5 %copy-start.2 = (bf16[8,128,128]{2,1,0:T(8,128)(2,1)}, bf16[8,128,128]{2,1,0:T(8,128)(2,1)S(1)}, u32[]{:S(2)}) copy-start(bf16[8,128,128]{2,1,0:T(8,128)(2,1)S(1)} %collective-permute-done.1.bank_refs_2_) | copy-start | bytes 786436
  68.9 10.0 %collective-permute-start.3 = (bf16[8,128,128]{2,1,0:T(8,128)(2,1)S(1)}, bf16[8,128,128]{2,1,0:T(8,128)(2,1)S(1)}, u32[]{:S(2)}, u32[]{:S(2)}) collective-permute-start(bf16[8,128,128]{2,1,0:T(8,128)(2,1)S(1)} %collective-permute-done.1.bank_refs_2_), channel_id=1, source_target_pairs={{0,31},{1,0},{2,1},{3,2},{4,3},{5,4},{6,5},{7,6},{8,7},{9,8},{10,9... | collective-permute-start | bytes 786440 | tf_op jit(solution)/shard_map/ppermute | solution.py:220
  72.8 13.5 %copy-start.3 = (bf16[8,128,128]{2,1,0:T(8,128)(2,1)}, bf16[8,128,128]{2,1,0:T(8,128)(2,1)S(1)}, u32[]{:S(2)}) copy-start(bf16[8,128,128]{2,1,0:T(8,128)(2,1)S(1)} %collective-permute-done.2.bank_refs_3_) | copy-start | bytes 786436
  72.8 10.6 %collective-permute-start.4 = (bf16[8,128,128]{2,1,0:T(8,128)(2,1)S(1)}, bf16[8,128,128]{2,1,0:T(8,128)(2,1)S(1)}, u32[]{:S(2)}, u32[]{:S(2)}) collective-permute-start(bf16[8,128,128]{2,1,0:T(8,128)(2,1)S(1)} %collective-permute-done.2.bank_refs_3_), channel_id=1, source_target_pairs={{0,1},{1,2},{2,3},{3,4},{4,5},{5,6},{6,7},{7,8},{8,9},{9,10},{10,1... | collective-permute-start | bytes 786440 | tf_op jit(solution)/shard_map/ppermute | solution.py:221
  75.4 10.9 %copy-start.11 = (s32[64]{0:T(128)}, s32[64]{0:T(128)S(1)}, u32[]{:S(2)}) copy-start(s32[64]{0:T(128)S(1)} %fusion.place_ref) | copy-start | bytes 772
  78.9 7.5 %copy-start.4 = (bf16[8,128,128]{2,1,0:T(8,128)(2,1)}, bf16[8,128,128]{2,1,0:T(8,128)(2,1)S(1)}, u32[]{:S(2)}) copy-start(bf16[8,128,128]{2,1,0:T(8,128)(2,1)S(1)} %collective-permute-done.3.bank_refs_4_) | copy-start | bytes 786436
  83.5 2.9 %copy-start.5 = (bf16[8,128,128]{2,1,0:T(8,128)(2,1)}, bf16[8,128,128]{2,1,0:T(8,128)(2,1)S(1)}, u32[]{:S(2)}) copy-start(bf16[8,128,128]{2,1,0:T(8,128)(2,1)S(1)} %collective-permute-done.4.bank_refs_5_) | copy-start | bytes 786436
  83.5 2.9 %copy-start.1 = (bf16[16,128,128]{2,1,0:T(8,128)(2,1)}, bf16[16,128,128]{2,1,0:T(8,128)(2,1)S(1)}, u32[]{:S(2)}) copy-start(bf16[16,128,128]{2,1,0:T(8,128)(2,1)S(1)} %collective-permute-done.bank_refs_1_) | copy-start | bytes 1572868
  127.3 23.0 %all-to-all-start.2 = ((bf16[64,8,384]{2,1,0:T(8,128)(2,1)}), bf16[64,8,384]{2,1,0:T(8,128)(2,1)S(1)}, u32[]{:S(2)}, u32[]{:S(2)}) async-start(bf16[64,8,384]{2,1,0:T(8,128)(2,1)} %broadcast_in_dim.13._), calls=%async_computation.2 | async-start | bytes 786432 | tf_op jit(solution)/shard_map/all_to_all | solution.py:295

commit v9 on v8

--- a/solution.py
+++ b/solution.py
@@ -193,6 +193,19 @@
     part_ref[...] = acc_ref[...].reshape(part_ref.shape).astype(part_ref.dtype)
 
 
+def finish_kernel(got_ref, self_ref, neigh_ref, bias_ref):
+    pairs, rows, _ = got_ref.shape
+    width, hid = self_ref.shape
+    got = got_ref[...].astype(jnp.float32).reshape(pairs // 2, 2, rows, got_ref.shape[2])
+    total = got[:, 0] + got[:, 1]
+    both = total[:, :, :hid].reshape(2 * width, hid)
+    self_ref[...] = both[:width]
+    neigh_ref[...] = both[width:]
+    half = hid // 2
+    bias_ref[:, :half] = total[0, 0:1, hid:]
+    bias_ref[:, half:] = total[0, 1:2, hid:]
+
+
 def body(
     adj_tiles, tile_pos, tile_count, node_feats, stale_part, w_self, w_neigh, bias_vec, cotangent
 ):
@@ -292,10 +305,18 @@
     piece = (jnp.sum(piece, axis=0) * scaling).astype(bf16)
     pair = plane * lax.axis_size("z_near")
     copies = jnp.broadcast_to(piece[None], (pair,) + piece.shape)
-    both = lax.all_to_all(copies, PLANE + ("z_near",), 0, 0, tiled=True).astype(f32)
-    both = jnp.sum(both.reshape((plane, 2) + piece.shape), axis=1)
-    grad_bias = both[0, :2, hid:].reshape(hid)
-    both = both[:, :, :hid].reshape(2 * width, hid)
+    got = lax.all_to_all(copies, PLANE + ("z_near",), 0, 0, tiled=True)
+    grad_self, grad_neigh, grad_bias = pl.pallas_call(
+        finish_kernel,
+        out_shape=(
+            jax.ShapeDtypeStruct((width, hid), f32),
+            jax.ShapeDtypeStruct((width, hid), f32),
+            jax.ShapeDtypeStruct((1, hid), f32),
+        ),
+        in_specs=[vmem],
+        out_specs=(vmem,) * 3,
+        compiler_params=limit,
+    )(got)
     new_part = pl.pallas_call(
         partial_kernel,
         out_shape=jax.ShapeDtypeStruct((groups, node_dev, width), bf16),
@@ -312,7 +333,7 @@
             flops=2 * slots * tile * tile * width, bytes_accessed=8 * 2**20, transcendentals=0
         ),
     )(tile_count, tile_pos, place, adj_tiles, list(banks), copies)
-    return new_part[None], hidden, both[:width], both[width:], grad_bias
+    return new_part[None], hidden, grad_self, grad_neigh, grad_bias.reshape(hid)
 
 
 def solution(mesh):

time: 152 us -> 151 us (level)
  Pallas kernels: 6.6 us -> 8.29 us
  transfers between devices with their start and end apart: 7 -> 7, of which waited for: 3 -> 3; matrix products, arithmetic and copies ran while one was open for 0% -> 0% of each run, Pallas kernels for 2% -> 3%
where the time goes in v9:
time: 151 us
  blocking collectives  84.9 us (56%)
  starting transfers between devices  40.3 us (27%)
  waiting for transfers between devices  14.6 us (10%)
  Pallas kernels  8.29 us (5%)
  between operations  1.55 us (1%)
    all_gather x1, blocking collectives, body(): same = lax.all_gather(node_feats, EVERY_OTHER)  45.3 us
    all_gather x1, blocking collectives, body(): lax.all_gather(jnp.sum(piece, axis=0).astype(bf16), EVERY_OTHER).astype(f32)  23.8 us
    all_to_all x1, blocking collectives, body(): piece = lax.all_to_all(grads, PLANE, 0, 0, tiled=True).astype(f32)  15.8 us
    all_to_all x1, starting transfers between devices, body(): stale = lax.all_to_all(stale_part[0], GRP, 0, 0, tiled=True)  13.3 us
    all_to_all x1, starting transfers between devices, body(): got = lax.all_to_all(copies, PLANE + ('z_near',), 0, 0, tiled=True)  11.7 us
    all_to_all x1, waiting for transfers between devices, body(): got = lax.all_to_all(copies, PLANE + ('z_near',), 0, 0, tiled=True)  6.78 us
    ppermute x1, starting transfers between devices, body(): lax.ppermute(low, 'x_hi', swap)  4.61 us
    ppermute x1, waiting for transfers between devices, body(): lax.ppermute(side_high, LINE, up)  4.6 us
  transfers between devices with their start and end apart: 7, of which 3 were waited for; matrix products, arithmetic and copies ran while one was open for 0% of the time, Pallas kernels for 3%

profile of v9, /device:TPU:1, one launch (start us, length us, event | category | flops | bytes accessed | tf_op | source)
XLA Modules:
  0.0 150.6 jit_solution(3134454889336644677)
XLA Ops:
  0.7 0.0 copy-start.10
  0.7 45.3 %all-gather = bf16[2048,128]{1,0:T(8,128)(2,1)S(1)} all-gather(bf16[128,128]{1,0:T(8,128)(2,1)} %feats_ref.3), channel_id=2, replica_groups=mesh['y'=4,'x_lo'=2,'core'=2,'x_hi'=2,'z_far'=8,'z_mid'=2,'z_near'=2] {'..., dimensions={0}, use_global_device_ids=true | all-gather | bytes 557056 | tf_op jit(solution)/shard_map/all_gather | solution.py:219
  46.1 4.6 %collective-permute-start.1 = (bf16[8,128,128]{2,1,0:T(8,128)(2,1)S(1)}, bf16[8,128,128]{2,1,0:T(8,128)(2,1)S(1)}, u32[]{:S(2)}, u32[]{:S(2)}) collective-permute-start(bf16[8,128,128]{2,1,0:T(8,128)(2,1)S(1)} %bitcast.18), channel_id=1, source_target_pairs={{0,32},{32,0},{1,33},{33,1},{2,34},{34,2},{3,35},{35,3},{4,36},{36... | collective-permute-start | bytes 786440 | tf_op jit(solution)/shard_map/ppermute | solution.py:226
  50.7 2.2 %collective-permute-start.2 = (bf16[8,128,128]{2,1,0:T(8,128)(2,1)S(1)}, bf16[8,128,128]{2,1,0:T(8,128)(2,1)S(1)}, u32[]{:S(2)}, u32[]{:S(2)}) collective-permute-start(bf16[8,128,128]{2,1,0:T(8,128)(2,1)S(1)} %bitcast.17), channel_id=1, source_target_pairs={{0,32},{32,0},{1,33},{33,1},{2,34},{34,2},{3,35},{35,3},{4,36},{36... | collective-permute-start | bytes 786440 | tf_op jit(solution)/shard_map/ppermute | solution.py:226
  52.9 2.6 %collective-permute-start = (bf16[16,128,128]{2,1,0:T(8,128)(2,1)S(1)}, bf16[16,128,128]{2,1,0:T(8,128)(2,1)S(1)}, u32[]{:S(2)}, u32[]{:S(2)}) collective-permute-start(bf16[16,128,128]{2,1,0:T(8,128)(2,1)S(1)} %bitcast.11), channel_id=1, source_target_pairs={{0,1},{1,2},{2,3},{3,4},{4,5},{5,6},{6,7},{7,8},{8,9},{9,10},{10,1... | collective-permute-start | bytes 1572872 | tf_op jit(solution)/shard_map/ppermute | solution.py:227
  55.5 13.3 %all-to-all-start = ((bf16[16,128,128]{2,1,0:T(8,128)(2,1)}), bf16[16,128,128]{2,1,0:T(8,128)(2,1)S(1)}, u32[]{:S(2)}, u32[]{:S(2)}) async-start(bf16[16,128,128]{2,1,0:T(8,128)(2,1)} %bitcast.16), calls=%async_computation | async-start | bytes 1048576 | tf_op jit(solution)/shard_map/all_to_all | solution.py:218
  68.9 0.0 collective-permute-done.1.bank_refs_2_
  68.9 3.9 %collective-permute-start.3 = (bf16[8,128,128]{2,1,0:T(8,128)(2,1)S(1)}, bf16[8,128,128]{2,1,0:T(8,128)(2,1)S(1)}, u32[]{:S(2)}, u32[]{:S(2)}) collective-permute-start(bf16[8,128,128]{2,1,0:T(8,128)(2,1)S(1)} %collective-permute-done.1.bank_refs_2_), channel_id=1, source_target_pairs={{0,31},{1,0},{2,1},{3,2},{4,3},{5,4},{6,5},{7,6},{8,7},{9,8},{10,9... | collective-permute-start | bytes 786440 | tf_op jit(solution)/shard_map/ppermute | solution.py:233
  72.8 0.0 collective-permute-done.2.bank_refs_3_
  72.8 1.9 %collective-permute-start.4 = (bf16[8,128,128]{2,1,0:T(8,128)(2,1)S(1)}, bf16[8,128,128]{2,1,0:T(8,128)(2,1)S(1)}, u32[]{:S(2)}, u32[]{:S(2)}) collective-permute-start(bf16[8,128,128]{2,1,0:T(8,128)(2,1)S(1)} %collective-permute-done.2.bank_refs_3_), channel_id=1, source_target_pairs={{0,1},{1,2},{2,3},{3,4},{4,5},{5,6},{6,7},{7,8},{8,9},{9,10},{10,1... | collective-permute-start | bytes 786440 | tf_op jit(solution)/shard_map/ppermute | solution.py:234
  75.4 0.0 copy-start.11
  75.5 3.2 %all-to-all-done.stale_ref = bf16[16,128,128]{2,1,0:T(8,128)(2,1)S(1)} async-done(((bf16[16,128,128]{2,1,0:T(8,128)(2,1)}), bf16[16,128,128]{2,1,0:T(8,128)(2,1)S(1)}, u32[]{:S(2)}, u32[]{:S(2)}) %all-to-all-start) | async-done | bytes 524320 | tf_op jit(solution)/shard_map/all_to_all | solution.py:218
  78.7 0.2 shard_map.128
  78.9 0.0 collective-permute-done.3.bank_refs_4_
  78.9 4.6 %collective-permute-done.4.bank_refs_5_ = bf16[8,128,128]{2,1,0:T(8,128)(2,1)S(1)} collective-permute-done((bf16[8,128,128]{2,1,0:T(8,128)(2,1)S(1)}, bf16[8,128,128]{2,1,0:T(8,128)(2,1)S(1)}, u32[]{:S(2)}, u32[]{:S(2)}) %collective-permute-start.4) | collective-permute-done | bytes 262176 | tf_op jit(solution)/shard_map/ppermute | solution.py:234
  83.5 0.0 collective-permute-done.bank_refs_1_
  83.5 3.0 %shard_map.129 = (bf16[128,256]{1,0:T(8,128)(2,1)}, bf16[32,8,384]{2,1,0:T(8,128)(2,1)S(1)}) custom-call(s32[1]{0:T(128)S(6)} %copy.14.count_ref, s32[16]{0:T(128)S(1)} %copy-done.10, s32[64]{0:T(128)S(1)} %fusion.place_ref, s32[1]{0:T(128)} %bitcast.3.own_ref, bf16[16,256,256]{2,1,0:T(8,128)(2,1)} %adj_ref.3, bf16[16,128,128]{2,1,0:T(8,128)(2,1)S(1)} %bitcast.12, ...), custom_call_target="tpu_custom_call" | custom-call | flops 33554432 | bytes 1048576 | tf_op jit(solution)/shard_map/pallas_call | solution.py:270
  86.6 15.8 %all_to_all.15 = bf16[32,8,384]{2,1,0:T(8,128)(2,1)S(1)} all-to-all(bf16[32,8,384]{2,1,0:T(8,128)(2,1)S(1)} %get-tuple-element.18), channel_id=1, replica_groups=mesh['y'=4,'x_lo'=2,'core'=2,'x_hi'=2,'z_far'=8,'z_mid'=2,'z_near'=2] {'..., dimensions={0} | all-to-all | bytes 393216 | tf_op jit(solution)/shard_map/all_to_all | solution.py:303
  102.5 23.8 %all-gather.1 = bf16[128,384]{1,0:T(8,128)(2,1)S(1)} all-gather(bf16[8,384]{1,0:T(8,128)(2,1)S(1)} %reduce_sum.21), channel_id=3, replica_groups=mesh['y'=4,'x_lo'=2,'core'=2,'x_hi'=2,'z_far'=8,'z_mid'=2,'z_near'=2] {'..., dimensions={0}, use_global_device_ids=true | all-gather | bytes 104448 | tf_op jit(solution)/shard_map/all_gather | solution.py:304
  126.3 0.8 broadcast_in_dim.13._
  127.1 11.7 %all-to-all-start.2 = ((bf16[64,8,384]{2,1,0:T(8,128)(2,1)}), bf16[64,8,384]{2,1,0:T(8,128)(2,1)S(1)}, u32[]{:S(2)}, u32[]{:S(2)}) async-start(bf16[64,8,384]{2,1,0:T(8,128)(2,1)} %broadcast_in_dim.13._), calls=%async_computation.2 | async-start | bytes 786432 | tf_op jit(solution)/shard_map/all_to_all | solution.py:308
  138.8 4.3 %shard_map.130 = bf16[16,128,128]{2,1,0:T(8,128)(2,1)} custom-call(s32[1]{0:T(128)S(6)} %copy.14.count_ref, s32[16]{0:T(128)} %pos_ref.3, s32[64]{0:T(128)} %copy-done.11, bf16[16,256,256]{2,1,0:T(8,128)(2,1)} %adj_ref.3, bf16[16,128,128]{2,1,0:T(8,128)(2,1)} %bitcast.13, bf16[16,128,128]{2,1,0:T(8,128)(2,1)} %copy-done.1, bf16[8,128,128]{2,1,0:T(8,128)(2,1)} %copy-done.2, ...), custom_call_target="tpu_custom_call" | custom-call | flops 268435456 | bytes 8388608 | tf_op jit(solution)/shard_map/pallas_call | solution.py:320
  143.1 6.8 %all-to-all-done.2.got_ref = bf16[64,8,384]{2,1,0:T(8,128)(2,1)S(1)} async-done(((bf16[64,8,384]{2,1,0:T(8,128)(2,1)}), bf16[64,8,384]{2,1,0:T(8,128)(2,1)S(1)}, u32[]{:S(2)}, u32[]{:S(2)}) %all-to-all-start.2) | async-done | bytes 393248 | tf_op jit(solution)/shard_map/all_to_all | solution.py:308
  149.9 0.7 shard_map.131
  (29 shorter events, 0.2 us)
Async XLA Ops:
  0.6 78.0 %copy-start.6 = (bf16[128,128]{1,0:T(8,128)(2,1)S(1)}, bf16[128,128]{1,0:T(8,128)(2,1)}, u32[]{:S(2)}) copy-start(bf16[128,128]{1,0:T(8,128)(2,1)} %feats_ref.3) | copy-start | bytes 98308
  0.6 78.0 %copy-start.9 = (bf16[128,256]{1,0:T(8,128)(2,1)S(1)}, bf16[128,256]{1,0:T(8,128)(2,1)}, u32[]{:S(2)}) copy-start(bf16[128,256]{1,0:T(8,128)(2,1)} %cot_ref.1) | copy-start | bytes 196612
  0.7 78.0 %copy-start.8 = (bf16[128,256]{1,0:T(8,128)(2,1)S(1)}, bf16[128,256]{1,0:T(8,128)(2,1)}, u32[]{:S(2)}) copy-start(bf16[128,256]{1,0:T(8,128)(2,1)} %w_neigh_ref.1) | copy-start | bytes 196612
  0.7 78.0 %copy-start.7 = (bf16[128,256]{1,0:T(8,128)(2,1)S(1)}, bf16[128,256]{1,0:T(8,128)(2,1)}, u32[]{:S(2)}) copy-start(bf16[128,256]{1,0:T(8,128)(2,1)} %w_self_ref.1) | copy-start | bytes 196612
  0.7 82.8 %copy-start.10 = (s32[16]{0:T(128)S(1)}, s32[16]{0:T(128)}, u32[]{:S(2)}) copy-start(s32[16]{0:T(128)} %pos_ref.3) | copy-start | bytes 196
  0.7 82.8 %copy-start.12 = (f32[256]{0:T(256)S(1)}, f32[256]{0:T(256)}, u32[]{:S(2)}) copy-start(f32[256]{0:T(256)} %param.16) | copy-start | bytes 3076
  46.0 40.5 %copy-start = (bf16[2048,128]{1,0:T(8,128)(2,1)}, bf16[2048,128]{1,0:T(8,128)(2,1)S(1)}, u32[]{:S(2)}) copy-start(bf16[2048,128]{1,0:T(8,128)(2,1)S(1)} %all-gather) | copy-start | bytes 1572868
  46.1 22.8 %collective-permute-start.1 = (bf16[8,128,128]{2,1,0:T(8,128)(2,1)S(1)}, bf16[8,128,128]{2,1,0:T(8,128)(2,1)S(1)}, u32[]{:S(2)}, u32[]{:S(2)}) collective-permute-start(bf16[8,128,128]{2,1,0:T(8,128)(2,1)S(1)} %bitcast.18), channel_id=1, source_target_pairs={{0,32},{32,0},{1,33},{33,1},{2,34},{34,2},{3,35},{35,3},{4,36},{36... | collective-permute-start | bytes 786440 | tf_op jit(solution)/shard_map/ppermute | solution.py:226
  50.7 22.1 %collective-permute-start.2 = (bf16[8,128,128]{2,1,0:T(8,128)(2,1)S(1)}, bf16[8,128,128]{2,1,0:T(8,128)(2,1)S(1)}, u32[]{:S(2)}, u32[]{:S(2)}) collective-permute-start(bf16[8,128,128]{2,1,0:T(8,128)(2,1)S(1)} %bitcast.17), channel_id=1, source_target_pairs={{0,32},{32,0},{1,33},{33,1},{2,34},{34,2},{3,35},{35,3},{4,36},{36... | collective-permute-start | bytes 786440 | tf_op jit(solution)/shard_map/ppermute | solution.py:226
  52.9 30.6 %collective-permute-start = (bf16[16,128,128]{2,1,0:T(8,128)(2,1)S(1)}, bf16[16,128,128]{2,1,0:T(8,128)(2,1)S(1)}, u32[]{:S(2)}, u32[]{:S(2)}) collective-permute-start(bf16[16,128,128]{2,1,0:T(8,128)(2,1)S(1)} %bitcast.11), channel_id=1, source_target_pairs={{0,1},{1,2},{2,3},{3,4},{4,5},{5,6},{6,7},{7,8},{8,9},{9,10},{10,1... | collective-permute-start | bytes 1572872 | tf_op jit(solution)/shard_map/ppermute | solution.py:227
  55.5 23.1 %all-to-all-start = ((bf16[16,128,128]{2,1,0:T(8,128)(2,1)}), bf16[16,128,128]{2,1,0:T(8,128)(2,1)S(1)}, u32[]{:S(2)}, u32[]{:S(2)}) async-start(bf16[16,128,128]{2,1,0:T(8,128)(2,1)} %bitcast.16), calls=%async_computation | async-start | bytes 1048576 | tf_op jit(solution)/shard_map/all_to_all | solution.py:218
  68.9 17.7 %copy-start.2 = (bf16[8,128,128]{2,1,0:T(8,128)(2,1)}, bf16[8,128,128]{2,1,0:T(8,128)(2,1)S(1)}, u32[]{:S(2)}) copy-start(bf16[8,128,128]{2,1,0:T(8,128)(2,1)S(1)} %collective-permute-done.1.bank_refs_2_) | copy-start | bytes 786436
  68.9 10.0 %collective-permute-start.3 = (bf16[8,128,128]{2,1,0:T(8,128)(2,1)S(1)}, bf16[8,128,128]{2,1,0:T(8,128)(2,1)S(1)}, u32[]{:S(2)}, u32[]{:S(2)}) collective-permute-start(bf16[8,128,128]{2,1,0:T(8,128)(2,1)S(1)} %collective-permute-done.1.bank_refs_2_), channel_id=1, source_target_pairs={{0,31},{1,0},{2,1},{3,2},{4,3},{5,4},{6,5},{7,6},{8,7},{9,8},{10,9... | collective-permute-start | bytes 786440 | tf_op jit(solution)/shard_map/ppermute | solution.py:233
  72.8 13.7 %copy-start.3 = (bf16[8,128,128]{2,1,0:T(8,128)(2,1)}, bf16[8,128,128]{2,1,0:T(8,128)(2,1)S(1)}, u32[]{:S(2)}) copy-start(bf16[8,128,128]{2,1,0:T(8,128)(2,1)S(1)} %collective-permute-done.2.bank_refs_3_) | copy-start | bytes 786436
  72.8 10.6 %collective-permute-start.4 = (bf16[8,128,128]{2,1,0:T(8,128)(2,1)S(1)}, bf16[8,128,128]{2,1,0:T(8,128)(2,1)S(1)}, u32[]{:S(2)}, u32[]{:S(2)}) collective-permute-start(bf16[8,128,128]{2,1,0:T(8,128)(2,1)S(1)} %collective-permute-done.2.bank_refs_3_), channel_id=1, source_target_pairs={{0,1},{1,2},{2,3},{3,4},{4,5},{5,6},{6,7},{7,8},{8,9},{9,10},{10,1... | collective-permute-start | bytes 786440 | tf_op jit(solution)/shard_map/ppermute | solution.py:234
  75.4 11.1 %copy-start.11 = (s32[64]{0:T(128)}, s32[64]{0:T(128)S(1)}, u32[]{:S(2)}) copy-start(s32[64]{0:T(128)S(1)} %fusion.place_ref) | copy-start | bytes 772
  78.9 7.7 %copy-start.4 = (bf16[8,128,128]{2,1,0:T(8,128)(2,1)}, bf16[8,128,128]{2,1,0:T(8,128)(2,1)S(1)}, u32[]{:S(2)}) copy-start(bf16[8,128,128]{2,1,0:T(8,128)(2,1)S(1)} %collective-permute-done.3.bank_refs_4_) | copy-start | bytes 786436
  83.5 3.1 %copy-start.5 = (bf16[8,128,128]{2,1,0:T(8,128)(2,1)}, bf16[8,128,128]{2,1,0:T(8,128)(2,1)S(1)}, u32[]{:S(2)}) copy-start(bf16[8,128,128]{2,1,0:T(8,128)(2,1)S(1)} %collective-permute-done.4.bank_refs_5_) | copy-start | bytes 786436
  83.5 3.1 %copy-start.1 = (bf16[16,128,128]{2,1,0:T(8,128)(2,1)}, bf16[16,128,128]{2,1,0:T(8,128)(2,1)S(1)}, u32[]{:S(2)}) copy-start(bf16[16,128,128]{2,1,0:T(8,128)(2,1)S(1)} %collective-permute-done.bank_refs_1_) | copy-start | bytes 1572868
  127.1 22.8 %all-to-all-start.2 = ((bf16[64,8,384]{2,1,0:T(8,128)(2,1)}), bf16[64,8,384]{2,1,0:T(8,128)(2,1)S(1)}, u32[]{:S(2)}, u32[]{:S(2)}) async-start(bf16[64,8,384]{2,1,0:T(8,128)(2,1)} %broadcast_in_dim.13._), calls=%async_computation.2 | async-start | bytes 786432 | tf_op jit(solution)/shard_map/all_to_all | solution.py:308
